TPU v7x, 32 devices: a whole 2x2x4 slice. The times are simulated.
32 devices in a mesh: dp: 4 (over y, core), seq: 8 (over z, x).
Axes of the slice: x: 2, y: 2, z: 4, core: 2. Of those that a mesh axis runs over, the one named last changes fastest.
Arguments:
- tokens: bfloat16 [2, 4, 2048, 768], P(None, 'dp', 'seq'), may hold values from -6 to 6
- cotangent: bfloat16 [2, 4, 2048, 768], P(None, 'dp', 'seq'), may hold values from -6 to 6
- norm_in: bfloat16 [768], P(('dp', 'seq')), may hold values from 0.5 to 1.5
- w_in: bfloat16 [768, 3352], P(('dp', 'seq')), may hold values from -0.21875 to 0.21875
- conv_w: bfloat16 [1792, 4], P(('dp', 'seq')), may hold values from -3 to 3
- conv_b: bfloat16 [1792], P(('dp', 'seq')), may hold values from -3 to 3
- dt_bias: float32 [24], replicated, may hold values from -5.5 to -4
- a_log: float32 [24], replicated, may hold values from -3.9 to 1.6
- skip: float32 [24], replicated, may hold values from 0.5 to 1.5
- norm_out: bfloat16 [1536], P(('dp', 'seq')), may hold values from 0.5 to 1.5
- w_out: bfloat16 [1536, 768], P(('dp', 'seq')), may hold values from -0.15625 to 0.15625
Outputs:
- block_out: bfloat16 [2, 4, 2048, 768], P(None, 'dp', 'seq')
- grad_tokens: bfloat16 [2, 4, 2048, 768], P(None, 'dp', 'seq')
- grad_norm_in: float32 [768], P(('dp', 'seq'))
- grad_w_in: float32 [768, 3352], P(('dp', 'seq'))
- grad_conv_w: float32 [1792, 4], P(('dp', 'seq'))
- grad_conv_b: float32 [1792], P(('dp', 'seq'))
- grad_dt_bias: float32 [24], replicated
- grad_a_log: float32 [24], replicated
- grad_skip: float32 [24], replicated
- grad_norm_out: float32 [1536], P(('dp', 'seq'))
- grad_w_out: float32 [1536, 768], P(('dp', 'seq'))
All inputs are finite; a program needn't handle non-finite values.
Results may differ from a plain program's by a relative error of at most 0.012.
Values may be sent and summed in bfloat16 or wider, within the bound.
No kernel may reach another device: no remote copies, remote signals or barrier semaphores. Data moves between devices by JAX's collectives and lax.ppermute only.
A program may use at most 256 MiB of HBM per device.

v0:
```python
import jax
import jax.numpy as jnp
from jax import lax
from jax.sharding import PartitionSpec as P

H = 24
HP = 64
N = 128
KW = 4
SEQ_LEN = 2048


epsilon = 1e-05
far_decay = -1e30


def from_behind(x, axis, by):
    size = lax.axis_size(axis)
    pairs = [(i, i + by) for i in range(size) if 0 <= i + by < size]
    return lax.ppermute(x, axis, pairs)


def prefix(value, axis, join, neutral):
    count, mine = (lax.axis_size(axis), lax.axis_index(axis))
    pieces = jax.tree.map(lambda part: lax.all_gather(part, axis), value)
    so_far = jax.tree.map(
        lambda part, zero: jnp.full_like(part, 0) + jnp.asarray(zero, part.dtype), value, neutral
    )

    def turn(position, so_far):
        longer = join(so_far, jax.tree.map(lambda part: part[position], pieces))
        return jax.tree.map(lambda new, old: jnp.where(position < mine, new, old), longer, so_far)

    return lax.fori_loop(0, count - 1, turn, so_far)


def entering(x, axis, join, neutral):
    count = lax.axis_size(axis)
    place = lax.axis_index(axis)
    ahead = count - 1 - place
    gathered = jax.tree.map(
        lambda a, kind: lax.all_gather(a.astype(kind), axis), x, (jnp.bfloat16, jnp.bfloat16)
    )
    state = jax.tree.map(lambda a, e: jnp.zeros_like(a) + jnp.asarray(e, a.dtype), x, neutral)

    def one(turn, state):
        source = count - 1 - turn
        return join(
            state,
            jax.tree.map(
                lambda a, own: lax.dynamic_index_in_dim(a, source, 0, False).astype(own.dtype),
                gathered,
                x,
            ),
        )

    return lax.fori_loop(0, ahead, one, state)


def prenorm(activ, gain):
    return activ * lax.rsqrt(jnp.mean(activ * activ, axis=-1, keepdims=True) + epsilon) * gain


def convolve(extended, kernel, bias):
    length = extended.shape[1] - kernel.shape[0] + 1
    summed = bias
    for shift_k in range(kernel.shape[0]):
        summed = summed + kernel[shift_k] * extended[:, shift_k : shift_k + length]
    return jax.nn.silu(summed)


def decays(raw_step, bias, alog):
    step_size = jax.nn.softplus(raw_step + bias)
    cumul = jnp.cumsum(step_size * -jnp.exp(alog), axis=1)
    return (step_size, cumul)


def mixing(scores, cumul, step_size, values_f):
    count = scores.shape[1]
    lower = (jnp.arange(count)[:, None] >= jnp.arange(count)[None, :])[None, None]
    cum_t = jnp.transpose(cumul, (0, 2, 1))
    step_t = jnp.transpose(step_size, (0, 2, 1))
    differ = cum_t[:, :, :, None] - cum_t[:, :, None, :]
    decay = jnp.where(lower, jnp.exp(jnp.where(lower, differ, 0.0)), 0.0)
    mixed = scores[:, None, :, :] * decay * step_t[:, :, None, :]
    weights = jnp.exp(cumul[:, -1:, :] - cumul)[..., None] * step_size[..., None] * values_f
    return (mixed, weights, jnp.exp(cumul), cumul[:, -1, :])


def gate_norm(ssd_flat, gate_f, gain):
    gated = ssd_flat * jax.nn.silu(gate_f)
    return gated * lax.rsqrt(jnp.mean(gated * gated, axis=-1, keepdims=True) + epsilon) * gain


def combine(earlier, later):
    return (earlier[0] + later[0], jnp.exp(later[0])[:, :, None, None] * earlier[1] + later[1])


def unpack(gathered):
    return (
        gathered[0].astype(jnp.float32),
        gathered[1],
        gathered[2].astype(jnp.float32).T,
        gathered[3].astype(jnp.float32),
        gathered[4].astype(jnp.float32),
        gathered[5],
    )


def project_in(block_rows, gain_in, w_in_full):
    rows = block_rows.astype(jnp.float32)
    hidden = prenorm(rows, gain_in).astype(jnp.bfloat16)
    projected = jnp.einsum(
        "sqd,de->sqe", hidden, w_in_full, preferred_element_type=jnp.float32
    ).astype(jnp.bfloat16)
    return (rows, hidden, projected)


def scan_inputs(projected, edge, kernel, bias, dt_bias, a_log):
    inner = H * HP
    conv_in = projected[:, :, inner : 2 * inner + 2 * N]
    raw_step = projected[:, :, 2 * inner + 2 * N :].astype(jnp.float32)
    extended = jnp.concatenate([edge, conv_in], axis=1).astype(jnp.float32)
    activated = convolve(extended, kernel, bias).astype(jnp.bfloat16)
    batch, count = (activated.shape[0], activated.shape[1])
    values = activated[:, :, :inner].reshape(batch, count, H, HP)
    bmat = activated[:, :, inner : inner + N]
    cmat = activated[:, :, inner + N :]
    step_size, cumul = decays(raw_step, dt_bias, a_log)
    scores = jnp.einsum("stn,sun->stu", cmat, bmat, preferred_element_type=jnp.float32)
    values_f = values.astype(jnp.float32)
    mixed, weights, growth, totals = mixing(scores, cumul, step_size, values_f)
    weights_b = weights.astype(jnp.bfloat16)
    local_state = jnp.einsum("sqhp,sqn->shpn", weights_b, bmat, preferred_element_type=jnp.float32)
    return {
        "extended": extended,
        "raw_step": raw_step,
        "values": values,
        "values_f": values_f,
        "bmat": bmat,
        "cmat": cmat,
        "step_size": step_size,
        "cumul": cumul,
        "scores": scores,
        "mixed_b": mixed.astype(jnp.bfloat16),
        "weights_b": weights_b,
        "growth": growth,
        "totals": totals,
        "local_state": local_state,
    }


def mixer_out(parts, incoming_b, skip):
    offset = jnp.einsum(
        "sqn,shpn->sqhp", parts["cmat"], incoming_b, preferred_element_type=jnp.float32
    )
    intra = jnp.einsum(
        "shtu,suhp->sthp", parts["mixed_b"], parts["values"], preferred_element_type=jnp.float32
    )
    ssd = intra + parts["growth"][..., None] * offset + skip[:, None] * parts["values_f"]
    return (offset, ssd.reshape(ssd.shape[0], ssd.shape[1], H * HP))


def local(tokens, cotangent, norm_in, w_in, conv_w, conv_b, dt_bias, a_log, skip, norm_out, w_out):
    inner = H * HP
    shards = (norm_in, w_in, conv_w, conv_b, norm_out, w_out)
    gathered = (
        lax.all_gather(shards[0], ("dp", "seq"), axis=0, tiled=True),
        lax.all_gather(shards[1], ("dp", "seq"), axis=0, tiled=True),
        lax.all_gather(shards[2], ("dp", "seq"), axis=0, tiled=True),
        lax.all_gather(shards[3], ("dp", "seq"), axis=0, tiled=True),
        lax.all_gather(shards[4], ("dp", "seq"), axis=0, tiled=True),
        lax.all_gather(shards[5], ("dp", "seq"), axis=0, tiled=True),
    )
    gain_in, w_in_full, kernel, bias, gain_out, w_out_full = unpack(gathered)
    micro = tokens.shape[0]
    batch = tokens.shape[1]
    count = tokens.shape[2]
    place = lax.axis_index("seq")
    opening = place * count % SEQ_LEN == 0
    closing = (place + 1) * count % SEQ_LEN == 0
    zero_totals = jnp.zeros((batch, H), jnp.float32)
    zero_states = jnp.zeros((batch, H, HP, N), jnp.float32)
    kept = []
    outputs = []
    for index in range(micro):
        rows, hidden, projected = project_in(tokens[index], gain_in, w_in_full)
        tail = projected[:, -(KW - 1) :, inner : 2 * inner + 2 * N]
        edge = from_behind(tail, "seq", 1)
        edge = jnp.where(opening, jnp.zeros_like(edge), edge)
        parts = scan_inputs(projected, edge, kernel, bias, dt_bias, a_log)
        send_totals = jnp.where(closing, jnp.full_like(parts["totals"], far_decay), parts["totals"])
        send_state = jnp.where(closing, jnp.zeros_like(parts["local_state"]), parts["local_state"])
        incoming = prefix((send_totals, send_state), "seq", combine, (zero_totals, zero_states))[1]
        offset, ssd_flat = mixer_out(parts, incoming.astype(jnp.bfloat16), skip)
        normed = gate_norm(ssd_flat, projected[:, :, :inner].astype(jnp.float32), gain_out).astype(
            jnp.bfloat16
        )
        result = rows + jnp.einsum(
            "sqi,id->sqd", normed, w_out_full, preferred_element_type=jnp.float32
        )
        outputs.append(result.astype(jnp.bfloat16))
        kept.append((rows, hidden, projected, parts, offset, ssd_flat, incoming))
    block_out = jnp.stack(outputs)
    regathered = (
        lax.all_gather(shards[0], ("dp", "seq"), axis=0, tiled=True),
        lax.all_gather(shards[1], ("dp", "seq"), axis=0, tiled=True),
        lax.all_gather(shards[2], ("dp", "seq"), axis=0, tiled=True),
        lax.all_gather(shards[3], ("dp", "seq"), axis=0, tiled=True),
        lax.all_gather(shards[4], ("dp", "seq"), axis=0, tiled=True),
        lax.all_gather(shards[5], ("dp", "seq"), axis=0, tiled=True),
    )
    gain_in, w_in_full, kernel, bias, gain_out, w_out_full = unpack(regathered)
    g_gin = jnp.zeros(gain_in.shape, jnp.float32)
    g_win = jnp.zeros(w_in_full.shape, jnp.float32)
    g_kernel = jnp.zeros(kernel.shape, jnp.float32)
    g_bias = jnp.zeros(bias.shape, jnp.float32)
    g_dtb = jnp.zeros((H,), jnp.float32)
    g_alog = jnp.zeros((H,), jnp.float32)
    g_skip = jnp.zeros((H,), jnp.float32)
    g_gout = jnp.zeros(gain_out.shape, jnp.float32)
    g_wout = jnp.zeros(w_out_full.shape, jnp.float32)
    grad_list = []
    for index in range(micro):
        rows, hidden, projected, parts, offset, ssd_flat, incoming = kept[index]
        incoming_b = incoming.astype(jnp.bfloat16)
        gate_f = projected[:, :, :inner].astype(jnp.float32)
        normed_f, pull_gate = jax.vjp(gate_norm, ssd_flat, gate_f, gain_out)
        normed = normed_f.astype(jnp.bfloat16)
        tangent = cotangent[index]
        g_wout = g_wout + jnp.einsum(
            "sqi,sqd->id", normed, tangent, preferred_element_type=jnp.float32
        )
        d_normed = jnp.einsum(
            "sqd,id->sqi", tangent, w_out_full, preferred_element_type=jnp.float32
        )
        d_ssd, d_gate, d_gout = pull_gate(d_normed)
        g_gout = g_gout + d_gout
        dy_b = d_ssd.astype(jnp.bfloat16).reshape(batch, count, H, HP)
        dy_f = dy_b.astype(jnp.float32)
        d_off_b = (parts["growth"][..., None] * dy_f).astype(jnp.bfloat16)
        d_growth = jnp.sum(dy_f * offset, axis=-1)
        d_cmat = jnp.einsum(
            "sqhp,shpn->sqn", d_off_b, incoming_b, preferred_element_type=jnp.float32
        )
        d_incoming = jnp.einsum(
            "sqhp,sqn->shpn", d_off_b, parts["cmat"], preferred_element_type=jnp.float32
        )
        g_skip = g_skip + jnp.sum(dy_f * parts["values_f"], axis=(0, 1, 3))
        d_values = skip[:, None] * dy_f
        d_mixed = jnp.einsum(
            "sthp,suhp->shtu", dy_b, parts["values"], preferred_element_type=jnp.float32
        )
        d_values = d_values + jnp.einsum(
            "shtu,sthp->suhp", parts["mixed_b"], dy_b, preferred_element_type=jnp.float32
        )
        back_totals = jnp.where(opening, jnp.full_like(parts["totals"], far_decay), parts["totals"])
        back_state = jnp.where(opening, jnp.zeros_like(d_incoming), d_incoming)
        later = entering((back_totals, back_state), "seq", combine, (zero_totals, zero_states))[1]
        d_local_b = later.astype(jnp.bfloat16)
        d_totals = jnp.sum(
            later * jnp.exp(parts["totals"])[:, :, None, None] * incoming, axis=(2, 3)
        )
        d_weights = jnp.einsum(
            "shpn,sqn->sqhp", d_local_b, parts["bmat"], preferred_element_type=jnp.float32
        )
        d_bmat = jnp.einsum(
            "shpn,sqhp->sqn", d_local_b, parts["weights_b"], preferred_element_type=jnp.float32
        )
        _, pull_mix = jax.vjp(
            mixing, parts["scores"], parts["cumul"], parts["step_size"], parts["values_f"]
        )
        d_scores, d_cumul, d_step, d_values_mix = pull_mix((d_mixed, d_weights, d_growth, d_totals))
        d_values = d_values + d_values_mix
        d_scores_b = d_scores.astype(jnp.bfloat16)
        d_cmat = d_cmat + jnp.einsum(
            "stu,sun->stn", d_scores_b, parts["bmat"], preferred_element_type=jnp.float32
        )
        d_bmat = d_bmat + jnp.einsum(
            "stu,stn->sun", d_scores_b, parts["cmat"], preferred_element_type=jnp.float32
        )
        _, pull_decay = jax.vjp(decays, parts["raw_step"], dt_bias, a_log)
        d_raw, d_dtb, d_alog = pull_decay((d_step, d_cumul))
        g_dtb = g_dtb + d_dtb
        g_alog = g_alog + d_alog
        d_act = jnp.concatenate([d_values.reshape(batch, count, inner), d_bmat, d_cmat], axis=-1)
        _, pull_conv = jax.vjp(convolve, parts["extended"], kernel, bias)
        d_extended, d_kernel, d_bias = pull_conv(d_act)
        g_kernel = g_kernel + d_kernel
        g_bias = g_bias + d_bias
        d_edge_out = jnp.where(
            opening, jnp.zeros_like(d_extended[:, : KW - 1]), d_extended[:, : KW - 1]
        )
        d_edge_back = from_behind(d_edge_out, "seq", -1)
        d_conv_in = d_extended[:, KW - 1 :].at[:, -(KW - 1) :].add(d_edge_back)
        d_projected = jnp.concatenate([d_gate, d_conv_in, d_raw], axis=-1).astype(jnp.bfloat16)
        g_win = g_win + jnp.einsum(
            "sqd,sqe->de", hidden, d_projected, preferred_element_type=jnp.float32
        )
        d_hidden = jnp.einsum(
            "sqe,de->sqd", d_projected, w_in_full, preferred_element_type=jnp.float32
        )
        _, pull_norm = jax.vjp(prenorm, rows, gain_in)
        d_rows, d_gin = pull_norm(d_hidden)
        g_gin = g_gin + d_gin
        grad_list.append((tangent.astype(jnp.float32) + d_rows).astype(jnp.bfloat16))
    grad_tokens = jnp.stack(grad_list)
    grads = (g_gin, g_win, g_kernel.T, g_bias, g_gout, g_wout)
    owned = (
        lax.psum_scatter(grads[0], ("dp", "seq"), scatter_dimension=0, tiled=True),
        lax.psum_scatter(grads[1], ("dp", "seq"), scatter_dimension=0, tiled=True),
        lax.psum_scatter(grads[2], ("dp", "seq"), scatter_dimension=0, tiled=True),
        lax.psum_scatter(grads[3], ("dp", "seq"), scatter_dimension=0, tiled=True),
        lax.psum_scatter(grads[4], ("dp", "seq"), scatter_dimension=0, tiled=True),
        lax.psum_scatter(grads[5], ("dp", "seq"), scatter_dimension=0, tiled=True),
    )
    head_sums = lax.psum((g_dtb, g_alog, g_skip), ("dp", "seq"))
    return (
        block_out,
        grad_tokens,
        owned[0],
        owned[1],
        owned[2],
        owned[3],
        head_sums[0],
        head_sums[1],
        head_sums[2],
        owned[4],
        owned[5],
    )


def solution(mesh):
    in_specs = (
        P(None, "dp", "seq", None),
        P(None, "dp", "seq", None),
        P(("dp", "seq")),
        P(("dp", "seq"), None),
        P(("dp", "seq"), None),
        P(("dp", "seq")),
        P(),
        P(),
        P(),
        P(("dp", "seq")),
        P(("dp", "seq"), None),
    )
    out_specs = (
        P(None, "dp", "seq", None),
        P(None, "dp", "seq", None),
        P(("dp", "seq")),
        P(("dp", "seq"), None),
        P(("dp", "seq"), None),
        P(("dp", "seq")),
        P(),
        P(),
        P(),
        P(("dp", "seq")),
        P(("dp", "seq"), None),
    )
    return jax.shard_map(local, mesh=mesh, in_specs=in_specs, out_specs=out_specs, check_vma=False)
```

profile of v0, /device:TPU:0, one launch (start us, length us, event | category | flops | bytes accessed | tf_op | source)
XLA Modules:
  0.0 781.6 jit_solution(3158861580012159668)
XLA Ops:
  12.7 42.2 %all-reduce.29 = (bf16[768]{0:T(1024)(128)(2,1)S(1)}, bf16[1792]{0:T(1024)(128)(2,1)S(1)}, bf16[1536]{0:T(1024)(128)(2,1)S(1)}) all-reduce(bf16[768]{0:T(1024)(128)(2,1)S(1)} %dynamic-update-slice.13, bf16[1792]{0:T(1024)(128)(2,1)S(1)} %dynamic-update-slice.12, ...), channel_id=1, replica_groups=mesh['dp'=4,'seq'=8] {'dp','seq'}, use_global_device_ids=true, to_apply=%add.21 | all-reduce | flops 4096 | bytes 16384
  55.0 66.5 %all-gather.4 = bf16[32,56,4]{1,2,0:T(4,128)(2,1)S(1)} all-gather(bf16[1,56,4]{1,2,0:T(4,128)(2,1)} %bitcast.653), channel_id=1, replica_groups=mesh['dp'=4,'seq'=8] {'dp','seq'}, dimensions={0}, use_global_device_ids=true | all-gather | bytes 14784 | tf_op jit(solution)/shard_map/all_gather | solution.py:170
  122.4 5.2 fusion.6
  128.8 2.2 collective-permute-start
  131.0 2.3 fusion.7
  144.5 2.5 collective-permute-done.1
  147.7 5.6 multiply_convert_fusion.7
  158.1 2.1 convolution_select_fusion.3
  161.1 3.8 fusion.89
  168.2 21.0 %all_gather.73 = f32[8,1,24]{2,1,0:T(1,128)} all-gather(f32[1,1,24]{2,1,0:T(1,128)S(1)} %copy.196), channel_id=1, replica_groups=mesh['dp'=4,'seq'=8] {'seq'}, dimensions={0}, use_global_device_ids=true | all-gather | bytes 864 | tf_op jit(solution)/shard_map/all_gather | solution.py:25
  189.2 17.8 %all_gather.68 = f32[8,1,24]{2,1,0:T(1,128)} all-gather(f32[1,1,24]{2,1,0:T(1,128)} %copy.188), channel_id=1, replica_groups=mesh['dp'=4,'seq'=8] {'seq'}, dimensions={0}, use_global_device_ids=true | all-gather | bytes 864 | tf_op jit(solution)/shard_map/all_gather | solution.py:25
  213.4 2.7 fusion.209
  217.7 41.1 %all-gather.18.cloned.1.call-done = f32[192,64,128]{2,1,0:T(8,128)} async-done(((f32[24,64,128]{2,1,0:T(8,128)}), f32[192,64,128]{2,1,0:T(8,128)}) %all-gather.18.cloned.1.call-update) | async-done | bytes 6291472 | tf_op jit(solution)/shard_map/all_gather | solution.py:25
  258.7 21.2 %while.61 = (s32[]{:T(128)}, f32[1,24,64,128]{3,2,1,0:T(8,128)}, s32[]{:T(128)}, f32[8,1,24]{2,1,0:T(1,128)}, f32[8,1,24,64,128]{4,3,2,1,0:T(8,128)}, /*index=5*/s32[]{:T(128)}, s32[]{:T(128)}) while((s32[]{:T(128)}, f32[1,24,64,128]{3,2,1,0:T(8,128)}, s32[]{:T(128)}, f32[8,1,24]{2,1,0:T(1,128)}, ...), condition=%wide.region_10.11_spmd.clone, body=%wide.region_9.10_spmd.clone.sunk | while | flops 786436 | bytes 2359697 | solution.py:34
  259.4 2.2 fusion.246
  262.2 2.4 fusion.246
  265.2 2.5 fusion.246
  268.4 2.4 fusion.246
  271.4 2.4 fusion.246
  274.5 2.4 fusion.246
  277.5 2.4 fusion.246
  281.9 3.5 fusion.34
  287.7 70.3 %all-gather.16.cloned.1.call-done = f32[192,64,128]{2,1,0:T(8,128)} async-done(((f32[24,64,128]{2,1,0:T(8,128)}), f32[192,64,128]{2,1,0:T(8,128)}) %all-gather.16.cloned.1.call-update) | async-done | bytes 6291472 | tf_op jit(solution)/shard_map/all_gather | solution.py:25
  358.0 17.4 %while.60 = (s32[]{:T(128)}, f32[1,24,64,128]{3,2,1,0:T(8,128)S(1)}, s32[]{:T(128)}, f32[8,1,24]{2,1,0:T(1,128)}, f32[8,1,24,64,128]{4,3,2,1,0:T(8,128)}, /*index=5*/s32[]{:T(128)}, s32[]{:T(128)}) while((s32[]{:T(128)}, f32[1,24,64,128]{3,2,1,0:T(8,128)S(1)}, s32[]{:T(128)}, f32[8,1,24]{2,1,0:T(1,128)}, ...), condition=%wide.region_4.5_spmd.clone, body=%wide.region_3.4_spmd.clone.sunk | while | flops 786436 | bytes 2359697 | solution.py:34
  377.4 3.3 fusion.35
  385.9 4.6 multiply_reduce_fusion.13
  395.9 2.0 fusion.44
  405.7 18.5 %all_gather.76 = bf16[8,1,24]{2,1,0:T(2,128)(2,1)} all-gather(bf16[1,1,24]{2,1,0:T(2,128)(2,1)} %copy.201), channel_id=1, replica_groups=mesh['dp'=4,'seq'=8] {'seq'}, dimensions={0}, use_global_device_ids=true | all-gather | bytes 432 | tf_op jit(solution)/shard_map/all_gather | solution.py:42
  424.2 17.5 %all_gather.79 = bf16[8,1,24]{2,1,0:T(2,128)(2,1)} all-gather(bf16[1,1,24]{2,1,0:T(2,128)(2,1)} %copy.213), channel_id=1, replica_groups=mesh['dp'=4,'seq'=8] {'seq'}, dimensions={0}, use_global_device_ids=true | all-gather | bytes 432 | tf_op jit(solution)/shard_map/all_gather | solution.py:42
  445.0 9.7 %fusion.9 = (f32[24,256]{1,0:T(8,128)}, f32[24,256]{1,0:T(8,128)}, f32[24,256]{1,0:T(8,128)}, bf16[256,256]{1,0:T(8,128)(2,1)S(1)}, bf16[256,256]{1,0:T(8,128)(2...) fusion(f32[24,256]{1,0:T(8,128)S(1)} %copy-done.134, f32[24,256]{1,0:T(8,128)S(1)} %copy-done.129, ...), kind=kOutput, calls=%fused_computation.31 | convolution fusion | flops 248344576 | bytes 8962048 | tf_op jit(solution)/shard_map/sthp,suhp->shtu/dot_general | solution.py:251
  461.9 3.0 convolution_add_fusion.1
  465.1 13.2 %while.59 = (s32[]{:T(128)}, f32[1,24,64,128]{3,2,1,0:T(8,128)S(1)}, s32[]{:T(128)}, bf16[8,1,24]{2,1,0:T(2,128)(2,1)}, bf16[8,1,24,64,128]{4,3,2,1,0:T(8,128)(2...) while((s32[]{:T(128)}, f32[1,24,64,128]{3,2,1,0:T(8,128)S(1)}, s32[]{:T(128)}, ...), condition=%wide.region_28.30_spmd, body=%wide.region_27.29_spmd.sunk | while | flops 589854 | bytes 1966475 | solution.py:57
  478.4 3.4 multiply_reduce_fusion.15
  482.7 30.9 %all-gather.20.cloned.1.call-done = bf16[192,64,128]{2,1,0:T(8,128)(2,1)} async-done(((bf16[24,64,128]{2,1,0:T(8,128)(2,1)}), bf16[192,64,128]{2,1,0:T(8,128)(2,1)}) %all-gather.20.cloned.1.call-update) | async-done | bytes 3145744 | tf_op jit(solution)/shard_map/all_gather | solution.py:42
  514.6 20.3 %while.58 = (s32[]{:T(128)}, f32[1,24,64,128]{3,2,1,0:T(8,128)}, s32[]{:T(128)}, bf16[8,1,24]{2,1,0:T(2,128)(2,1)}, bf16[8,1,24,64,128]{4,3,2,1,0:T(8,128)(2,1)}...) while((s32[]{:T(128)}, f32[1,24,64,128]{3,2,1,0:T(8,128)}, s32[]{:T(128)}, ...), condition=%wide.region_14.15_spmd, body=%wide.region_13.14_spmd.sunk | while | flops 589854 | bytes 1966475 | solution.py:57
  515.2 2.3 convert_add_fusion.6
  518.1 2.3 convert_add_fusion.6
  521.1 2.3 convert_add_fusion.6
  523.9 2.3 convert_add_fusion.6
  526.8 2.3 convert_add_fusion.6
  529.7 2.3 convert_add_fusion.6
  532.6 2.3 convert_add_fusion.6
  535.0 3.1 multiply_reduce_fusion.17
  541.9 2.3 multiply_reduce_fusion.21
  546.9 2.1 multiply_reduce_fusion.20
  550.8 2.5 reduce-window.34
  553.4 2.5 reduce-window.36
  558.5 4.1 fusion.32
  562.7 2.3 fusion.33
  565.0 4.8 multiply_reduce_fusion.7
  569.8 4.7 multiply_reduce_fusion.11
  575.0 5.6 broadcast_multiply_fusion
  580.6 2.2 pad_add_fusion
  586.5 5.4 pad_add_fusion.1
  598.9 3.1 slice_bitcast_fusion.1
  606.1 5.9 scatter-add.9
  612.4 2.2 fusion.65
  614.5 6.0 scatter-add.6
  622.4 5.8 convolution_add_fusion
  630.0 2.5 fusion.48
  635.4 4.3 fusion.80
  639.8 5.1 fusion.69
  644.9 43.8 %all-reduce.28 = (f32[768]{0:T(1024)S(1)}, f32[1792,4]{0,1:T(4,128)S(1)}, f32[1792]{0:T(1024)S(1)}, f32[24]{0:T(128)}, f32[24]{0:T(128)}, /*index=5*/f32[24]{0:T(128)}, f32[1536]{0:T(1024)S(1)}) all-reduce(f32[768]{0:T(1024)S(1)} %add.472, f32[1792,4]{0,1:T(4,128)S(1)} %add_bitcast_fusion, ...), channel_id=6, replica_groups=mesh['dp'=4,'seq'=8] {'dp','seq'}, use_global_device_ids=true, to_apply=%region_42.44.clone | all-reduce | flops 11336 | bytes 90688
  693.7 80.9 %reduce-scatter.8.cloned.1.call-done = f32[24,3352]{1,0:T(8,128)} async-done(((f32[768,3352]{1,0:T(8,128)}), f32[24,3352]{1,0:T(8,128)}) %reduce-scatter.8.cloned.1.call-update) | async-done | bytes 321808
  (557 shorter events, 149.2 us)
Async XLA Ops:
  7.2 115.2 %all-gather.12.cloned.1.call-start = ((), (), s32[]{:S(2)}) async-start(), calls=%async_computation.2 | async-start | bytes 5474304 | tf_op jit(solution)/shard_map/all_gather | solution.py:169
  7.9 153.2 %all-gather.14.cloned.1.call-start = ((), (), s32[]{:S(2)}) async-start(), calls=%async_computation.3 | async-start | bytes 2433024 | tf_op jit(solution)/shard_map/all_gather | solution.py:173
  8.7 250.1 %all-gather.18.cloned.1.call-start = ((), (), s32[]{:S(2)}) async-start(), calls=%async_computation.6 | async-start | bytes 7077888 | tf_op jit(solution)/shard_map/all_gather | solution.py:25
  10.1 117.5 %copy-start.152 = (f32[256]{0:T(256)}, f32[256]{0:T(256)S(1)}, u32[]{:S(2)}) copy-start(f32[256]{0:T(256)S(1)} %get-tuple-element.567) | copy-start | bytes 3076
  10.1 120.9 %copy-start.138 = (f32[256]{0:T(256)}, f32[256]{0:T(256)S(1)}, u32[]{:S(2)}) copy-start(f32[256]{0:T(256)S(1)} %fusion.182) | copy-start | bytes 3076
  54.9 72.7 %copy-start.124 = (f32[256]{0:T(256)}, f32[256]{0:T(256)S(1)}, u32[]{:S(2)}) copy-start(f32[256]{0:T(256)S(1)} %fusion.180) | copy-start | bytes 3076
  121.7 26.0 %copy-start.95 = (f32[1792]{0:T(1024)}, f32[1792]{0:T(1024)S(1)}, u32[]{:S(2)}) copy-start(f32[1792]{0:T(1024)S(1)} %get-tuple-element.573) | copy-start | bytes 21508
  121.7 26.0 %copy-start.97 = (f32[1792]{0:T(1024)}, f32[1792]{0:T(1024)S(1)}, u32[]{:S(2)}) copy-start(f32[1792]{0:T(1024)S(1)} %get-tuple-element.574) | copy-start | bytes 21508
  121.7 26.0 %copy-start.99 = (f32[1792]{0:T(1024)}, f32[1792]{0:T(1024)S(1)}, u32[]{:S(2)}) copy-start(f32[1792]{0:T(1024)S(1)} %get-tuple-element.575) | copy-start | bytes 21508
  121.7 26.0 %copy-start.101 = (f32[1792]{0:T(1024)}, f32[1792]{0:T(1024)S(1)}, u32[]{:S(2)}) copy-start(f32[1792]{0:T(1024)S(1)} %get-tuple-element.576) | copy-start | bytes 21508
  122.4 13.8 %copy-start.156 = (f32[24]{0:T(128)}, f32[24]{0:T(128)S(1)}, u32[]{:S(2)}) copy-start(f32[24]{0:T(128)S(1)} %exponential_negate_fusion) | copy-start | bytes 292
  122.4 8.6 %copy-start.16 = (bf16[2,1,256,768]{3,2,1,0:T(8,128)(2,1)S(1)}, bf16[2,1,256,768]{3,2,1,0:T(8,128)(2,1)}, u32[]{:S(2)}) copy-start(bf16[2,1,256,768]{3,2,1,0:T(8,128)(2,1)} %param.24) | copy-start | bytes 2359300
  122.4 8.6 %copy-start.164 = (bf16[768,3352]{1,0:T(8,128)(2,1)S(1)}, bf16[768,3352]{1,0:T(8,128)(2,1)}, u32[]{:S(2)}) copy-start(bf16[768,3352]{1,0:T(8,128)(2,1)} %all-gather.12.cloned.1.call-done) | copy-start | bytes 15446020
  127.6 15.1 %copy-start.40 = (bf16[1,256,3352]{1,2,0:T(8,128)(2,1)}, bf16[1,256,3352]{1,2,0:T(8,128)(2,1)S(1)}, u32[]{:S(2)}) copy-start(bf16[1,256,3352]{1,2,0:T(8,128)(2,1)S(1)} %fusion.6) | copy-start | bytes 5148676
  128.8 7.5 copy-start.141
  128.8 14.0 %collective-permute-start = (bf16[1,3,1792]{1,2,0:T(8,128)(2,1)}, bf16[1,3,1792]{1,2,0:T(8,128)(2,1)}, u32[]{:S(2)}, u32[]{:S(2)}) collective-permute-start(bf16[1,3,1792]{1,2,0:T(8,128)(2,1)} %slice.255), channel_id=1, source_target_pairs={{0,1},{1,2},{2,3},{3,4},{4,5},{5,6},{6,7},{8,9},{9,10},{10,11},{11... | collective-permute-start | bytes 32264 | tf_op jit(solution)/shard_map/ppermute | solution.py:20
  134.4 12.6 %collective-permute-start.1 = (bf16[1,3,1792]{1,2,0:T(8,128)(2,1)}, bf16[1,3,1792]{1,2,0:T(8,128)(2,1)S(1)}, u32[]{:S(2)}, u32[]{:S(2)}) collective-permute-start(bf16[1,3,1792]{1,2,0:T(8,128)(2,1)} %slice.271), channel_id=1, source_target_pairs={{0,1},{1,2},{2,3},{3,4},{4,5},{5,6},{6,7},{8,9},{9,10},{10,11},{11... | collective-permute-start | bytes 32264 | tf_op jit(solution)/shard_map/ppermute | solution.py:20
  138.0 4.7 copy-start.82
  142.7 10.7 %copy-start.94 = (f32[256,24]{0,1:T(8,128)}, f32[256,24]{0,1:T(8,128)S(1)}, u32[]{:S(2)}) copy-start(f32[256,24]{0,1:T(8,128)S(1)} %get-tuple-element.696) | copy-start | bytes 73732
  142.7 13.2 %copy-start.92 = (f32[256,24]{0,1:T(8,128)}, f32[256,24]{0,1:T(8,128)S(1)}, u32[]{:S(2)}) copy-start(f32[256,24]{0,1:T(8,128)S(1)} %get-tuple-element.668) | copy-start | bytes 73732
  147.7 5.7 copy-start
  155.8 202.2 %all-gather.16.cloned.1.call-start = ((), (), s32[]{:S(2)}) async-start(), calls=%async_computation.5 | async-start | bytes 7077888 | tf_op jit(solution)/shard_map/all_gather | solution.py:25
  160.2 304.8 %all-gather.22.cloned.1.call-start = ((), (), s32[]{:S(2)}) async-start(), calls=%async_computation.8 | async-start | bytes 3538944 | tf_op jit(solution)/shard_map/all_gather | solution.py:42
  161.1 4.4 copy-start.83
  211.5 4.6 copy-start.11
  375.4 81.0 %copy-start.3 = (f32[1,24,64,128]{3,2,1,0:T(8,128)}, f32[1,24,64,128]{3,2,1,0:T(8,128)S(1)}, u32[]{:S(2)}) copy-start(f32[1,24,64,128]{3,2,1,0:T(8,128)S(1)} %get-tuple-element.395) | copy-start | bytes 2359300
  385.9 5.5 copy-start.91
  393.6 120.0 %all-gather.20.cloned.1.call-start = ((), (), s32[]{:S(2)}) async-start(), calls=%async_computation.7 | async-start | bytes 3538944 | tf_op jit(solution)/shard_map/all_gather | solution.py:42
  397.9 295.8 %reduce-scatter.6.cloned.1.call-start = ((), (), s32[]{:S(2)}) async-start(), calls=%async_computation.4 | async-start | bytes 4866048 | tf_op jit(solution)/shard_map/reduce_scatter | solution.py:315
  405.7 37.7 %copy-start.19 = (bf16[1,256,1536]{1,2,0:T(8,128)(2,1)S(1)}, bf16[1,256,1536]{1,2,0:T(8,128)(2,1)}, u32[]{:S(2)}) copy-start(bf16[1,256,1536]{1,2,0:T(8,128)(2,1)} %copy-done.18) | copy-start | bytes 2359300
  405.7 37.7 %copy-start.33 = (bf16[1,256,1536]{1,2,0:T(8,128)(2,1)S(1)}, bf16[1,256,1536]{1,2,0:T(8,128)(2,1)}, u32[]{:S(2)}) copy-start(bf16[1,256,1536]{1,2,0:T(8,128)(2,1)} %get-tuple-element.675) | copy-start | bytes 2359300
  444.9 11.5 %copy-start.58 = (bf16[1,256,1536]{1,2,0:T(8,128)(2,1)S(1)}, bf16[1,256,1536]{1,2,0:T(8,128)(2,1)}, u32[]{:S(2)}) copy-start(bf16[1,256,1536]{1,2,0:T(8,128)(2,1)} %copy-done.57) | copy-start | bytes 2359300
  454.6 4.9 copy-start.74
  454.6 4.9 copy-start.75
  464.9 309.7 %reduce-scatter.8.cloned.1.call-start = ((), (), s32[]{:S(2)}) async-start(), calls=%async_computation.9 | async-start | bytes 10948608
  565.0 4.8 copy-start.24
  565.0 4.8 copy-start.72
  569.8 5.1 copy-start.96
  569.8 5.1 copy-start.98
  569.8 5.1 copy-start.100
  569.8 5.1 copy-start.102
  585.2 18.2 %collective-permute-start.3 = (f32[1,3,1792]{2,0,1:T(1,128)S(1)}, f32[1,3,1792]{2,0,1:T(1,128)S(1)}, u32[]{:S(2)}, u32[]{:S(2)}) collective-permute-start(f32[1,3,1792]{2,0,1:T(1,128)S(1)} %copy.217), channel_id=1, source_target_pairs={{1,0},{2,1},{3,2},{4,3},{5,4},{6,5},{7,6},{9,8},{10,9},{11,10},{12... | collective-permute-start | bytes 64520 | tf_op jit(solution)/shard_map/ppermute | solution.py:20
  595.9 6.0 copy-start.43
  595.9 6.0 copy-start.47
  595.9 6.0 copy-start.67
  596.0 6.0 copy-start.70
  596.0 6.0 copy-start.77
  596.0 6.0 copy-start.79
  596.0 6.0 copy-start.126
  596.0 6.0 copy-start.127
  596.0 6.0 copy-start.143
  596.0 6.0 copy-start.146
  596.0 6.0 copy-start.149
  596.0 6.0 copy-start.157
  596.0 15.9 %collective-permute-start.2 = (f32[1,3,1792]{2,0,1:T(1,128)S(1)}, f32[1,3,1792]{2,0,1:T(1,128)S(1)}, u32[]{:S(2)}, u32[]{:S(2)}) collective-permute-start(f32[1,3,1792]{2,0,1:T(1,128)S(1)} %copy.205), channel_id=1, source_target_pairs={{1,0},{2,1},{3,2},{4,3},{5,4},{6,5},{7,6},{9,8},{10,9},{11,10},{12... | collective-permute-start | bytes 64520 | tf_op jit(solution)/shard_map/ppermute | solution.py:20
  612.3 8.2 %copy-start.17 = (bf16[2,1,256,768]{3,2,1,0:T(8,128)(2,1)S(1)}, bf16[2,1,256,768]{3,2,1,0:T(8,128)(2,1)}, u32[]{:S(2)}) copy-start(bf16[2,1,256,768]{3,2,1,0:T(8,128)(2,1)} %param.24) | copy-start | bytes 2359300
  612.3 8.2 %copy-start.53 = (bf16[1,256,1536]{1,2,0:T(8,128)(2,1)S(1)}, bf16[1,256,1536]{1,2,0:T(8,128)(2,1)}, u32[]{:S(2)}) copy-start(bf16[1,256,1536]{1,2,0:T(8,128)(2,1)} %get-tuple-element.653) | copy-start | bytes 2359300
  612.4 8.2 %copy-start.106 = (bf16[1,256,24]{1,2,0:T(8,128)(2,1)S(1)}, bf16[1,256,24]{1,2,0:T(8,128)(2,1)}, u32[]{:S(2)}) copy-start(bf16[1,256,24]{1,2,0:T(8,128)(2,1)} %get-tuple-element.666) | copy-start | bytes 36868
  612.4 8.2 %copy-start.125 = (f32[256]{0:T(256)S(1)}, f32[256]{0:T(256)}, u32[]{:S(2)}) copy-start(f32[256]{0:T(256)} %copy-done.124) | copy-start | bytes 3076
  639.7 5.2 copy-start.71
  639.7 5.2 copy-start.162
  639.7 51.4 %copy-start.153 = (f32[256]{0:T(256)S(1)}, f32[256]{0:T(256)}, u32[]{:S(2)}) copy-start(f32[256]{0:T(256)} %copy-done.152) | copy-start | bytes 3076
  639.7 51.4 %copy-start.155 = (f32[256]{0:T(256)S(1)}, f32[256]{0:T(256)}, u32[]{:S(2)}) copy-start(f32[256]{0:T(256)} %copy-done.154) | copy-start | bytes 3076
  639.7 51.4 %copy-start.23 = (bf16[2,1,256,768]{3,2,1,0:T(8,128)(2,1)S(1)}, bf16[2,1,256,768]{3,2,1,0:T(8,128)(2,1)}, u32[]{:S(2)}) copy-start(bf16[2,1,256,768]{3,2,1,0:T(8,128)(2,1)} %param.25) | copy-start | bytes 2359300
  (118 other events, 287.0 us)
Sparse Core Ops, SparseCore 0:
  10.9 68.5 all-gather.11
  82.4 58.6 all-gather.13
  156.0 102.7 all-gather.17
  260.8 97.1 all-gather.15
  393.8 58.6 all-gather.21
  454.5 59.0 all-gather.19
  519.7 106.1 reduce-scatter.5
  633.5 141.0 reduce-scatter.7
where the time goes:
time: 793 us; the launch traced here: 782 us
  waiting for transfers between devices  227 us (29%)
  blocking collectives  227 us (29%)
  other arithmetic  142 us (18%)
  matrix products  90.9 us (11%)
  local copies, waits for them, and re-layouts  70.3 us (9%)
  between operations  16.6 us (2%)
    all_gather x2, waiting for transfers between devices, prefix(): pieces = jax.tree.map(lambda part: lax.all_gather(part, axis), value)  111 us
    unnamed x2, blocking collectives  86 us
    unnamed x9, waiting for transfers between devices  82.4 us
    all_gather x1, blocking collectives, local(): lax.all_gather(shards[2], ('dp', 'seq'), axis=0, tiled=True)  66.5 us
    all_gather x2, blocking collectives, prefix(): pieces = jax.tree.map(lambda part: lax.all_gather(part, axis), value)  38.8 us
    all_gather x2, blocking collectives, entering(): lax.all_gather(a.astype(kind), axis)  36 us
    all_gather x2, waiting for transfers between devices, entering(): lax.all_gather(a.astype(kind), axis)  30.9 us
    select_n x14, other arithmetic, turn(): jnp.where(position < mine, new, old)  25.9 us
  transfers between devices with their start and end apart: 12, of which 5 were waited for; matrix products, arithmetic and copies ran while one was open for 33% of the time, Pallas kernels for 0%

commit v1 on v0

v1 whole, which is shorter than its diff:
```python
import math

import jax
import jax.numpy as jnp
from jax import lax
from jax.experimental import pallas as pl
from jax.experimental.pallas import tpu as pltpu
from jax.sharding import Mesh
from jax.sharding import PartitionSpec as P

H = 24
HP = 64
N = 128
KW = 4
SEQ_LEN = 2048
PIECE = 256
D = 768
DI = H * HP
CONV = DI + 2 * N
PC = 1920
GROUPS = 3
GC = PC // GROUPS
NEAR = SEQ_LEN // PIECE
NB = N // NEAR
HALO = 16
LANES = 128
EPS = 1e-05
F32 = jnp.float32
BF16 = jnp.bfloat16
AX = ("dp", "far", "near")
MIB = 1 << 20


def dot(a, b):
    return lax.dot_general(a, b, (((1,), (0,)), ((), ())), preferred_element_type=F32)


def dot_nt(a, b):
    return lax.dot_general(a, b, (((1,), (1,)), ((), ())), preferred_element_type=F32)


def dot_tn(a, b):
    return lax.dot_general(a, b, (((0,), (0,)), ((), ())), preferred_element_type=F32)


def split(x):
    high = x.astype(BF16)
    return high, (x - high.astype(F32)).astype(BF16)


def heads_to_lanes():
    head = lax.broadcasted_iota(jnp.int32, (LANES, DI), 0)
    lane = lax.broadcasted_iota(jnp.int32, (LANES, DI), 1)
    return jnp.where((lane >> 6) == head, 1.0, 0.0).astype(BF16)


def expand(x, spread):
    high, low = split(x)
    return dot(high, spread) + dot(low, spread)


def collect(high, low, spread):
    return dot_nt(high, spread) + dot_nt(low, spread)


def triangle(count, lower):
    row = lax.broadcasted_iota(jnp.int32, (count, count), 0)
    col = lax.broadcasted_iota(jnp.int32, (count, count), 1)
    return (row >= col) if lower else (row <= col)


def running(mask, x):
    ones = jnp.where(mask, 1.0, 0.0).astype(BF16)
    high, rest = split(x)
    left = x - high.astype(F32)
    mid, low = split(left)
    return dot(ones, high) + dot(ones, mid) + dot(ones, low)


def softplus(z):
    e = jnp.exp(-jnp.abs(z))
    near = e * (1.0 + e * (-0.5 + e * (1.0 / 3.0 + e * (-0.25 + e * 0.2))))
    return jnp.maximum(z, 0.0) + jnp.where(e < 0.02, near, jnp.log(1.0 + e))


def params(limit):
    return pltpu.CompilerParams(vmem_limit_bytes=limit * MIB)


def cost(flops, nbytes, trans=0):
    return pl.CostEstimate(flops=int(flops), bytes_accessed=int(nbytes), transcendentals=int(trans))


def whole(shape):
    return pl.BlockSpec(shape, lambda *_: (0,) * len(shape))


def per_row(shape):
    return pl.BlockSpec((1,) + shape, lambda r: (r,) + (0,) * len(shape))


def struct(shape, kind):
    return jax.ShapeDtypeStruct(shape, kind)


def assemble(core, mine, recv, weight_s):
    count, rows, _ = mine[0].shape
    for g in range(GROUPS):
        cols = slice(g * GC, (g + 1) * GC)
        for y in range(count):
            first = pl.multiple_of((2 * y + core) * rows, 16)
            other = pl.multiple_of((2 * y + 1 - core) * rows, 16)
            weight_s[pl.ds(first, rows), cols] = mine[g][y]
            weight_s[pl.ds(other, rows), cols] = recv[g][y]


def enter_kernel(
    core_ref, tok, halo, m0, m1, m2, r0, r1, r2, par, heads,
    hid, conv, raw, act, dsilu, step, cum, pay, weight, ext
):
    @pl.when(pl.program_id(0) == 0)
    def _():
        assemble(core_ref[0], (m0, m1, m2), (r0, r1, r2), weight)

    gain = par[5:6, :D].astype(F32)
    rows = jnp.concatenate([halo[0], tok[0]], axis=0).astype(F32)
    scale = lax.rsqrt(jnp.mean(rows * rows, axis=-1, keepdims=True) + EPS)
    hidden = (rows * scale * gain).astype(BF16)
    hid[0] = hidden[HALO:]
    for t in range(CONV // 256):
        cols = slice(t * 256, (t + 1) * 256)
        part = dot(hidden, weight[:, cols]).astype(BF16)
        conv[0, :, cols] = part
        ext[:, cols] = part.astype(F32)
    for t in range(CONV // LANES):
        cols = slice(t * LANES, (t + 1) * LANES)
        total = par[4:5, cols].astype(F32)
        for k in range(KW):
            total = total + par[k : k + 1, cols].astype(F32) * ext[pl.ds(HALO - KW + 1 + k, PIECE), cols]
        gate = jax.nn.sigmoid(total)
        act[0, :, cols] = (total * gate).astype(BF16)
        dsilu[0, :, cols] = gate * (1.0 + total * (1.0 - gate))
    raw_step = dot(hidden[HALO:], weight[:, CONV:]).astype(BF16).astype(F32)
    raw[0] = raw_step
    size = softplus(raw_step + heads[0:1])
    cumul = running(triangle(PIECE, True), size * -jnp.exp(heads[1:2]))
    step[0] = size
    cum[0] = cumul
    spread = heads_to_lanes()
    last = cumul[PIECE - 1 :]
    reach = jnp.exp(last - cumul) * size
    bmat = act[0, :, DI : DI + N]
    for t in range(DI // 256):
        cols = slice(t * 256, (t + 1) * 256)
        weights = (expand(reach, spread[:, cols]) * act[0, :, cols].astype(F32)).astype(BF16)
        state = dot_tn(bmat, weights).astype(BF16)
        pay[:, 0, :, cols] = state.reshape(NEAR, NB, 256)
    growth = jnp.exp(last)
    high, low = split(growth)
    row = lax.broadcasted_iota(jnp.int32, (NB, LANES), 0)
    growths = jnp.where(row == 0, high.astype(F32), jnp.where(row == 1, low.astype(F32), 0.0))
    for j in range(NEAR):
        pay[j, 0, :, DI:] = growths.astype(BF16)


def pass_kernel(backward, pieces, growths, out):
    spread = heads_to_lanes()
    count = out.shape[1]
    for r in range(count):
        high = jnp.concatenate([growths[j, r, 0:1, :] for j in range(NEAR)], axis=0)
        low = jnp.concatenate([growths[j, r, 1:2, :] for j in range(NEAR)], axis=0)
        grow = dot(high, spread) + dot(low, spread)
        state = jnp.zeros((NB, DI), F32)
        order = range(NEAR - 1, -1, -1) if backward else range(NEAR)
        for j in order:
            out[j, r] = state.astype(BF16)
            state = grow[j : j + 1] * state + pieces[j, r, :, :DI].astype(F32)


def inside_kernel(act, step, cum, intra, xdt_s):
    spread = heads_to_lanes()
    size, cumul = step[0], cum[0]
    for t in range(DI // 256):
        cols = slice(t * 256, (t + 1) * 256)
        xdt_s[:, cols] = (expand(size, spread[:, cols]) * act[0, :, cols].astype(F32)).astype(BF16)
    bmat, cmat = act[0, :, DI : DI + N], act[0, :, DI + N :]
    scores = dot_nt(cmat, bmat)
    lower = triangle(PIECE, True)
    turned = cumul.T
    left = lax.broadcasted_iota(jnp.int32, (PIECE, LANES), 1) < HP
    for pair in range(H // 2):
        cols = slice(pair * LANES, (pair + 1) * LANES)
        xdt = xdt_s[:, cols]
        both = []
        for h in (2 * pair, 2 * pair + 1):
            differ = cumul[:, h : h + 1] - turned[h : h + 1, :]
            mix = (scores * jnp.exp(jnp.where(lower, differ, -1e30))).astype(BF16)
            both.append(dot(mix, xdt))
        intra[0, :, cols] = jnp.where(left, both[0], both[1])


def gate_kernel(hid, cot, wg0, wg1, wo, gate, dnorm):
    gate[0, :, :D] = dot(hid[0], wg0[...]).astype(BF16)
    gate[0, :, D:] = dot(hid[0], wg1[...]).astype(BF16)
    dnorm[0] = dot_nt(cot[0], wo[...])


def middle_kernel(
    st, act, intra, cum, gate, dnorm, par, heads,
    normed, dgate, dy, reach, pay, sums, off_s, grow_s, high_s, low_s, doff_s, sum_s
):
    spread = heads_to_lanes()
    state = st[:, 0].reshape(N, DI)
    cmat = act[0, :, DI + N :]
    off_s[...] = dot(cmat, state)
    grow_s[...] = expand(jnp.exp(cum[0]), spread)
    skip = expand(jnp.broadcast_to(heads[2:3], (8, LANES)), spread)[0:1]
    gain = par[6:7, :DI].astype(F32)
    sum_s[...] = jnp.zeros_like(sum_s)
    size = 16

    def chunk(i, carry):
        at = pl.ds(pl.multiple_of(i * size, size), size)
        value = act[0, at, :DI].astype(F32)
        grow = grow_s[at, :]
        base = intra[0, at, :] + grow * off_s[at, :]
        ssd = base + skip * value
        z = gate[0, at, :].astype(F32)
        sig = jax.nn.sigmoid(z)
        silu = z * sig
        gated = ssd * silu
        scale = lax.rsqrt(jnp.mean(gated * gated, axis=-1, keepdims=True) + EPS)
        unit = gated * scale
        normed[0, at, :] = (unit * gain).astype(BF16)
        d_normed = dnorm[0, at, :]
        sum_s[0:8] += (d_normed * unit).reshape(size // 8, 8, DI).sum(axis=0)
        d_unit = d_normed * gain
        along = jnp.mean(d_unit * unit, axis=-1, keepdims=True)
        d_gated = scale * (d_unit - unit * along)
        dgate[0, at, :] = (d_gated * ssd * (sig * (1.0 + z * (1.0 - sig)))).astype(BF16)
        d_ssd = (d_gated * silu).astype(BF16)
        dy[0, at, :] = d_ssd
        d_ssd = d_ssd.astype(F32)
        doff_s[at, :] = (grow * d_ssd).astype(BF16)
        sum_s[8:16] += (d_ssd * value).reshape(size // 8, 8, DI).sum(axis=0)
        high, low = split(d_ssd * base)
        high_s[at, :] = high
        low_s[at, :] = low
        return carry

    lax.fori_loop(0, PIECE // size, chunk, 0)
    d_state = dot_tn(cmat, doff_s[...]).astype(BF16)
    pay[:, 0] = d_state.reshape(NEAR, NB, DI)
    reach[0] = collect(high_s[...], low_s[...], spread)
    high, low = split(sum_s[8:16])
    sums[0, 0:8] = sum_s[0:8]
    sums[0, 8:16, :LANES] = collect(high, low, spread)
    sums[0, 8:16, LANES:] = jnp.zeros((8, DI - LANES), F32)


def outer_kernel(core_ref, tok, cot, hid, normed, dgate, wo, out, keep, send, total):
    core = core_ref[0]
    count = tok.shape[0]
    for r in range(count):
        out[r] = (tok[r].astype(F32) + dot(normed[r], wo[...])).astype(BF16)
    tangent = cot[...].reshape(count * PIECE, D)
    hidden = hid[...].reshape(count * PIECE, D)
    blocks = keep.shape[0]
    left = [
        dot_tn(normed[...].reshape(count * PIECE, DI), tangent),
        dot_tn(hidden, dgate[:, :, :D].reshape(count * PIECE, D)),
        dot_tn(hidden, dgate[:, :, D:].reshape(count * PIECE, D)),
    ]
    base = 0
    for part in left:
        total[: part.shape[0]] = part
        rows = part.shape[0] // (2 * blocks)
        for y in range(blocks):
            mine = pl.multiple_of((2 * y + core) * rows, 16)
            other = pl.multiple_of((2 * y + 1 - core) * rows, 16)
            keep[y, base : base + rows] = total[pl.ds(mine, rows)]
            send[y, base : base + rows] = total[pl.ds(other, rows)].astype(BF16)
        base += rows


def pair_kernel(act, step, cum, dy, st, u, dcm, dbm, xdt_s, doff_s, dsc_s):
    spread = heads_to_lanes()
    size, cumul = step[0], cum[0]
    grown = jnp.exp(cumul)
    for t in range(DI // 256):
        cols = slice(t * 256, (t + 1) * 256)
        xdt_s[:, cols] = (expand(size, spread[:, cols]) * act[0, :, cols].astype(F32)).astype(BF16)
        doff_s[:, cols] = (expand(grown, spread[:, cols]) * dy[0, :, cols].astype(F32)).astype(BF16)
    bmat, cmat = act[0, :, DI : DI + N], act[0, :, DI + N :]
    scores = dot_nt(cmat, bmat)
    lower = triangle(PIECE, True)
    turned = cumul.T
    dsc_s[...] = jnp.zeros_like(dsc_s)
    left = lax.broadcasted_iota(jnp.int32, (PIECE, LANES), 1) < HP
    zero = jnp.zeros((PIECE, LANES), BF16)
    for pair in range(H // 2):
        cols = slice(pair * LANES, (pair + 1) * LANES)
        xdt = xdt_s[:, cols]
        slope = dy[0, :, cols]
        slope_t = slope.astype(F32).T.astype(BF16)
        both = []
        for side in (0, 1):
            h = 2 * pair + side
            differ = cumul[:, h : h + 1] - turned[h : h + 1, :]
            decay = jnp.exp(jnp.where(lower, differ, -1e30))
            mix = (scores * decay).astype(BF16)
            own = jnp.where(left, slope, zero) if side == 0 else jnp.where(left, zero, slope)
            dsc_s[...] += dot_nt(own, xdt) * decay
            both.append(dot(slope_t[side * HP : (side + 1) * HP], mix))
        u[0, :, cols] = jnp.concatenate(both, axis=0).T
    d_scores = dsc_s[...].astype(BF16)
    state = st[:, 0].reshape(N, DI)
    dcm[0] = dot_nt(doff_s[...], state) + dot(d_scores, bmat)
    dbm[0] = dot_tn(d_scores, cmat)


def back_kernel(
    later, st, act, cum, step, raw, u, dcm, dbm, dy, dsilu, reach, heads,
    dpre, edge, draw, hsum, dw_s, far_s, size_s, high_s, low_s, wts_s, sum_s
):
    spread = heads_to_lanes()
    size, cumul = step[0], cum[0]
    last = cumul[PIECE - 1 :]
    d_local = later[:, 0].reshape(N, DI)
    bmat = act[0, :, DI : DI + N]
    dw_s[...] = dot(bmat, d_local)
    far_s[...] = expand(jnp.exp(last - cumul), spread)
    size_s[...] = expand(size, spread)
    skip = expand(jnp.broadcast_to(heads[2:3], (8, LANES)), spread)[0:1]
    sum_s[...] = jnp.zeros_like(sum_s)
    rows = 16

    def chunk(i, carry):
        at = pl.ds(pl.multiple_of(i * rows, rows), rows)
        value = act[0, at, :DI].astype(F32)
        far, long = far_s[at, :], size_s[at, :]
        through = far * dw_s[at, :]
        d_xdt = u[0, at, :] + through
        d_value = long * d_xdt + skip * dy[0, at, :].astype(F32)
        dpre[0, at, :DI] = d_value * dsilu[0, at, :DI]
        high, low = split(value * d_xdt)
        high_s[at, :] = high
        low_s[at, :] = low
        xdt = long * value
        wts_s[at, :] = (far * xdt).astype(BF16)
        sum_s[0:8] += (xdt * through).reshape(rows // 8, 8, DI).sum(axis=0)
        return carry

    lax.fori_loop(0, PIECE // rows, chunk, 0)
    for j in range(NEAR):
        prod = later[j, 0].astype(F32) * st[j, 0].astype(F32)
        sum_s[8:16] += prod.reshape(NB // 8, 8, DI).sum(axis=0)
    d_bmat = dbm[0] + dot_nt(wts_s[...], d_local)
    dpre[0, :, DI : DI + N] = d_bmat * dsilu[0, :, DI : DI + N]
    dpre[0, :, DI + N :] = dcm[0] * dsilu[0, :, DI + N :]
    edge[0] = dpre[0, 0:8, :]
    q = collect(high_s[...], low_s[...], spread)
    high, low = split(sum_s[...])
    sums = collect(high, low, spread)
    d_last = jnp.sum(sums[0:8], axis=0, keepdims=True)
    d_last = d_last + jnp.exp(last) * jnp.sum(sums[8:16], axis=0, keepdims=True)
    d_cum = reach[0] - size * q
    row = lax.broadcasted_iota(jnp.int32, (PIECE, LANES), 0)
    d_cum = d_cum + jnp.where(row == PIECE - 1, d_last, 0.0)
    d_rate = running(triangle(PIECE, False), d_cum)
    decay = jnp.exp(heads[1:2])
    d_size = q - d_rate * decay
    d_raw = d_size * jax.nn.sigmoid(raw[0] + heads[0:1])
    draw[0] = d_raw
    for_bias = jnp.sum(d_raw, axis=0, keepdims=True)
    for_log = -jnp.sum(d_rate * size, axis=0, keepdims=True) * decay
    pick = lax.broadcasted_iota(jnp.int32, (8, LANES), 0)
    hsum[0] = jnp.where(pick == 0, for_bias, jnp.where(pick == 1, for_log, 0.0))


def input_kernel(core_ref, dpre, edge, draw, hid, par, dproj, k0, k1, k2, s0, s1, s2, ext, total):
    core = core_ref[0]
    count = dpre.shape[0]
    for r in range(count):
        ext[:PIECE] = dpre[r]
        ext[PIECE:] = edge[r]
        for t in range(CONV // LANES):
            cols = slice(t * LANES, (t + 1) * LANES)
            sum_k = par[KW - 1 : KW, cols].astype(F32) * ext[0:PIECE, cols]
            for k in range(KW - 1):
                sum_k = sum_k + par[k : k + 1, cols].astype(F32) * ext[pl.ds(KW - 1 - k, PIECE), cols]
            dproj[r, :, cols] = sum_k.astype(BF16)
        dproj[r, :, CONV:] = draw[r].astype(BF16)
    hidden = hid[...].reshape(count * PIECE, D)
    for g, (keep, send) in enumerate(((k0, s0), (k1, s1), (k2, s2))):
        total[...] = dot_tn(hidden, dproj[:, :, g * GC : (g + 1) * GC].reshape(count * PIECE, GC))
        blocks, rows, _ = keep.shape
        for y in range(blocks):
            mine = pl.multiple_of((2 * y + core) * rows, 16)
            other = pl.multiple_of((2 * y + 1 - core) * rows, 16)
            keep[y] = total[pl.ds(mine, rows)]
            send[y] = total[pl.ds(other, rows)].astype(BF16)


def token_kernel(
    tok, cot, dgate, dproj, wg0, wg1, weight, par, dpre, conv, sums, hsum,
    grad, small, dh_s, ext, acc
):
    r = pl.program_id(0)
    dh_s[...] = (
        dot_nt(dgate[0, :, :D], wg0[...])
        + dot_nt(dgate[0, :, D:], wg1[...])
        + dot_nt(dproj[0], weight[...])
    )
    gain = par[5:6, :D].astype(F32)

    @pl.when(r == 0)
    def _():
        acc[...] = jnp.zeros_like(acc)
        small[...] = jnp.zeros_like(small)

    rows = 32

    def chunk(i, carry):
        at = pl.ds(pl.multiple_of(i * rows, rows), rows)
        x = tok[0, at, :].astype(F32)
        scale = lax.rsqrt(jnp.mean(x * x, axis=-1, keepdims=True) + EPS)
        unit = x * scale
        d_hidden = dh_s[at, :]
        acc[...] += (d_hidden * unit).reshape(rows // 8, 8, D).sum(axis=0)
        d_unit = d_hidden * gain
        along = jnp.mean(d_unit * unit, axis=-1, keepdims=True)
        grad[0, at, :] = (cot[0, at, :].astype(F32) + scale * (d_unit - unit * along)).astype(BF16)
        return carry

    lax.fori_loop(0, PIECE // rows, chunk, 0)
    for t in range(CONV // LANES):
        cols = slice(t * LANES, (t + 1) * LANES)
        slope = dpre[0, :, cols]
        ext[...] = conv[0, :, cols].astype(F32)
        for k in range(KW):
            prod = slope * ext[pl.ds(HALO - KW + 1 + k, PIECE), :]
            small[k : k + 1, cols] += jnp.sum(prod, axis=0, keepdims=True)
        small[4:5, cols] += jnp.sum(slope, axis=0, keepdims=True)
    small[6:7, :DI] += jnp.sum(sums[0, 0:8], axis=0, keepdims=True)
    small[7:8, 0:LANES] += hsum[0, 0:1]
    small[7:8, LANES : 2 * LANES] += hsum[0, 1:2]
    small[7:8, 2 * LANES : 3 * LANES] += jnp.sum(sums[0, 8:16, :LANES], axis=0, keepdims=True)

    @pl.when(r == pl.num_programs(0) - 1)
    def _():
        small[5:6, :D] = jnp.sum(acc[...], axis=0, keepdims=True)


def local(size, tokens, cotangent, norm_in, w_in, conv_w, conv_b, dt_bias, a_log, skip, norm_out, w_out):
    devices, along = size
    bits = int(math.log2(devices))
    core_bit = int(math.log2(along))
    me = lax.axis_index(AX)
    core = ((me >> core_bit) & 1).astype(jnp.int32)
    core_arg = core.reshape(1)
    high_bits = list(range(bits - 1, core_bit, -1))
    far_bits = list(range(core_bit - 1, -1, -1))
    dims = [far_bits[-1:], far_bits[:-1], high_bits] if core_bit == 3 else [far_bits[-3:], far_bits[:-3], high_bits]
    orders = [
        dims[1] + dims[2] + dims[0],
        dims[0] + dims[1] + dims[2],
        dims[2] + dims[0] + dims[1],
    ]

    def swap(x, bit):
        return lax.ppermute(x, AX, [(i, i ^ (1 << bit)) for i in range(devices)])

    def bit_of(bit):
        return (me >> bit) & 1

    def gather(x, order):
        have = []
        for bit in order:
            other = swap(x, bit)
            have = sorted(have + [bit], reverse=True)
            mine = bit_of(bit) == 0
            low, high = jnp.where(mine, x, other), jnp.where(mine, other, x)
            x = jnp.stack([low, high], axis=have.index(bit))
        return x

    def scatter(x, order):
        have = sorted(order, reverse=True)
        for bit in order:
            axis = have.index(bit)
            mine = lax.dynamic_index_in_dim(x, bit_of(bit), axis, False)
            other = lax.dynamic_index_in_dim(x, 1 - bit_of(bit), axis, False)
            x = mine + swap(other.astype(BF16), bit).astype(F32)
            have.remove(bit)
        return x

    micro, batch, count = tokens.shape[:3]
    tok = tokens.reshape(micro * batch, count, D)
    cot = cotangent.reshape(micro * batch, count, D)
    R = micro * batch
    heads = jnp.zeros((8, LANES), F32)
    for i, a in enumerate((dt_bias, a_log, skip)):
        heads = heads.at[i, :H].set(a)

    own_conv, own_in, own_out = conv_b.shape[0], norm_in.shape[0], norm_out.shape[0]
    par = jnp.zeros((8, CONV), BF16)
    taps = jnp.concatenate([conv_w.T, conv_b[None]], axis=0)
    par = lax.dynamic_update_slice(par, taps, (0, me * own_conv))
    par = lax.dynamic_update_slice(par, norm_in[None], (5, me * own_in))
    par = lax.dynamic_update_slice(par, norm_out[None], (6, me * own_out))
    for bit in range(bits):
        par = par + swap(par, bit)

    halo = lax.ppermute(tok[:, count - HALO :], "near", [(i, i + 1) for i in range(NEAR - 1)])
    rows_in = w_in.shape[0]
    first = jnp.pad(w_in[:, DI:], ((0, 0), (0, PC - (w_in.shape[1] - DI))))
    blocks = devices // (2 * along)
    mine, recv = [], []
    for g in range(GROUPS):
        part = gather(first[:, g * GC : (g + 1) * GC], orders[g])
        part = part.reshape(blocks, along * rows_in, GC)
        mine.append(part)
        recv.append(swap(part, core_bit))

    rest = jnp.concatenate([w_in[:, :D], w_in[:, D:DI], w_out], axis=0)
    rest = lax.all_gather(rest, AX, axis=0, tiled=False)
    wg0 = rest[:, :rows_in].reshape(D, D)
    wg1 = rest[:, rows_in : 2 * rows_in].reshape(D, D)
    wo = rest[:, 2 * rows_in :].reshape(DI, D)

    smem = pl.BlockSpec(memory_space=pltpu.SMEM)
    half = (blocks, along * rows_in, GC)
    par_spec, head_spec = whole((8, CONV)), whole((8, LANES))
    row_d, row_i, row_c = per_row((PIECE, D)), per_row((PIECE, DI)), per_row((PIECE, CONV))
    row_l = per_row((PIECE, LANES))
    state_spec = pl.BlockSpec((NEAR, 1, NB, DI), lambda r: (0, r, 0, 0))
    hid, conv, raw, act, dsilu, step, cum, pay, weight = pl.pallas_call(
        enter_kernel,
        grid=(R,),
        in_specs=[smem, row_d, per_row((HALO, D))] + [whole(half)] * 6 + [par_spec, head_spec],
        out_specs=[
            row_d, per_row((HALO + PIECE, CONV)), row_l, row_c, row_c, row_l, row_l,
            pl.BlockSpec((NEAR, 1, NB, DI + LANES), lambda r: (0, r, 0, 0)),
            whole((D, PC)),
        ],
        out_shape=[
            struct((R, PIECE, D), BF16), struct((R, HALO + PIECE, CONV), BF16), struct((R, PIECE, LANES), F32),
            struct((R, PIECE, CONV), BF16), struct((R, PIECE, CONV), F32), struct((R, PIECE, LANES), F32),
            struct((R, PIECE, LANES), F32), struct((NEAR, R, NB, DI + LANES), BF16), struct((D, PC), BF16),
        ],
        scratch_shapes=[pltpu.VMEM((HALO + PIECE, CONV), F32)],
        compiler_params=params(44),
        cost_estimate=cost(R * 2e9, 2e7),
        name="enter",
    )(core_arg, tok, halo, *mine, *recv, par, heads)

    def exchange(x):
        return lax.all_to_all(x, "near", split_axis=0, concat_axis=0, tiled=True)

    def carry_on(pieces, growths, backward):
        shape = pieces.shape
        def kernel(p, g, o):
            pass_kernel(backward, p, g, o)
        return pl.pallas_call(
            kernel,
            grid=(1,),
            in_specs=[whole(shape), pl.BlockSpec((NEAR, R, NB, LANES), lambda r: (0, 0, 0, DI // LANES))],
            out_specs=whole((NEAR, R, NB, DI)),
            out_shape=struct((NEAR, R, NB, DI), BF16),
            compiler_params=params(16),
            cost_estimate=cost(1e7, 2e6),
            name="pass",
        )(pieces, growths)

    pieces = exchange(pay)
    intra = pl.pallas_call(
        inside_kernel,
        grid=(R,),
        in_specs=[row_c, row_l, row_l],
        out_specs=row_i,
        out_shape=struct((R, PIECE, DI), F32),
        scratch_shapes=[pltpu.VMEM((PIECE, DI), BF16)],
        compiler_params=params(32),
        cost_estimate=cost(R * 4e9, 5e6),
        name="inside",
    )(act, step, cum)
    gate, dnorm = pl.pallas_call(
        gate_kernel,
        grid=(R,),
        in_specs=[row_d, row_d, whole((D, D)), whole((D, D)), whole((DI, D))],
        out_specs=[row_i, row_i],
        out_shape=[struct((R, PIECE, DI), BF16), struct((R, PIECE, DI), F32)],
        compiler_params=params(32),
        cost_estimate=cost(R * 2e9, 1e7),
        name="gates",
    )(hid, cot, wg0, wg1, wo)
    st = exchange(carry_on(pieces, pieces, False))

    wide = pltpu.VMEM((PIECE, DI), F32)
    slim = pltpu.VMEM((PIECE, DI), BF16)
    normed, dgate, dy, reach, back, sums = pl.pallas_call(
        middle_kernel,
        grid=(R,),
        in_specs=[state_spec, row_c, row_i, row_l, row_i, row_i, par_spec, head_spec],
        out_specs=[row_i, row_i, row_i, row_l, state_spec, per_row((16, DI))],
        out_shape=[
            struct((R, PIECE, DI), BF16), struct((R, PIECE, DI), BF16), struct((R, PIECE, DI), BF16),
            struct((R, PIECE, LANES), F32), struct((NEAR, R, NB, DI), BF16), struct((R, 16, DI), F32),
        ],
        scratch_shapes=[wide, wide, slim, slim, slim, pltpu.VMEM((16, DI), F32)],
        compiler_params=params(40),
        cost_estimate=cost(R * 2e9, 1.5e7),
        name="middle",
    )(st, act, intra, cum, gate, dnorm, par, heads)

    pieces_b = exchange(back)
    rest_rows = (DI + 2 * D) // (2 * blocks)
    block_out, keep, send = pl.pallas_call(
        outer_kernel,
        grid=(1,),
        in_specs=[
            smem, whole((R, PIECE, D)), whole((R, PIECE, D)), whole((R, PIECE, D)),
            whole((R, PIECE, DI)), whole((R, PIECE, DI)), whole((DI, D)),
        ],
        out_specs=[whole((R, PIECE, D)), whole((blocks, rest_rows, D)), whole((blocks, rest_rows, D))],
        out_shape=[
            struct((R, PIECE, D), BF16), struct((blocks, rest_rows, D), F32), struct((blocks, rest_rows, D), BF16),
        ],
        scratch_shapes=[pltpu.VMEM((DI, D), F32)],
        compiler_params=params(48),
        cost_estimate=cost(6e9, 2e7),
        name="outer",
    )(core_arg, tok, cot, hid, normed, dgate, wo)
    part = (keep + swap(send, core_bit).astype(F32)).reshape((2,) * len(high_bits) + (rest_rows, D))
    part = scatter(part, high_bits)
    cuts = (DI // (2 * blocks), D // (2 * blocks))
    part = jnp.concatenate(
        [
            part[: cuts[0]].reshape(along, cuts[0] // along, D),
            part[cuts[0] : cuts[0] + cuts[1]].reshape(along, rows_in, D),
            part[cuts[0] + cuts[1] :].reshape(along, rows_in, D),
        ],
        axis=1,
    )
    own = lax.psum_scatter(part, ("far", "near"), scatter_dimension=0, tiled=False)
    rows_out = w_out.shape[0]
    g_wout = own[:rows_out]
    g_gate = jnp.concatenate([own[rows_out : rows_out + rows_in], own[rows_out + rows_in :]], axis=1)

    u, dcm, dbm = pl.pallas_call(
        pair_kernel,
        grid=(R,),
        in_specs=[row_c, row_l, row_l, row_i, state_spec],
        out_specs=[row_i, row_l, row_l],
        out_shape=[struct((R, PIECE, DI), F32), struct((R, PIECE, N), F32), struct((R, PIECE, N), F32)],
        scratch_shapes=[slim, slim, pltpu.VMEM((PIECE, PIECE), F32)],
        compiler_params=params(40),
        cost_estimate=cost(R * 8e9, 1e7),
        name="pair",
    )(act, step, cum, dy, st)
    later = exchange(carry_on(pieces_b, pieces, True))

    dpre, edge, draw, hsum = pl.pallas_call(
        back_kernel,
        grid=(R,),
        in_specs=[
            state_spec, state_spec, row_c, row_l, row_l, row_l, row_i, row_l, row_l, row_i, row_c, row_l, head_spec,
        ],
        out_specs=[row_c, per_row((8, CONV)), row_l, per_row((8, LANES))],
        out_shape=[
            struct((R, PIECE, CONV), F32), struct((R, 8, CONV), F32),
            struct((R, PIECE, LANES), F32), struct((R, 8, LANES), F32),
        ],
        scratch_shapes=[wide, wide, wide, slim, slim, slim, pltpu.VMEM((16, DI), F32)],
        compiler_params=params(44),
        cost_estimate=cost(R * 2e9, 1.5e7),
        name="back",
    )(later, st, act, cum, step, raw, u, dcm, dbm, dy, dsilu, reach, heads)
    edge = lax.ppermute(edge, "near", [(i + 1, i) for i in range(NEAR - 1)])

    dproj, k0, k1, k2, s0, s1, s2 = pl.pallas_call(
        input_kernel,
        grid=(1,),
        in_specs=[
            smem, whole((R, PIECE, CONV)), whole((R, 8, CONV)), whole((R, PIECE, LANES)), whole((R, PIECE, D)), par_spec,
        ],
        out_specs=[whole((R, PIECE, PC))] + [whole(half)] * 6,
        out_shape=[struct((R, PIECE, PC), BF16)] + [struct(half, F32)] * 3 + [struct(half, BF16)] * 3,
        scratch_shapes=[pltpu.VMEM((PIECE + 8, CONV), F32), pltpu.VMEM((D, GC), F32)],
        compiler_params=params(44),
        cost_estimate=cost(2e9, 1e7),
        name="input",
    )(core_arg, dpre, edge, draw, hid, par)

    grad_tokens, small = pl.pallas_call(
        token_kernel,
        grid=(R,),
        in_specs=[
            row_d, row_d, row_i, per_row((PIECE, PC)), whole((D, D)), whole((D, D)), whole((D, PC)), par_spec,
            row_c, per_row((HALO + PIECE, CONV)), per_row((16, DI)), per_row((8, LANES)),
        ],
        out_specs=[row_d, whole((8, CONV))],
        out_shape=[struct((R, PIECE, D), BF16), struct((8, CONV), F32)],
        scratch_shapes=[
            pltpu.VMEM((PIECE, D), F32), pltpu.VMEM((HALO + PIECE, LANES), F32), pltpu.VMEM((8, D), F32),
        ],
        compiler_params=params(48),
        cost_estimate=cost(R * 2e9, 1.5e7),
        name="token",
    )(tok, cot, dgate, dproj, wg0, wg1, weight, par, dpre, conv, sums, hsum)

    owned = []
    for g, (keep_g, send_g) in enumerate(((k0, s0), (k1, s1), (k2, s2))):
        part = keep_g + swap(send_g, core_bit).astype(F32)
        part = part.reshape((2,) * (bits - 1) + (rows_in, GC))
        owned.append(scatter(part, orders[g][::-1]))
    g_win = jnp.concatenate([g_gate] + owned, axis=1)[:, : w_in.shape[1]]
    for bit in range(bits):
        small = small + swap(small, bit)
    taps = lax.dynamic_slice(small, (0, me * own_conv), (5, own_conv))
    g_gin = lax.dynamic_slice(small, (5, me * own_in), (1, own_in))[0]
    g_gout = lax.dynamic_slice(small, (6, me * own_out), (1, own_out))[0]
    return (
        block_out.reshape(tokens.shape),
        grad_tokens.reshape(tokens.shape),
        g_gin,
        g_win,
        taps[:KW].T,
        taps[KW],
        small[7, :H],
        small[7, LANES : LANES + H],
        small[7, 2 * LANES : 2 * LANES + H],
        g_gout,
        g_wout,
    )


def solution(mesh):
    dp, seq = mesh.shape["dp"], mesh.shape["seq"]
    inner = Mesh(mesh.devices.reshape(dp, seq // NEAR, NEAR), AX)
    split_seq = ("far", "near")
    act = P(None, "dp", split_seq, None)
    vec, mat = P(AX), P(AX, None)

    def run(*args):
        return local((dp * seq, seq), *args)

    return jax.shard_map(
        run,
        mesh=inner,
        in_specs=(act, act, vec, mat, mat, vec, P(), P(), P(), vec, mat),
        out_specs=(act, act, vec, mat, mat, vec, P(), P(), P(), vec, mat),
        check_vma=False,
    )
```

time: 793 us -> 378 us (0.48); the launches traced: 782 us -> 376 us
  blocking collectives: 227 us -> 26.4 us
  other arithmetic: 142 us -> 15.4 us
  waiting for transfers between devices: 227 us -> 106 us
  matrix products: 90.9 us -> 0 us
  Pallas kernels: 0 us -> 82.6 us
  starting transfers between devices: 7.3 us -> 63.4 us
    all_gather x6 -> x1, waiting for transfers between devices: 142 us -> 0.01 us  [local(): rest = lax.all_gather(rest, AX, axis=0, tiled=False)]
    all_gather x5 -> x0, blocking collectives: 141 us -> none  [the longest x1 66.5 us: local(): lax.all_gather(shards[2], ('dp', 'seq'), axis=0, tiled=True)]
    dot_general x36 -> x0, matrix products: 90.9 us -> none  [the longest x2 10.7 us: local(): jnp.einsum('sthp,suhp->shtu', dy_b, parts['values'], preferred_element_ty...]
    unnamed x2 -> x0, blocking collectives: 86 us -> none
    pallas_call x0 -> x11, Pallas kernels: none -> 82.6 us  [the longest x1 14.7 us: local(): pl.pallas_call(middle_kernel, grid=(R,), in_specs=[state_spec, row_c, row...]
    unnamed x9 -> x2, waiting for transfers between devices: 82.4 us -> 0.03 us
    ppermute x4 -> x44, waiting for transfers between devices: 2.54 us -> 66.3 us  [the longest x42 64 us: swap(): return lax.ppermute(x, AX, [(i, i ^ 1 << bit) for i in range(devices)])]
    ppermute x4 -> x44, starting transfers between devices: 6.8 us -> 50.3 us  [the longest x42 46.2 us: swap(): return lax.ppermute(x, AX, [(i, i ^ 1 << bit) for i in range(devices)])]
  transfers between devices with their start and end apart: 12 -> 49, of which waited for: 5 -> 25; matrix products, arithmetic and copies ran while one was open for 33% -> 7% of each run, Pallas kernels for 0% -> 15%
where the time goes in v1:
time: 378 us; the launch traced here: 376 us
  waiting for transfers between devices  106 us (28%)
  Pallas kernels  82.6 us (22%)
  local copies, waits for them, and re-layouts  67.4 us (18%)
  starting transfers between devices  63.4 us (17%)
  blocking collectives  26.4 us (7%)
  other arithmetic  15.4 us (4%)
  between operations  15.1 us (4%)
    ppermute x42, waiting for transfers between devices, swap(): return lax.ppermute(x, AX, [(i, i ^ 1 << bit) for i in range(devices)])  64 us
    unnamed x144, local copies, waits for them, and re-layouts  54.4 us
    ppermute x42, starting transfers between devices, swap(): return lax.ppermute(x, AX, [(i, i ^ 1 << bit) for i in range(devices)])  46.2 us
    reduce_scatter x1, waiting for transfers between devices, local(): lax.psum_scatter(part, ('far', 'near'), scatter_dimension=0, tiled=False)  34.9 us
    all_to_all x1, blocking collectives, exchange(): return lax.all_to_all(x, 'near', split_axis=0, concat_axis=0, tiled=True)  26.4 us
    pallas_call x1, Pallas kernels, local(): pl.pallas_call(middle_kernel, grid=(R,), in_specs=[state_spec, row_c, row...  14.7 us
    pallas_call x1, Pallas kernels, local(): pl.pallas_call(token_kernel, grid=(R,), in_specs=[row_d, row_d, row_i, pe...  13 us
    all_to_all x3, starting transfers between devices, exchange(): return lax.all_to_all(x, 'near', split_axis=0, concat_axis=0, tiled=True)  12.8 us
  transfers between devices with their start and end apart: 49, of which 25 were waited for; matrix products, arithmetic and copies ran while one was open for 7% of the time, Pallas kernels for 15%

profile of v1, /device:TPU:0, one launch (start us, length us, event | category | flops | bytes accessed | tf_op | source)
XLA Modules:
  0.0 376.2 jit_solution(14455318335957604974)
XLA Ops:
  8.0 1.6 pad_maximum_fusion.7
  10.5 3.0 collective-permute-start.9
  14.3 2.6 collective-permute-start.1
  19.1 1.9 collective-permute-done.5
  21.8 1.6 collective-permute-start.2
  24.5 2.1 collective-permute-start.11
  27.4 5.2 %collective-permute-done.6 = bf16[2,24,640]{2,1,0:T(8,128)(2,1)S(1)} collective-permute-done((bf16[2,24,640]{2,1,0:T(8,128)(2,1)S(1)}, bf16[2,24,640]{2,1,0:T(8,128)(2,1)S(1)}, u32[]{:S(2)}, u32[]{:S(2)}) %collective-permute-start.6) | collective-permute-done | bytes 61472 | tf_op jit(solution)/shard_map/ppermute | solution.py:472
  33.7 2.0 collective-permute-done.11
  35.9 1.8 collective-permute-done.7
  37.7 2.3 collective-permute-start.8
  40.2 2.6 collective-permute-done.12
  43.1 3.1 collective-permute-done.8
  46.6 3.4 collective-permute-done.4
  51.9 3.2 collective-permute-done.16
  55.3 3.8 %collective-permute-done.17 = bf16[8,1792]{1,0:T(8,128)(2,1)S(1)} collective-permute-done((bf16[8,1792]{1,0:T(8,128)(2,1)S(1)}, bf16[8,1792]{1,0:T(8,128)(2,1)S(1)}, u32[]{:S(2)}, u32[]{:S(2)}) %collective-permute-start.17) | collective-permute-done | bytes 28704 | tf_op jit(solution)/shard_map/ppermute | solution.py:472
  60.5 3.7 collective-permute-done.18
  64.2 2.4 collective-permute-start
  68.5 2.7 collective-permute-done.20
  71.3 12.2 %enter.1 = (bf16[2,256,768]{2,1,0:T(8,128)(2,1)S(1)}, bf16[2,272,1792]{2,1,0:T(8,128)(2,1)S(1)}, f32[2,256,128]{2,1,0:T(8,128)S(1)}, bf16[2,256,1792]{2,1,0:T(8,...) custom-call(s32[1]{0:T(128)} %bitcast.core_ref, ...), custom_call_target="tpu_custom_call" | custom-call | flops 4000000000 | bytes 20000000 | tf_op jit(solution)/shard_map/enter/pallas_call | solution.py:537
  86.1 26.4 %all_to_all.20.p.g = bf16[8,2,16,1664]{3,2,1,0:T(8,128)(2,1)S(1)} all-to-all(bf16[8,2,16,1664]{3,2,1,0:T(8,128)(2,1)S(1)} %get-tuple-element.84), channel_id=1, replica_groups=mesh['dp'=4,'seq'=8] {'seq'}, dimensions={0} | all-to-all | bytes 1703936 | tf_op jit(solution)/shard_map/all_to_all | solution.py:558
  113.8 4.4 %all-to-all-start.1 = ((bf16[8,2,16,1536]{3,2,1,0:T(8,128)(2,1)}), bf16[8,2,16,1536]{3,2,1,0:T(8,128)(2,1)}, u32[]{:S(2)}, u32[]{:S(2)}) async-start(bf16[8,2,16,1536]{3,2,1,0:T(8,128)(2,1)} %pass.2), calls=%async_computation.1 | async-start | bytes 1572864 | tf_op jit(solution)/shard_map/all_to_all | solution.py:558
  120.1 3.6 inside.1.intra
  123.7 1.7 copy-done.34
  125.5 2.0 slice.161
  130.7 2.8 gates.1
  133.5 1.7 copy-done.36
  137.2 1.5 copy-done.28
  138.7 1.9 copy-done.35
  143.0 14.7 %middle.1 = (bf16[2,256,1536]{2,1,0:T(8,128)(2,1)S(1)}, bf16[2,256,1536]{2,1,0:T(8,128)(2,1)S(1)}, bf16[2,256,1536]{2,1,0:T(8,128)(2,1)S(1)}, f32[2,256,128]{2,1...) custom-call(bf16[8,2,16,1536]{3,2,1,0:T(8,128)(2,1)} %all-to-all-done.1.st, ...), custom_call_target="tpu_custom_call" | custom-call | flops 4000000000 | bytes 15000000 | tf_op jit(solution)/shard_map/middle/pallas_call | solution.py:601
  162.8 4.9 %all-to-all-start.2 = ((bf16[8,2,16,1536]{3,2,1,0:T(8,128)(2,1)}), bf16[8,2,16,1536]{3,2,1,0:T(8,128)(2,1)}, u32[]{:S(2)}, u32[]{:S(2)}) async-start(bf16[8,2,16,1536]{3,2,1,0:T(8,128)(2,1)} %copy-done.14), calls=%async_computation.2 | async-start | bytes 1572864 | tf_op jit(solution)/shard_map/all_to_all | solution.py:558
  173.9 9.0 %outer.1 = (bf16[2,256,768]{2,1,0:T(8,128)(2,1)}, f32[2,768,768]{2,1,0:T(8,128)}, bf16[2,768,768]{2,1,0:T(8,128)(2,1)}) custom-call(s32[1]{0:T(128)} %bitcast.core_ref, bf16[2,256,768]{2,1,0:T(8,128)(2,1)S(1)} %bitcast.165, bf16[2,256,768]{2,1,0:T(8,128)(2,1)S(1)} %bitcast.168, bf16[2,256,768]{2,1,0:T(8,128)(2,1)S(1)} %copy-done.56, ...), custom_call_target="tpu_custom_call" | custom-call | flops 6000000000 | bytes 20000000 | tf_op jit(solution)/shard_map/outer/pallas_call | solution.py:618
  183.0 3.9 %all-to-all-done.2.p = bf16[8,2,16,1536]{3,2,1,0:T(8,128)(2,1)} async-done(((bf16[8,2,16,1536]{3,2,1,0:T(8,128)(2,1)}), bf16[8,2,16,1536]{3,2,1,0:T(8,128)(2,1)}, u32[]{:S(2)}, u32[]{:S(2)}) %all-to-all-start.2) | async-done | bytes 786464 | tf_op jit(solution)/shard_map/all_to_all | solution.py:558
  186.8 1.6 pass.3
  189.3 3.5 all-to-all-start.3
  197.9 7.9 %pair.1 = (f32[2,256,1536]{2,1,0:T(8,128)S(1)}, f32[2,256,128]{2,1,0:T(8,128)S(1)}, f32[2,256,128]{2,1,0:T(8,128)S(1)}) custom-call(bf16[2,256,1792]{2,1,0:T(8,128)(2,1)S(1)} %copy-done.29, f32[2,256,128]{2,1,0:T(8,128)S(1)} %copy-done.41, f32[2,256,128]{2,1,0:T(8,128)S(1)} %copy-done.46, bf16[2,256,1536]{2,1,0:T(8,128)(2,1)S(1)} %copy-done.32, ...), custom_call_target="tpu_custom_call" | custom-call | flops 16000000000 | bytes 10000000 | tf_op jit(solution)/shard_map/pair/pallas_call | solution.py:650
  205.9 1.6 copy-done.24
  209.0 5.8 %convert_add_fusion = f32[2,768,768]{2,1,0:T(8,128)} fusion(f32[2,768,768]{2,1,0:T(8,128)} %get-tuple-element.111, bf16[2,768,768]{2,1,0:T(8,128)(2,1)} %collective-permute-done.27), kind=kLoop, calls=%fused_computation | loop fusion | flops 2359296 | bytes 11796480 | tf_op jit(solution)/shard_map/add | solution.py:634
  214.7 1.9 copy-done.25
  216.6 1.5 copy-done.30
  225.2 11.0 %back.1 = (f32[2,256,1792]{2,1,0:T(8,128)}, f32[2,8,1792]{2,1,0:T(8,128)S(1)}, f32[2,256,128]{2,1,0:T(8,128)S(1)}, f32[2,8,128]{2,1,0:T(8,128)S(1)}) custom-call(bf16[8,2,16,1536]{3,2,1,0:T(8,128)(2,1)S(1)} %all-to-all-done.3.later, bf16[8,2,16,1536]{3,2,1,0:T(8,128)(2,1)} %all-to-all-done.1.st, bf16[2,256,1792]{2,1,0:T(8,128)(2,1)S(1)} %copy-done.30, ...), custom_call_target="tpu_custom_call" | custom-call | flops 4000000000 | bytes 15000000 | tf_op jit(solution)/shard_map/back/pallas_call | solution.py:663
  236.2 1.7 collective-permute-start.21
  237.9 2.9 fusion
  240.8 2.3 collective-permute-done.21.edge
  243.1 5.4 %input.1 = (bf16[2,256,1920]{2,1,0:T(8,128)(2,1)S(1)}, f32[2,192,640]{2,1,0:T(8,128)S(1)}, f32[2,192,640]{2,1,0:T(8,128)S(1)}, f32[2,192,640]{2,1,0:T(8,128)S(1)...) custom-call(s32[1]{0:T(128)} %bitcast.core_ref, ...), custom_call_target="tpu_custom_call" | custom-call | flops 2000000000 | bytes 10000000 | tf_op jit(solution)/shard_map/input/pallas_call | solution.py:681
  251.8 13.0 %token_.1 = (bf16[2,256,768]{2,1,0:T(8,128)(2,1)}, f32[8,1792]{1,0:T(8,128)S(1)}) custom-call(bf16[2,256,768]{2,1,0:T(8,128)(2,1)S(1)} %bitcast.166, bf16[2,256,768]{2,1,0:T(8,128)(2,1)S(1)} %bitcast.169, bf16[2,256,1536]{2,1,0:T(8,128)(2,1)S(1)} %copy-done.6, bf16[2,256,1920]{2,1,0:T(8,128)(2,1)} %copy-done.2, bf16[768,768]{1,0:T(8,128)(2,1)S(1)} %bitcast.160, ...), custom_call_target="tpu_custom_call" | custom-call | flops 4000000000 | bytes 15000000 | tf_op jit(solution)/shard_map/token/pallas_call | solution.py:695
  264.8 2.7 collective-permute-start.22
  267.6 2.2 collective-permute-done.22
  269.7 1.5 collective-permute-start.23
  271.3 3.3 collective-permute-done.23
  274.6 2.0 collective-permute-start.24
  276.6 3.7 collective-permute-done.24
  282.5 3.5 collective-permute-done.26
  286.6 2.3 bitcast_add_fusion
  289.0 1.6 pad_maximum_fusion
  297.8 7.2 %collective-permute-done.40 = bf16[2,2,2,24,640]{4,3,0,2,1:T(8,128)(2,1)S(1)} collective-permute-done((bf16[2,2,2,24,640]{4,3,0,2,1:T(8,128)(2,1)S(1)}, bf16[2,2,2,24,640]{4,3,0,2,1:T(8,128)(2,1)S(1)}, u32[]{:S(2)}, u32[]{:S(2)}) %collective-permute-start.40) | collective-permute-done | bytes 245792 | tf_op jit(solution)/shard_map/ppermute | solution.py:472
  305.1 1.5 collective-permute-start.41
  306.7 4.4 %collective-permute-start.36 = (bf16[2,2,24,640]{3,2,1,0:T(8,128)(2,1)S(1)}, bf16[2,2,24,640]{3,2,1,0:T(8,128)(2,1)S(1)}, u32[]{:S(2)}, u32[]{:S(2)}) collective-permute-start(bf16[2,2,24,640]{3,2,1,0:T(8,128)(2,1)S(1)} %fusion.5), channel_id=1, source_target_pairs={{0,2},{1,3},{2,0},{3,1},{4,6},{5,7},{6,4},{7,5},{8,10},{9,11},{10,... | collective-permute-start | bytes 368648 | tf_op jit(solution)/shard_map/ppermute | solution.py:472
  311.1 2.2 collective-permute-start.31
  313.3 5.8 %collective-permute-done.41 = bf16[2,2,24,640]{3,2,0,1:T(8,128)(2,1)S(1)} collective-permute-done((bf16[2,2,24,640]{3,2,0,1:T(8,128)(2,1)S(1)}, bf16[2,2,24,640]{3,2,0,1:T(8,128)(2,1)S(1)}, u32[]{:S(2)}, u32[]{:S(2)}) %collective-permute-start.41) | collective-permute-done | bytes 122912 | tf_op jit(solution)/shard_map/ppermute | solution.py:472
  321.6 3.0 collective-permute-start.32
  324.7 1.8 collective-permute-start.43
  326.4 2.7 collective-permute-done.37
  330.2 34.9 %reduce-scatter.2.cloned.1.call-done = f32[1,96,768]{2,1,0:T(8,128)} async-done(((f32[8,96,768]{2,1,0:T(8,128)}), f32[1,96,768]{2,1,0:T(8,128)}) %reduce-scatter.2.cloned.1.call-update) | async-done | bytes 294928 | tf_op jit(solution)/shard_map/reduce_scatter | solution.py:645
  366.0 1.6 slice_bitcast_fusion
  (283 shorter events, 73.4 us)
Async XLA Ops:
  7.2 118.3 %all-gather.3.cloned.1.call-start = ((), (), s32[]{:S(2)}) async-start(), calls=%async_computation.6 | async-start | bytes 4866048 | tf_op jit(solution)/shard_map/all_gather | solution.py:526
  10.5 7.9 %collective-permute-start.9 = (bf16[24,640]{1,0:T(8,128)(2,1)S(1)}, bf16[24,640]{1,0:T(8,128)(2,1)S(1)}, u32[]{:S(2)}, u32[]{:S(2)}) collective-permute-start(bf16[24,640]{1,0:T(8,128)(2,1)S(1)} %pad_slice_fusion), channel_id=1, source_target_pairs={{0,16},{1,17},{2,18},{3,19},{4,20},{5,21},{6,22},{7,23},{8,24},{9,... | collective-permute-start | bytes 92168 | tf_op jit(solution)/shard_map/ppermute | solution.py:472
  14.3 4.8 %collective-permute-start.1 = (bf16[24,640]{1,0:T(8,128)(2,1)S(1)}, bf16[24,640]{1,0:T(8,128)(2,1)S(1)}, u32[]{:S(2)}, u32[]{:S(2)}) collective-permute-start(bf16[24,640]{1,0:T(8,128)(2,1)S(1)} %get-tuple-element.155), channel_id=1, source_target_pairs={{0,4},{1,5},{2,6},{3,7},{4,0},{5,1},{6,2},{7,3},{8,12},{9,13},{10,... | collective-permute-start | bytes 92168 | tf_op jit(solution)/shard_map/ppermute | solution.py:472
  16.9 4.1 %collective-permute-start.5 = (bf16[24,640]{1,0:T(8,128)(2,1)S(1)}, bf16[24,640]{1,0:T(8,128)(2,1)S(1)}, u32[]{:S(2)}, u32[]{:S(2)}) collective-permute-start(bf16[24,640]{1,0:T(8,128)(2,1)S(1)} %get-tuple-element.154), channel_id=1, source_target_pairs={{0,1},{1,0},{2,3},{3,2},{4,5},{5,4},{6,7},{7,6},{8,9},{9,8},{10,11... | collective-permute-start | bytes 92168 | tf_op jit(solution)/shard_map/ppermute | solution.py:472
  18.4 6.0 %collective-permute-start.10 = (bf16[2,24,640]{2,1,0:T(8,128)(2,1)S(1)}, bf16[2,24,640]{2,1,0:T(8,128)(2,1)S(1)}, u32[]{:S(2)}, u32[]{:S(2)}) collective-permute-start(bf16[2,24,640]{2,1,0:T(8,128)(2,1)S(1)} %pad_maximum_fusion.13), channel_id=1, source_target_pairs={{0,1},{1,0},{2,3},{3,2},{4,5},{5,4},{6,7},{7,6},{8,9},{9,8},{10,11... | collective-permute-start | bytes 184328 | tf_op jit(solution)/shard_map/ppermute | solution.py:472
  21.8 5.5 %collective-permute-start.2 = (bf16[2,24,640]{2,1,0:T(8,128)(2,1)S(1)}, bf16[2,24,640]{2,1,0:T(8,128)(2,1)S(1)}, u32[]{:S(2)}, u32[]{:S(2)}) collective-permute-start(bf16[2,24,640]{2,1,0:T(8,128)(2,1)S(1)} %pad_maximum_fusion.11), channel_id=1, source_target_pairs={{0,2},{1,3},{2,0},{3,1},{4,6},{5,7},{6,4},{7,5},{8,10},{9,11},{10,... | collective-permute-start | bytes 184328 | tf_op jit(solution)/shard_map/ppermute | solution.py:472
  23.5 9.1 %collective-permute-start.6 = (bf16[2,24,640]{2,1,0:T(8,128)(2,1)S(1)}, bf16[2,24,640]{2,1,0:T(8,128)(2,1)S(1)}, u32[]{:S(2)}, u32[]{:S(2)}) collective-permute-start(bf16[2,24,640]{2,1,0:T(8,128)(2,1)S(1)} %pad_maximum_fusion.12), channel_id=1, source_target_pairs={{0,4},{1,5},{2,6},{3,7},{4,0},{5,1},{6,2},{7,3},{8,12},{9,13},{10,... | collective-permute-start | bytes 184328 | tf_op jit(solution)/shard_map/ppermute | solution.py:472
  24.5 11.2 %collective-permute-start.11 = (bf16[2,2,24,640]{3,2,0,1:T(8,128)(2,1)S(1)}, bf16[2,2,24,640]{3,2,0,1:T(8,128)(2,1)S(1)}, u32[]{:S(2)}, u32[]{:S(2)}) collective-permute-start(bf16[2,2,24,640]{3,2,0,1:T(8,128)(2,1)S(1)} %pad_maximum_fusion.10), channel_id=1, source_target_pairs={{0,4},{1,5},{2,6},{3,7},{4,0},{5,1},{6,2},{7,3},{8,12},{9,13},{10,... | collective-permute-start | bytes 368648 | tf_op jit(solution)/shard_map/ppermute | solution.py:472
  32.6 5.1 %collective-permute-start.7 = (bf16[2,2,24,640]{3,2,1,0:T(8,128)(2,1)S(1)}, bf16[2,2,24,640]{3,2,1,0:T(8,128)(2,1)S(1)}, u32[]{:S(2)}, u32[]{:S(2)}) collective-permute-start(bf16[2,2,24,640]{3,2,1,0:T(8,128)(2,1)S(1)} %pad_maximum_fusion.9), channel_id=1, source_target_pairs={{0,2},{1,3},{2,0},{3,1},{4,6},{5,7},{6,4},{7,5},{8,10},{9,11},{10,... | collective-permute-start | bytes 368648 | tf_op jit(solution)/shard_map/ppermute | solution.py:472
  32.7 7.3 %collective-permute-start.3 = (bf16[2,2,24,640]{3,2,0,1:T(8,128)(2,1)S(1)}, bf16[2,2,24,640]{3,2,0,1:T(8,128)(2,1)S(1)}, u32[]{:S(2)}, u32[]{:S(2)}) collective-permute-start(bf16[2,2,24,640]{3,2,0,1:T(8,128)(2,1)S(1)} %pad_maximum_fusion.8), channel_id=1, source_target_pairs={{0,16},{1,17},{2,18},{3,19},{4,20},{5,21},{6,22},{7,23},{8,24},{9,... | collective-permute-start | bytes 368648 | tf_op jit(solution)/shard_map/ppermute | solution.py:472
  35.8 7.1 %collective-permute-start.12 = (bf16[2,2,2,24,640]{4,3,0,2,1:T(8,128)(2,1)S(1)}, bf16[2,2,2,24,640]{4,3,0,2,1:T(8,128)(2,1)S(1)}, u32[]{:S(2)}, u32[]{:S(2)}) collective-permute-start(bf16[2,2,2,24,640]{4,3,0,2,1:T(8,128)(2,1)S(1)} %pad_maximum_fusion.6), channel_id=1, source_target_pairs={{0,2},{1,3},{2,0},{3,1},{4,6},{5,7},{6,4},{7,5},{8,10},{9,11},{10,... | collective-permute-start | bytes 737288 | tf_op jit(solution)/shard_map/ppermute | solution.py:472
  37.7 8.5 %collective-permute-start.8 = (bf16[2,2,2,24,640]{4,3,2,0,1:T(8,128)(2,1)S(1)}, bf16[2,2,2,24,640]{4,3,2,0,1:T(8,128)(2,1)S(1)}, u32[]{:S(2)}, u32[]{:S(2)}) collective-permute-start(bf16[2,2,2,24,640]{4,3,2,0,1:T(8,128)(2,1)S(1)} %pad_maximum_fusion.5), channel_id=1, source_target_pairs={{0,16},{1,17},{2,18},{3,19},{4,20},{5,21},{6,22},{7,23},{8,24},{9,... | collective-permute-start | bytes 737288 | tf_op jit(solution)/shard_map/ppermute | solution.py:472
  40.1 9.9 %collective-permute-start.4 = (bf16[2,2,2,24,640]{4,3,1,2,0:T(8,128)(2,1)S(1)}, bf16[2,2,2,24,640]{4,3,1,2,0:T(8,128)(2,1)S(1)}, u32[]{:S(2)}, u32[]{:S(2)}) collective-permute-start(bf16[2,2,2,24,640]{4,3,1,2,0:T(8,128)(2,1)S(1)} %pad_maximum_fusion.4), channel_id=1, source_target_pairs={{0,1},{1,0},{2,3},{3,2},{4,5},{5,4},{6,7},{7,6},{8,9},{9,8},{10,11... | collective-permute-start | bytes 737288 | tf_op jit(solution)/shard_map/ppermute | solution.py:472
  43.0 28.2 %collective-permute-start.15 = (bf16[2,192,640]{2,1,0:T(8,128)(2,1)S(1)}, bf16[2,192,640]{2,1,0:T(8,128)(2,1)S(1)}, u32[]{:S(2)}, u32[]{:S(2)}) collective-permute-start(bf16[2,192,640]{2,1,0:T(8,128)(2,1)S(1)} %bitcast.170), channel_id=1, source_target_pairs={{0,8},{1,9},{2,10},{3,11},{4,12},{5,13},{6,14},{7,15},{8,0},{9,1},... | collective-permute-start | bytes 1474568 | tf_op jit(solution)/shard_map/ppermute | solution.py:472
  46.4 17.8 %copy-start.11 = (bf16[2,1,256,768]{3,2,1,0:T(8,128)(2,1)S(1)}, bf16[2,1,256,768]{3,2,1,0:T(8,128)(2,1)}, u32[]{:S(2)}) copy-start(bf16[2,1,256,768]{3,2,1,0:T(8,128)(2,1)} %param.17) | copy-start | bytes 2359300
  46.4 21.7 %copy-start.66 = (f32[24]{0:T(128)S(1)}, f32[24]{0:T(128)}, u32[]{:S(2)}) copy-start(f32[24]{0:T(128)} %param.23) | copy-start | bytes 292
  46.5 21.6 %copy-start.69 = (f32[24]{0:T(128)S(1)}, f32[24]{0:T(128)}, u32[]{:S(2)}) copy-start(f32[24]{0:T(128)} %param.24) | copy-start | bytes 292
  46.5 21.8 %copy-start.70 = (f32[24]{0:T(128)S(1)}, f32[24]{0:T(128)}, u32[]{:S(2)}) copy-start(f32[24]{0:T(128)} %param.25) | copy-start | bytes 292
  46.5 24.7 %collective-permute-start.14 = (bf16[2,192,640]{2,1,0:T(8,128)(2,1)S(1)}, bf16[2,192,640]{2,1,0:T(8,128)(2,1)S(1)}, u32[]{:S(2)}, u32[]{:S(2)}) collective-permute-start(bf16[2,192,640]{2,1,0:T(8,128)(2,1)S(1)} %pad_maximum_fusion.2.m1), channel_id=1, source_target_pairs={{0,8},{1,9},{2,10},{3,11},{4,12},{5,13},{6,14},{7,15},{8,0},{9,1},... | collective-permute-start | bytes 1474568 | tf_op jit(solution)/shard_map/ppermute | solution.py:472
  50.2 21.0 %collective-permute-start.13 = (bf16[2,192,640]{2,1,0:T(8,128)(2,1)S(1)}, bf16[2,192,640]{2,1,0:T(8,128)(2,1)}, u32[]{:S(2)}, u32[]{:S(2)}) collective-permute-start(bf16[2,192,640]{2,1,0:T(8,128)(2,1)S(1)} %bitcast.172), channel_id=1, source_target_pairs={{0,8},{1,9},{2,10},{3,11},{4,12},{5,13},{6,14},{7,15},{8,0},{9,1},... | collective-permute-start | bytes 1474568 | tf_op jit(solution)/shard_map/ppermute | solution.py:472
  51.1 4.1 %collective-permute-start.16 = (bf16[8,1792]{1,0:T(8,128)(2,1)S(1)}, bf16[8,1792]{1,0:T(8,128)(2,1)S(1)}, u32[]{:S(2)}, u32[]{:S(2)}) collective-permute-start(bf16[8,1792]{1,0:T(8,128)(2,1)S(1)} %dynamic_update_slice.11), channel_id=1, source_target_pairs={{0,1},{1,0},{2,3},{3,2},{4,5},{5,4},{6,7},{7,6},{8,9},{9,8},{10,11... | collective-permute-start | bytes 86024 | tf_op jit(solution)/shard_map/ppermute | solution.py:472
  55.2 3.9 %collective-permute-start.17 = (bf16[8,1792]{1,0:T(8,128)(2,1)S(1)}, bf16[8,1792]{1,0:T(8,128)(2,1)S(1)}, u32[]{:S(2)}, u32[]{:S(2)}) collective-permute-start(bf16[8,1792]{1,0:T(8,128)(2,1)S(1)} %add.168), channel_id=1, source_target_pairs={{0,2},{1,3},{2,0},{3,1},{4,6},{5,7},{6,4},{7,5},{8,10},{9,11},{10,... | collective-permute-start | bytes 86024 | tf_op jit(solution)/shard_map/ppermute | solution.py:472
  59.1 5.0 %collective-permute-start.18 = (bf16[8,1792]{1,0:T(8,128)(2,1)S(1)}, bf16[8,1792]{1,0:T(8,128)(2,1)S(1)}, u32[]{:S(2)}, u32[]{:S(2)}) collective-permute-start(bf16[8,1792]{1,0:T(8,128)(2,1)S(1)} %add.169), channel_id=1, source_target_pairs={{0,4},{1,5},{2,6},{3,7},{4,0},{5,1},{6,2},{7,3},{8,12},{9,13},{10,... | collective-permute-start | bytes 86024 | tf_op jit(solution)/shard_map/ppermute | solution.py:472
  64.1 2.5 collective-permute-start.19
  64.2 7.0 %collective-permute-start = (bf16[2,16,768]{2,1,0:T(8,128)(2,1)S(1)}, bf16[2,16,768]{2,1,0:T(8,128)(2,1)S(1)}, u32[]{:S(2)}, u32[]{:S(2)}) collective-permute-start(bf16[2,16,768]{2,1,0:T(8,128)(2,1)S(1)} %slice.158), channel_id=1, source_target_pairs={{0,1},{1,2},{2,3},{3,4},{4,5},{5,6},{6,7},{8,9},{9,10},{10,11},{11... | collective-permute-start | bytes 147464 | tf_op jit(solution)/shard_map/ppermute | solution.py:514
  66.7 4.6 %collective-permute-start.20 = (bf16[8,1792]{1,0:T(8,128)(2,1)S(1)}, bf16[8,1792]{1,0:T(8,128)(2,1)S(1)}, u32[]{:S(2)}, u32[]{:S(2)}) collective-permute-start(bf16[8,1792]{1,0:T(8,128)(2,1)S(1)} %add.171), channel_id=1, source_target_pairs={{0,16},{1,17},{2,18},{3,19},{4,20},{5,21},{6,22},{7,23},{8,24},{9,... | collective-permute-start | bytes 86024 | tf_op jit(solution)/shard_map/ppermute | solution.py:472
  71.2 12.2 %copy-start.18 = (bf16[8,1792]{1,0:T(8,128)(2,1)}, bf16[8,1792]{1,0:T(8,128)(2,1)S(1)}, u32[]{:S(2)}) copy-start(bf16[8,1792]{1,0:T(8,128)(2,1)S(1)} %add.172.par) | copy-start | bytes 86020
  86.1 26.4 %copy-start.37 = (f32[2,256,128]{2,1,0:T(8,128)}, f32[2,256,128]{2,1,0:T(8,128)S(1)}, u32[]{:S(2)}) copy-start(f32[2,256,128]{2,1,0:T(8,128)S(1)} %get-tuple-element.94.raw) | copy-start | bytes 786436
  86.1 26.4 %copy-start.39 = (f32[2,256,128]{2,1,0:T(8,128)}, f32[2,256,128]{2,1,0:T(8,128)S(1)}, u32[]{:S(2)}) copy-start(f32[2,256,128]{2,1,0:T(8,128)S(1)} %get-tuple-element.86.step) | copy-start | bytes 786436
  86.1 26.4 %copy-start.43 = (f32[2,256,128]{2,1,0:T(8,128)}, f32[2,256,128]{2,1,0:T(8,128)S(1)}, u32[]{:S(2)}) copy-start(f32[2,256,128]{2,1,0:T(8,128)S(1)} %get-tuple-element.87.cum) | copy-start | bytes 786436
  86.1 26.4 %copy-start.54 = (bf16[2,256,768]{2,1,0:T(8,128)(2,1)}, bf16[2,256,768]{2,1,0:T(8,128)(2,1)S(1)}, u32[]{:S(2)}) copy-start(bf16[2,256,768]{2,1,0:T(8,128)(2,1)S(1)} %get-tuple-element.83.hid) | copy-start | bytes 2359300
  113.8 23.4 %all-to-all-start.1 = ((bf16[8,2,16,1536]{3,2,1,0:T(8,128)(2,1)}), bf16[8,2,16,1536]{3,2,1,0:T(8,128)(2,1)}, u32[]{:S(2)}, u32[]{:S(2)}) async-start(bf16[8,2,16,1536]{3,2,1,0:T(8,128)(2,1)} %pass.2), calls=%async_computation.1 | async-start | bytes 1572864 | tf_op jit(solution)/shard_map/all_to_all | solution.py:558
  162.8 24.0 %all-to-all-start.2 = ((bf16[8,2,16,1536]{3,2,1,0:T(8,128)(2,1)}), bf16[8,2,16,1536]{3,2,1,0:T(8,128)(2,1)}, u32[]{:S(2)}, u32[]{:S(2)}) async-start(bf16[8,2,16,1536]{3,2,1,0:T(8,128)(2,1)} %copy-done.14), calls=%async_computation.2 | async-start | bytes 1572864 | tf_op jit(solution)/shard_map/all_to_all | solution.py:558
  183.0 26.0 %collective-permute-start.27 = (bf16[2,768,768]{2,1,0:T(8,128)(2,1)}, bf16[2,768,768]{2,1,0:T(8,128)(2,1)}, u32[]{:S(2)}, u32[]{:S(2)}) collective-permute-start(bf16[2,768,768]{2,1,0:T(8,128)(2,1)} %get-tuple-element.112), channel_id=1, source_target_pairs={{0,8},{1,9},{2,10},{3,11},{4,12},{5,13},{6,14},{7,15},{8,0},{9,1},... | collective-permute-start | bytes 7077896 | tf_op jit(solution)/shard_map/ppermute | solution.py:472
  189.3 25.4 %all-to-all-start.3 = ((bf16[8,2,16,1536]{3,2,1,0:T(8,128)(2,1)}), bf16[8,2,16,1536]{3,2,1,0:T(8,128)(2,1)S(1)}, u32[]{:S(2)}, u32[]{:S(2)}) async-start(bf16[8,2,16,1536]{3,2,1,0:T(8,128)(2,1)} %copy-done), calls=%async_computation.3 | async-start | bytes 1572864 | tf_op jit(solution)/shard_map/all_to_all | solution.py:558
  192.9 172.3 %reduce-scatter.2.cloned.1.call-start = ((), (), s32[]{:S(2)}) async-start(), calls=%async_computation.5 | async-start | bytes 2654208 | tf_op jit(solution)/shard_map/reduce_scatter | solution.py:645
  236.2 6.8 %collective-permute-start.21 = (f32[2,8,1792]{2,1,0:T(8,128)S(1)}, f32[2,8,1792]{2,1,0:T(8,128)S(1)}, u32[]{:S(2)}, u32[]{:S(2)}) collective-permute-start(f32[2,8,1792]{2,1,0:T(8,128)S(1)} %get-tuple-element.102), channel_id=1, source_target_pairs={{1,0},{2,1},{3,2},{4,3},{5,4},{6,5},{7,6},{9,8},{10,9},{11,10},{12... | collective-permute-start | bytes 344072 | tf_op jit(solution)/shard_map/ppermute | solution.py:679
  240.8 45.8 %collective-permute-start.28 = (bf16[768,768]{1,0:T(8,128)(2,1)}, bf16[768,768]{1,0:T(8,128)(2,1)}, u32[]{:S(2)}, u32[]{:S(2)}) collective-permute-start(bf16[768,768]{1,0:T(8,128)(2,1)} %fusion), channel_id=1, source_target_pairs={{0,16},{1,17},{2,18},{3,19},{4,20},{5,21},{6,22},{7,23},{8,24},{9,... | collective-permute-start | bytes 3538952 | tf_op jit(solution)/shard_map/ppermute | solution.py:472
  243.0 8.7 %copy-start.6 = (bf16[2,256,1536]{2,1,0:T(8,128)(2,1)S(1)}, bf16[2,256,1536]{2,1,0:T(8,128)(2,1)}, u32[]{:S(2)}) copy-start(bf16[2,256,1536]{2,1,0:T(8,128)(2,1)} %copy-done.4) | copy-start | bytes 4718596
  243.0 8.7 %copy-start.13 = (bf16[2,1,256,768]{3,2,1,0:T(8,128)(2,1)S(1)}, bf16[2,1,256,768]{3,2,1,0:T(8,128)(2,1)}, u32[]{:S(2)}) copy-start(bf16[2,1,256,768]{3,2,1,0:T(8,128)(2,1)} %param.17) | copy-start | bytes 2359300
  243.1 8.7 %copy-start.17 = (bf16[2,1,256,768]{3,2,1,0:T(8,128)(2,1)S(1)}, bf16[2,1,256,768]{3,2,1,0:T(8,128)(2,1)}, u32[]{:S(2)}) copy-start(bf16[2,1,256,768]{3,2,1,0:T(8,128)(2,1)} %param.18) | copy-start | bytes 2359300
  251.8 13.1 %copy-start.21 = (bf16[2,192,640]{2,1,0:T(8,128)(2,1)}, bf16[2,192,640]{2,1,0:T(8,128)(2,1)S(1)}, u32[]{:S(2)}) copy-start(bf16[2,192,640]{2,1,0:T(8,128)(2,1)S(1)} %get-tuple-element.114) | copy-start | bytes 1474564
  251.8 13.1 %copy-start.22 = (bf16[2,192,640]{2,1,0:T(8,128)(2,1)}, bf16[2,192,640]{2,1,0:T(8,128)(2,1)S(1)}, u32[]{:S(2)}) copy-start(bf16[2,192,640]{2,1,0:T(8,128)(2,1)S(1)} %get-tuple-element.116) | copy-start | bytes 1474564
  251.8 13.1 %copy-start.23 = (bf16[2,192,640]{2,1,0:T(8,128)(2,1)}, bf16[2,192,640]{2,1,0:T(8,128)(2,1)S(1)}, u32[]{:S(2)}) copy-start(bf16[2,192,640]{2,1,0:T(8,128)(2,1)S(1)} %get-tuple-element.118) | copy-start | bytes 1474564
  264.8 4.9 %collective-permute-start.22 = (f32[8,1792]{1,0:T(8,128)S(1)}, f32[8,1792]{1,0:T(8,128)S(1)}, u32[]{:S(2)}, u32[]{:S(2)}) collective-permute-start(f32[8,1792]{1,0:T(8,128)S(1)} %get-tuple-element.110), channel_id=1, source_target_pairs={{0,1},{1,0},{2,3},{3,2},{4,5},{5,4},{6,7},{7,6},{8,9},{9,8},{10,11... | collective-permute-start | bytes 172040 | tf_op jit(solution)/shard_map/ppermute | solution.py:472
  269.7 4.9 %collective-permute-start.23 = (f32[8,1792]{1,0:T(8,128)S(1)}, f32[8,1792]{1,0:T(8,128)S(1)}, u32[]{:S(2)}, u32[]{:S(2)}) collective-permute-start(f32[8,1792]{1,0:T(8,128)S(1)} %add.173), channel_id=1, source_target_pairs={{0,2},{1,3},{2,0},{3,1},{4,6},{5,7},{6,4},{7,5},{8,10},{9,11},{10,... | collective-permute-start | bytes 172040 | tf_op jit(solution)/shard_map/ppermute | solution.py:472
  274.6 5.8 %collective-permute-start.24 = (f32[8,1792]{1,0:T(8,128)S(1)}, f32[8,1792]{1,0:T(8,128)S(1)}, u32[]{:S(2)}, u32[]{:S(2)}) collective-permute-start(f32[8,1792]{1,0:T(8,128)S(1)} %add.174), channel_id=1, source_target_pairs={{0,4},{1,5},{2,6},{3,7},{4,0},{5,1},{6,2},{7,3},{8,12},{9,13},{10,... | collective-permute-start | bytes 172040 | tf_op jit(solution)/shard_map/ppermute | solution.py:472
  280.4 1.3 collective-permute-start.25
  281.7 4.2 %collective-permute-start.26 = (f32[8,1792]{1,0:T(8,128)S(1)}, f32[8,1792]{1,0:T(8,128)S(1)}, u32[]{:S(2)}, u32[]{:S(2)}) collective-permute-start(f32[8,1792]{1,0:T(8,128)S(1)} %add.176), channel_id=1, source_target_pairs={{0,16},{1,17},{2,18},{3,19},{4,20},{5,21},{6,22},{7,23},{8,24},{9,... | collective-permute-start | bytes 172040 | tf_op jit(solution)/shard_map/ppermute | solution.py:472
  281.9 10.4 %collective-permute-start.39 = (bf16[2,192,640]{2,1,0:T(8,128)(2,1)}, bf16[2,192,640]{2,1,0:T(8,128)(2,1)}, u32[]{:S(2)}, u32[]{:S(2)}) collective-permute-start(bf16[2,192,640]{2,1,0:T(8,128)(2,1)} %copy-done.23), channel_id=1, source_target_pairs={{0,8},{1,9},{2,10},{3,11},{4,12},{5,13},{6,14},{7,15},{8,0},{9,1},... | collective-permute-start | bytes 1474568 | tf_op jit(solution)/shard_map/ppermute | solution.py:472
  281.9 12.1 %collective-permute-start.34 = (bf16[2,192,640]{2,1,0:T(8,128)(2,1)}, bf16[2,192,640]{2,1,0:T(8,128)(2,1)}, u32[]{:S(2)}, u32[]{:S(2)}) collective-permute-start(bf16[2,192,640]{2,1,0:T(8,128)(2,1)} %copy-done.22), channel_id=1, source_target_pairs={{0,8},{1,9},{2,10},{3,11},{4,12},{5,13},{6,14},{7,15},{8,0},{9,1},... | collective-permute-start | bytes 1474568 | tf_op jit(solution)/shard_map/ppermute | solution.py:472
  282.4 14.1 %collective-permute-start.29 = (bf16[2,192,640]{2,1,0:T(8,128)(2,1)}, bf16[2,192,640]{2,1,0:T(8,128)(2,1)S(1)}, u32[]{:S(2)}, u32[]{:S(2)}) collective-permute-start(bf16[2,192,640]{2,1,0:T(8,128)(2,1)} %copy-done.21), channel_id=1, source_target_pairs={{0,8},{1,9},{2,10},{3,11},{4,12},{5,13},{6,14},{7,15},{8,0},{9,1},... | collective-permute-start | bytes 1474568 | tf_op jit(solution)/shard_map/ppermute | solution.py:472
  293.5 11.5 %collective-permute-start.40 = (bf16[2,2,2,24,640]{4,3,0,2,1:T(8,128)(2,1)S(1)}, bf16[2,2,2,24,640]{4,3,0,2,1:T(8,128)(2,1)S(1)}, u32[]{:S(2)}, u32[]{:S(2)}) collective-permute-start(bf16[2,2,2,24,640]{4,3,0,2,1:T(8,128)(2,1)S(1)} %fusion.3), channel_id=1, source_target_pairs={{0,2},{1,3},{2,0},{3,1},{4,6},{5,7},{6,4},{7,5},{8,10},{9,11},{10,... | collective-permute-start | bytes 737288 | tf_op jit(solution)/shard_map/ppermute | solution.py:472
  295.2 11.4 %collective-permute-start.35 = (bf16[2,2,2,24,640]{4,3,2,0,1:T(8,128)(2,1)S(1)}, bf16[2,2,2,24,640]{4,3,2,0,1:T(8,128)(2,1)S(1)}, u32[]{:S(2)}, u32[]{:S(2)}) collective-permute-start(bf16[2,2,2,24,640]{4,3,2,0,1:T(8,128)(2,1)S(1)} %fusion.2), channel_id=1, source_target_pairs={{0,16},{1,17},{2,18},{3,19},{4,20},{5,21},{6,22},{7,23},{8,24},{9,... | collective-permute-start | bytes 737288 | tf_op jit(solution)/shard_map/ppermute | solution.py:472
  296.7 14.4 %collective-permute-start.30 = (bf16[2,2,2,24,640]{4,3,1,2,0:T(8,128)(2,1)S(1)}, bf16[2,2,2,24,640]{4,3,1,2,0:T(8,128)(2,1)S(1)}, u32[]{:S(2)}, u32[]{:S(2)}) collective-permute-start(bf16[2,2,2,24,640]{4,3,1,2,0:T(8,128)(2,1)S(1)} %fusion.1), channel_id=1, source_target_pairs={{0,1},{1,0},{2,3},{3,2},{4,5},{5,4},{6,7},{7,6},{8,9},{9,8},{10,11... | collective-permute-start | bytes 737288 | tf_op jit(solution)/shard_map/ppermute | solution.py:472
  305.1 14.0 %collective-permute-start.41 = (bf16[2,2,24,640]{3,2,0,1:T(8,128)(2,1)S(1)}, bf16[2,2,24,640]{3,2,0,1:T(8,128)(2,1)S(1)}, u32[]{:S(2)}, u32[]{:S(2)}) collective-permute-start(bf16[2,2,24,640]{3,2,0,1:T(8,128)(2,1)S(1)} %fusion.6), channel_id=1, source_target_pairs={{0,4},{1,5},{2,6},{3,7},{4,0},{5,1},{6,2},{7,3},{8,12},{9,13},{10,... | collective-permute-start | bytes 368648 | tf_op jit(solution)/shard_map/ppermute | solution.py:472
  306.7 13.5 %collective-permute-start.36 = (bf16[2,2,24,640]{3,2,1,0:T(8,128)(2,1)S(1)}, bf16[2,2,24,640]{3,2,1,0:T(8,128)(2,1)S(1)}, u32[]{:S(2)}, u32[]{:S(2)}) collective-permute-start(bf16[2,2,24,640]{3,2,1,0:T(8,128)(2,1)S(1)} %fusion.5), channel_id=1, source_target_pairs={{0,2},{1,3},{2,0},{3,1},{4,6},{5,7},{6,4},{7,5},{8,10},{9,11},{10,... | collective-permute-start | bytes 368648 | tf_op jit(solution)/shard_map/ppermute | solution.py:472
  311.1 10.4 %collective-permute-start.31 = (bf16[2,2,24,640]{3,2,0,1:T(8,128)(2,1)S(1)}, bf16[2,2,24,640]{3,2,0,1:T(8,128)(2,1)S(1)}, u32[]{:S(2)}, u32[]{:S(2)}) collective-permute-start(bf16[2,2,24,640]{3,2,0,1:T(8,128)(2,1)S(1)} %fusion.4), channel_id=1, source_target_pairs={{0,16},{1,17},{2,18},{3,19},{4,20},{5,21},{6,22},{7,23},{8,24},{9,... | collective-permute-start | bytes 368648 | tf_op jit(solution)/shard_map/ppermute | solution.py:472
  319.1 5.5 %collective-permute-start.42 = (bf16[2,24,640]{2,1,0:T(8,128)(2,1)S(1)}, bf16[2,24,640]{2,1,0:T(8,128)(2,1)S(1)}, u32[]{:S(2)}, u32[]{:S(2)}) collective-permute-start(bf16[2,24,640]{2,1,0:T(8,128)(2,1)S(1)} %fusion.11), channel_id=1, source_target_pairs={{0,1},{1,0},{2,3},{3,2},{4,5},{5,4},{6,7},{7,6},{8,9},{9,8},{10,11... | collective-permute-start | bytes 184328 | tf_op jit(solution)/shard_map/ppermute | solution.py:472
  320.3 8.8 %collective-permute-start.37 = (bf16[2,24,640]{2,1,0:T(8,128)(2,1)S(1)}, bf16[2,24,640]{2,1,0:T(8,128)(2,1)S(1)}, u32[]{:S(2)}, u32[]{:S(2)}) collective-permute-start(bf16[2,24,640]{2,1,0:T(8,128)(2,1)S(1)} %fusion.10), channel_id=1, source_target_pairs={{0,4},{1,5},{2,6},{3,7},{4,0},{5,1},{6,2},{7,3},{8,12},{9,13},{10,... | collective-permute-start | bytes 184328 | tf_op jit(solution)/shard_map/ppermute | solution.py:472
  321.6 8.2 %collective-permute-start.32 = (bf16[2,24,640]{2,1,0:T(8,128)(2,1)S(1)}, bf16[2,24,640]{2,1,0:T(8,128)(2,1)S(1)}, u32[]{:S(2)}, u32[]{:S(2)}) collective-permute-start(bf16[2,24,640]{2,1,0:T(8,128)(2,1)S(1)} %fusion.9), channel_id=1, source_target_pairs={{0,2},{1,3},{2,0},{3,1},{4,6},{5,7},{6,4},{7,5},{8,10},{9,11},{10,... | collective-permute-start | bytes 184328 | tf_op jit(solution)/shard_map/ppermute | solution.py:472
  324.7 43.9 %collective-permute-start.43 = (bf16[24,640]{1,0:T(8,128)(2,1)S(1)}, bf16[24,640]{1,0:T(8,128)(2,1)S(1)}, u32[]{:S(2)}, u32[]{:S(2)}) collective-permute-start(bf16[24,640]{1,0:T(8,128)(2,1)S(1)} %fusion.17), channel_id=1, source_target_pairs={{0,16},{1,17},{2,18},{3,19},{4,20},{5,21},{6,22},{7,23},{8,24},{9,... | collective-permute-start | bytes 92168 | tf_op jit(solution)/shard_map/ppermute | solution.py:472
  329.1 39.4 %collective-permute-start.38 = (bf16[24,640]{1,0:T(8,128)(2,1)S(1)}, bf16[24,640]{1,0:T(8,128)(2,1)S(1)}, u32[]{:S(2)}, u32[]{:S(2)}) collective-permute-start(bf16[24,640]{1,0:T(8,128)(2,1)S(1)} %fusion.16), channel_id=1, source_target_pairs={{0,1},{1,0},{2,3},{3,2},{4,5},{5,4},{6,7},{7,6},{8,9},{9,8},{10,11... | collective-permute-start | bytes 92168 | tf_op jit(solution)/shard_map/ppermute | solution.py:472
  329.8 38.7 %collective-permute-start.33 = (bf16[24,640]{1,0:T(8,128)(2,1)S(1)}, bf16[24,640]{1,0:T(8,128)(2,1)S(1)}, u32[]{:S(2)}, u32[]{:S(2)}) collective-permute-start(bf16[24,640]{1,0:T(8,128)(2,1)S(1)} %fusion.15), channel_id=1, source_target_pairs={{0,4},{1,5},{2,6},{3,7},{4,0},{5,1},{6,2},{7,3},{8,12},{9,13},{10,... | collective-permute-start | bytes 92168 | tf_op jit(solution)/shard_map/ppermute | solution.py:472
  (56 other events, 105.6 us)
Sparse Core Ops, SparseCore 0:
  11.6 69.9 all-gather.2
  290.8 74.3 reduce-scatter.1

commit v2 on v1

--- a/solution.py
+++ b/solution.py
@@ -1,3 +1,4 @@
+import functools
 import math
 
 import jax
@@ -114,15 +115,39 @@
             weight_s[pl.ds(other, rows), cols] = recv[g][y]
 
 
+def lay_out(weight, par, owned):
+    held = weight[:, CONV:]
+    for own, kinds in owned:
+        rows_in = own * D // CONV if len(kinds) > 1 else (own if kinds[0] == KW + 1 else own // 2)
+        devices = D // rows_in
+        width = own * devices
+        lane = lax.broadcasted_iota(jnp.int32, (LANES, width), 1)
+        row = lax.broadcasted_iota(jnp.int32, (LANES, width), 0)
+        source = lax.broadcasted_iota(jnp.int32, (devices, D), 1)
+        device = lax.broadcasted_iota(jnp.int32, (devices, D), 0)
+        place = lax.broadcasted_iota(jnp.int32, (devices, width), 1)
+        holder = lax.broadcasted_iota(jnp.int32, (devices, width), 0)
+        mine = (place >= holder * own) & (place < holder * own + own)
+        for kind in kinds:
+            at, block = kind % rows_in, kind // rows_in
+            pick = jnp.where(source == device * rows_in + at, 1.0, 0.0).astype(BF16)
+            start = H + block * (rows_in * CONV // D)
+            spread = jnp.where(row == start + lane % own, 1.0, 0.0).astype(BF16)
+            values = dot(dot(pick, held).astype(BF16), spread)
+            par[kind : kind + 1, :width] = jnp.sum(jnp.where(mine, values, 0.0), axis=0, keepdims=True)
+
+
 def enter_kernel(
-    core_ref, tok, halo, m0, m1, m2, r0, r1, r2, par, heads,
-    hid, conv, raw, act, dsilu, step, cum, pay, weight, ext
+    owned, core_ref, tok, halo, m0, m1, m2, r0, r1, r2, heads,
+    hid, conv, raw, act, dsilu, step, cum, pay, weight, par, ext
 ):
     @pl.when(pl.program_id(0) == 0)
     def _():
         assemble(core_ref[0], (m0, m1, m2), (r0, r1, r2), weight)
-
-    gain = par[5:6, :D].astype(F32)
+        par[...] = jnp.zeros_like(par)
+        lay_out(weight, par, owned)
+
+    gain = par[5:6, :D]
     rows = jnp.concatenate([halo[0], tok[0]], axis=0).astype(F32)
     scale = lax.rsqrt(jnp.mean(rows * rows, axis=-1, keepdims=True) + EPS)
     hidden = (rows * scale * gain).astype(BF16)
@@ -134,13 +159,14 @@
         ext[:, cols] = part.astype(F32)
     for t in range(CONV // LANES):
         cols = slice(t * LANES, (t + 1) * LANES)
-        total = par[4:5, cols].astype(F32)
+        total = par[4:5, cols]
         for k in range(KW):
-            total = total + par[k : k + 1, cols].astype(F32) * ext[pl.ds(HALO - KW + 1 + k, PIECE), cols]
+            total = total + par[k : k + 1, cols] * ext[pl.ds(HALO - KW + 1 + k, PIECE), cols]
         gate = jax.nn.sigmoid(total)
         act[0, :, cols] = (total * gate).astype(BF16)
         dsilu[0, :, cols] = gate * (1.0 + total * (1.0 - gate))
     raw_step = dot(hidden[HALO:], weight[:, CONV:]).astype(BF16).astype(F32)
+    raw_step = jnp.where(lax.broadcasted_iota(jnp.int32, (PIECE, LANES), 1) < H, raw_step, 0.0)
     raw[0] = raw_step
     size = softplus(raw_step + heads[0:1])
     cumul = running(triangle(PIECE, True), size * -jnp.exp(heads[1:2]))
@@ -215,7 +241,7 @@
     off_s[...] = dot(cmat, state)
     grow_s[...] = expand(jnp.exp(cum[0]), spread)
     skip = expand(jnp.broadcast_to(heads[2:3], (8, LANES)), spread)[0:1]
-    gain = par[6:7, :DI].astype(F32)
+    gain = par[6:7, :DI]
     sum_s[...] = jnp.zeros_like(sum_s)
     size = 16
 
@@ -258,29 +284,38 @@
     sums[0, 8:16, LANES:] = jnp.zeros((8, DI - LANES), F32)
 
 
-def outer_kernel(core_ref, tok, cot, hid, normed, dgate, wo, out, keep, send, total):
-    core = core_ref[0]
+def outer_kernel(fused, tok, cot, hid, normed, dgate, wo, out, *refs):
     count = tok.shape[0]
+    tangent = cot[...].reshape(count * PIECE, D)
+    hidden = hid[...].reshape(count * PIECE, D)
+    parts = (
+        lambda: dot_tn(normed[...].reshape(count * PIECE, DI), tangent),
+        lambda: dot_tn(hidden, dgate[:, :, :D].reshape(count * PIECE, D)),
+        lambda: dot_tn(hidden, dgate[:, :, D:].reshape(count * PIECE, D)),
+    )
+    if fused:
+        rest, total = refs
+        devices = rest.shape[0]
+        at = 0
+        for part in parts:
+            made = part()
+            total[at : at + made.shape[0]] = made
+            at += made.shape[0]
+        long, short = DI // devices, D // devices
+        for d in range(devices):
+            rest[d] = jnp.concatenate(
+                [
+                    total[d * long : (d + 1) * long],
+                    total[DI + d * short : DI + (d + 1) * short],
+                    total[DI + D + d * short : DI + D + (d + 1) * short],
+                ],
+                axis=0,
+            ).astype(BF16)
+    else:
+        for ref, part in zip(refs, parts):
+            ref[...] = part().astype(BF16)
     for r in range(count):
         out[r] = (tok[r].astype(F32) + dot(normed[r], wo[...])).astype(BF16)
-    tangent = cot[...].reshape(count * PIECE, D)
-    hidden = hid[...].reshape(count * PIECE, D)
-    blocks = keep.shape[0]
-    left = [
-        dot_tn(normed[...].reshape(count * PIECE, DI), tangent),
-        dot_tn(hidden, dgate[:, :, :D].reshape(count * PIECE, D)),
-        dot_tn(hidden, dgate[:, :, D:].reshape(count * PIECE, D)),
-    ]
-    base = 0
-    for part in left:
-        total[: part.shape[0]] = part
-        rows = part.shape[0] // (2 * blocks)
-        for y in range(blocks):
-            mine = pl.multiple_of((2 * y + core) * rows, 16)
-            other = pl.multiple_of((2 * y + 1 - core) * rows, 16)
-            keep[y, base : base + rows] = total[pl.ds(mine, rows)]
-            send[y, base : base + rows] = total[pl.ds(other, rows)].astype(BF16)
-        base += rows
 
 
 def pair_kernel(act, step, cum, dy, st, u, dcm, dbm, xdt_s, doff_s, dsc_s):
@@ -386,9 +421,9 @@
         ext[PIECE:] = edge[r]
         for t in range(CONV // LANES):
             cols = slice(t * LANES, (t + 1) * LANES)
-            sum_k = par[KW - 1 : KW, cols].astype(F32) * ext[0:PIECE, cols]
+            sum_k = par[KW - 1 : KW, cols] * ext[0:PIECE, cols]
             for k in range(KW - 1):
-                sum_k = sum_k + par[k : k + 1, cols].astype(F32) * ext[pl.ds(KW - 1 - k, PIECE), cols]
+                sum_k = sum_k + par[k : k + 1, cols] * ext[pl.ds(KW - 1 - k, PIECE), cols]
             dproj[r, :, cols] = sum_k.astype(BF16)
         dproj[r, :, CONV:] = draw[r].astype(BF16)
     hidden = hid[...].reshape(count * PIECE, D)
@@ -402,38 +437,11 @@
             send[y] = total[pl.ds(other, rows)].astype(BF16)
 
 
-def token_kernel(
-    tok, cot, dgate, dproj, wg0, wg1, weight, par, dpre, conv, sums, hsum,
-    grad, small, dh_s, ext, acc
-):
-    r = pl.program_id(0)
-    dh_s[...] = (
-        dot_nt(dgate[0, :, :D], wg0[...])
-        + dot_nt(dgate[0, :, D:], wg1[...])
-        + dot_nt(dproj[0], weight[...])
-    )
-    gain = par[5:6, :D].astype(F32)
-
-    @pl.when(r == 0)
+def taps_kernel(dpre, conv, sums, hsum, small, ext):
+    @pl.when(pl.program_id(0) == 0)
     def _():
-        acc[...] = jnp.zeros_like(acc)
         small[...] = jnp.zeros_like(small)
 
-    rows = 32
-
-    def chunk(i, carry):
-        at = pl.ds(pl.multiple_of(i * rows, rows), rows)
-        x = tok[0, at, :].astype(F32)
-        scale = lax.rsqrt(jnp.mean(x * x, axis=-1, keepdims=True) + EPS)
-        unit = x * scale
-        d_hidden = dh_s[at, :]
-        acc[...] += (d_hidden * unit).reshape(rows // 8, 8, D).sum(axis=0)
-        d_unit = d_hidden * gain
-        along = jnp.mean(d_unit * unit, axis=-1, keepdims=True)
-        grad[0, at, :] = (cot[0, at, :].astype(F32) + scale * (d_unit - unit * along)).astype(BF16)
-        return carry
-
-    lax.fori_loop(0, PIECE // rows, chunk, 0)
     for t in range(CONV // LANES):
         cols = slice(t * LANES, (t + 1) * LANES)
         slope = dpre[0, :, cols]
@@ -447,9 +455,27 @@
     small[7:8, LANES : 2 * LANES] += hsum[0, 1:2]
     small[7:8, 2 * LANES : 3 * LANES] += jnp.sum(sums[0, 8:16, :LANES], axis=0, keepdims=True)
 
-    @pl.when(r == pl.num_programs(0) - 1)
-    def _():
-        small[5:6, :D] = jnp.sum(acc[...], axis=0, keepdims=True)
+
+def slope_kernel(dgate, wg0, wg1, dh):
+    dh[0] = dot_nt(dgate[0, :, :D], wg0[...]) + dot_nt(dgate[0, :, D:], wg1[...])
+
+
+def token_kernel(tok, cot, dh, dproj, weight, par, _, grad, dh_s):
+    dh_s[...] = dh[0] + dot_nt(dproj[0], weight[...])
+    gain = par[5:6, :D]
+    rows = 32
+
+    def chunk(i, carry):
+        at = pl.ds(pl.multiple_of(i * rows, rows), rows)
+        x = tok[0, at, :].astype(F32)
+        scale = lax.rsqrt(jnp.mean(x * x, axis=-1, keepdims=True) + EPS)
+        unit = x * scale
+        d_unit = dh_s[at, :] * gain
+        along = jnp.mean(d_unit * unit, axis=-1, keepdims=True)
+        grad[0, at, :] = (cot[0, at, :].astype(F32) + scale * (d_unit - unit * along)).astype(BF16)
+        return carry
+
+    lax.fori_loop(0, PIECE // rows, chunk, 0)
 
 
 def local(size, tokens, cotangent, norm_in, w_in, conv_w, conv_b, dt_bias, a_log, skip, norm_out, w_out):
@@ -484,16 +510,6 @@
             x = jnp.stack([low, high], axis=have.index(bit))
         return x
 
-    def scatter(x, order):
-        have = sorted(order, reverse=True)
-        for bit in order:
-            axis = have.index(bit)
-            mine = lax.dynamic_index_in_dim(x, bit_of(bit), axis, False)
-            other = lax.dynamic_index_in_dim(x, 1 - bit_of(bit), axis, False)
-            x = mine + swap(other.astype(BF16), bit).astype(F32)
-            have.remove(bit)
-        return x
-
     micro, batch, count = tokens.shape[:3]
     tok = tokens.reshape(micro * batch, count, D)
     cot = cotangent.reshape(micro * batch, count, D)
@@ -503,17 +519,25 @@
         heads = heads.at[i, :H].set(a)
 
     own_conv, own_in, own_out = conv_b.shape[0], norm_in.shape[0], norm_out.shape[0]
-    par = jnp.zeros((8, CONV), BF16)
-    taps = jnp.concatenate([conv_w.T, conv_b[None]], axis=0)
-    par = lax.dynamic_update_slice(par, taps, (0, me * own_conv))
-    par = lax.dynamic_update_slice(par, norm_in[None], (5, me * own_in))
-    par = lax.dynamic_update_slice(par, norm_out[None], (6, me * own_out))
-    for bit in range(bits):
-        par = par + swap(par, bit)
+    owned_by = ((own_conv, tuple(range(KW + 1))), (own_in, (KW + 1,)), (own_out, (KW + 2,)))
 
     halo = lax.ppermute(tok[:, count - HALO :], "near", [(i, i + 1) for i in range(NEAR - 1)])
     rows_in = w_in.shape[0]
-    first = jnp.pad(w_in[:, DI:], ((0, 0), (0, PC - (w_in.shape[1] - DI))))
+    kinds = jnp.concatenate(
+        [
+            conv_w.T,
+            conv_b[None],
+            jnp.pad(norm_in, (0, own_conv - own_in))[None],
+            jnp.pad(norm_out, (0, own_conv - own_out))[None],
+        ],
+        axis=0,
+    )
+    turns = -(-kinds.shape[0] // rows_in)
+    kinds = jnp.pad(kinds, ((0, turns * rows_in - kinds.shape[0]), (0, 0)))
+    kinds = jnp.concatenate([kinds[t * rows_in : (t + 1) * rows_in] for t in range(turns)], axis=1)
+    spare = PC - (w_in.shape[1] - DI)
+    kinds = jnp.pad(kinds, ((0, 0), (0, spare - kinds.shape[1])))
+    first = jnp.concatenate([w_in[:, DI:], kinds], axis=1)
     blocks = devices // (2 * along)
     mine, recv = [], []
     for g in range(GROUPS):
@@ -529,48 +553,53 @@
     wo = rest[:, 2 * rows_in :].reshape(DI, D)
 
     smem = pl.BlockSpec(memory_space=pltpu.SMEM)
+    anywhere = pl.BlockSpec(memory_space=pl.ANY)
     half = (blocks, along * rows_in, GC)
     par_spec, head_spec = whole((8, CONV)), whole((8, LANES))
     row_d, row_i, row_c = per_row((PIECE, D)), per_row((PIECE, DI)), per_row((PIECE, CONV))
     row_l = per_row((PIECE, LANES))
     state_spec = pl.BlockSpec((NEAR, 1, NB, DI), lambda r: (0, r, 0, 0))
-    hid, conv, raw, act, dsilu, step, cum, pay, weight = pl.pallas_call(
-        enter_kernel,
+    hid, conv, raw, act, dsilu, step, cum, pay, weight, par = pl.pallas_call(
+        functools.partial(enter_kernel, owned_by),
         grid=(R,),
-        in_specs=[smem, row_d, per_row((HALO, D))] + [whole(half)] * 6 + [par_spec, head_spec],
+        in_specs=[smem, row_d, per_row((HALO, D))] + [whole(half)] * 6 + [head_spec],
         out_specs=[
             row_d, per_row((HALO + PIECE, CONV)), row_l, row_c, row_c, row_l, row_l,
             pl.BlockSpec((NEAR, 1, NB, DI + LANES), lambda r: (0, r, 0, 0)),
             whole((D, PC)),
+            par_spec,
         ],
         out_shape=[
             struct((R, PIECE, D), BF16), struct((R, HALO + PIECE, CONV), BF16), struct((R, PIECE, LANES), F32),
             struct((R, PIECE, CONV), BF16), struct((R, PIECE, CONV), F32), struct((R, PIECE, LANES), F32),
             struct((R, PIECE, LANES), F32), struct((NEAR, R, NB, DI + LANES), BF16), struct((D, PC), BF16),
+            struct((8, CONV), F32),
         ],
         scratch_shapes=[pltpu.VMEM((HALO + PIECE, CONV), F32)],
-        compiler_params=params(44),
+        compiler_params=params(60),
         cost_estimate=cost(R * 2e9, 2e7),
         name="enter",
-    )(core_arg, tok, halo, *mine, *recv, par, heads)
+    )(core_arg, tok, halo, *mine, *recv, heads)
 
     def exchange(x):
         return lax.all_to_all(x, "near", split_axis=0, concat_axis=0, tiled=True)
 
-    def carry_on(pieces, growths, backward):
+    def carry_on(pieces, growths, backward, ready):
         shape = pieces.shape
-        def kernel(p, g, o):
+
+        def kernel(p, g, _, o):
             pass_kernel(backward, p, g, o)
+
         return pl.pallas_call(
             kernel,
             grid=(1,),
-            in_specs=[whole(shape), pl.BlockSpec((NEAR, R, NB, LANES), lambda r: (0, 0, 0, DI // LANES))],
+            in_specs=[whole(shape), pl.BlockSpec((NEAR, R, NB, LANES), lambda r: (0, 0, 0, DI // LANES)), anywhere],
             out_specs=whole((NEAR, R, NB, DI)),
             out_shape=struct((NEAR, R, NB, DI), BF16),
-            compiler_params=params(16),
+            compiler_params=params(60),
             cost_estimate=cost(1e7, 2e6),
             name="pass",
-        )(pieces, growths)
+        )(pieces, growths, ready)
 
     pieces = exchange(pay)
     intra = pl.pallas_call(
@@ -580,7 +609,7 @@
         out_specs=row_i,
         out_shape=struct((R, PIECE, DI), F32),
         scratch_shapes=[pltpu.VMEM((PIECE, DI), BF16)],
-        compiler_params=params(32),
+        compiler_params=params(60),
         cost_estimate=cost(R * 4e9, 5e6),
         name="inside",
     )(act, step, cum)
@@ -590,11 +619,11 @@
         in_specs=[row_d, row_d, whole((D, D)), whole((D, D)), whole((DI, D))],
         out_specs=[row_i, row_i],
         out_shape=[struct((R, PIECE, DI), BF16), struct((R, PIECE, DI), F32)],
-        compiler_params=params(32),
+        compiler_params=params(60),
         cost_estimate=cost(R * 2e9, 1e7),
         name="gates",
     )(hid, cot, wg0, wg1, wo)
-    st = exchange(carry_on(pieces, pieces, False))
+    st = exchange(carry_on(pieces, pieces, False, intra))
 
     wide = pltpu.VMEM((PIECE, DI), F32)
     slim = pltpu.VMEM((PIECE, DI), BF16)
@@ -608,42 +637,37 @@
             struct((R, PIECE, LANES), F32), struct((NEAR, R, NB, DI), BF16), struct((R, 16, DI), F32),
         ],
         scratch_shapes=[wide, wide, slim, slim, slim, pltpu.VMEM((16, DI), F32)],
-        compiler_params=params(40),
+        compiler_params=params(60),
         cost_estimate=cost(R * 2e9, 1.5e7),
         name="middle",
     )(st, act, intra, cum, gate, dnorm, par, heads)
 
     pieces_b = exchange(back)
-    rest_rows = (DI + 2 * D) // (2 * blocks)
-    block_out, keep, send = pl.pallas_call(
-        outer_kernel,
+    rows_out = w_out.shape[0]
+    fused = rows_in % 8 == 0
+    if fused:
+        shapes = [(devices, rows_out + 2 * rows_in, D)]
+        scratch = [pltpu.VMEM((DI + 2 * D, D), F32)]
+    else:
+        shapes = [(DI, D), (D, D), (D, D)]
+        scratch = []
+    block_out, *made = pl.pallas_call(
+        functools.partial(outer_kernel, fused),
         grid=(1,),
         in_specs=[
-            smem, whole((R, PIECE, D)), whole((R, PIECE, D)), whole((R, PIECE, D)),
+            whole((R, PIECE, D)), whole((R, PIECE, D)), whole((R, PIECE, D)),
             whole((R, PIECE, DI)), whole((R, PIECE, DI)), whole((DI, D)),
         ],
-        out_specs=[whole((R, PIECE, D)), whole((blocks, rest_rows, D)), whole((blocks, rest_rows, D))],
-        out_shape=[
-            struct((R, PIECE, D), BF16), struct((blocks, rest_rows, D), F32), struct((blocks, rest_rows, D), BF16),
-        ],
-        scratch_shapes=[pltpu.VMEM((DI, D), F32)],
-        compiler_params=params(48),
+        out_specs=[whole((R, PIECE, D))] + [whole(shape) for shape in shapes],
+        out_shape=[struct((R, PIECE, D), BF16)] + [struct(shape, BF16) for shape in shapes],
+        scratch_shapes=scratch,
+        compiler_params=params(60),
         cost_estimate=cost(6e9, 2e7),
         name="outer",
-    )(core_arg, tok, cot, hid, normed, dgate, wo)
-    part = (keep + swap(send, core_bit).astype(F32)).reshape((2,) * len(high_bits) + (rest_rows, D))
-    part = scatter(part, high_bits)
-    cuts = (DI // (2 * blocks), D // (2 * blocks))
-    part = jnp.concatenate(
-        [
-            part[: cuts[0]].reshape(along, cuts[0] // along, D),
-            part[cuts[0] : cuts[0] + cuts[1]].reshape(along, rows_in, D),
-            part[cuts[0] + cuts[1] :].reshape(along, rows_in, D),
-        ],
-        axis=1,
-    )
-    own = lax.psum_scatter(part, ("far", "near"), scatter_dimension=0, tiled=False)
-    rows_out = w_out.shape[0]
+    )(tok, cot, hid, normed, dgate, wo)
+    if not fused:
+        made = [jnp.concatenate([part.reshape(devices, part.shape[0] // devices, D) for part in made], axis=1)]
+    own = lax.psum_scatter(made[0], AX, scatter_dimension=0, tiled=False).astype(F32)
     g_wout = own[:rows_out]
     g_gate = jnp.concatenate([own[rows_out : rows_out + rows_in], own[rows_out + rows_in :]], axis=1)
 
@@ -654,11 +678,21 @@
         out_specs=[row_i, row_l, row_l],
         out_shape=[struct((R, PIECE, DI), F32), struct((R, PIECE, N), F32), struct((R, PIECE, N), F32)],
         scratch_shapes=[slim, slim, pltpu.VMEM((PIECE, PIECE), F32)],
-        compiler_params=params(40),
+        compiler_params=params(60),
         cost_estimate=cost(R * 8e9, 1e7),
         name="pair",
     )(act, step, cum, dy, st)
-    later = exchange(carry_on(pieces_b, pieces, True))
+    dh = pl.pallas_call(
+        slope_kernel,
+        grid=(R,),
+        in_specs=[row_i, whole((D, D)), whole((D, D))],
+        out_specs=row_d,
+        out_shape=struct((R, PIECE, D), F32),
+        compiler_params=params(60),
+        cost_estimate=cost(R * 6e8, 6e6),
+        name="slope",
+    )(dgate, wg0, wg1)
+    later = exchange(carry_on(pieces_b, pieces, True, made[0]))
 
     dpre, edge, draw, hsum = pl.pallas_call(
         back_kernel,
@@ -672,7 +706,7 @@
             struct((R, PIECE, LANES), F32), struct((R, 8, LANES), F32),
         ],
         scratch_shapes=[wide, wide, wide, slim, slim, slim, pltpu.VMEM((16, DI), F32)],
-        compiler_params=params(44),
+        compiler_params=params(60),
         cost_estimate=cost(R * 2e9, 1.5e7),
         name="back",
     )(later, st, act, cum, step, raw, u, dcm, dbm, dy, dsilu, reach, heads)
@@ -687,38 +721,57 @@
         out_specs=[whole((R, PIECE, PC))] + [whole(half)] * 6,
         out_shape=[struct((R, PIECE, PC), BF16)] + [struct(half, F32)] * 3 + [struct(half, BF16)] * 3,
         scratch_shapes=[pltpu.VMEM((PIECE + 8, CONV), F32), pltpu.VMEM((D, GC), F32)],
-        compiler_params=params(44),
+        compiler_params=params(60),
         cost_estimate=cost(2e9, 1e7),
         name="input",
     )(core_arg, dpre, edge, draw, hid, par)
 
-    grad_tokens, small = pl.pallas_call(
+    small = pl.pallas_call(
+        taps_kernel,
+        grid=(R,),
+        in_specs=[row_c, per_row((HALO + PIECE, CONV)), per_row((16, DI)), per_row((8, LANES))],
+        out_specs=whole((8, CONV)),
+        out_shape=struct((8, CONV), F32),
+        scratch_shapes=[pltpu.VMEM((HALO + PIECE, LANES), F32)],
+        compiler_params=params(60),
+        cost_estimate=cost(2e7, 6e6),
+        name="taps",
+    )(dpre, conv, sums, hsum)
+
+    states = []
+    for keep_g, send_g in ((k0, s0), (k1, s1), (k2, s2)):
+        part = keep_g + swap(send_g, core_bit).astype(F32)
+        states.append(part.reshape((2,) * (bits - 1) + (rows_in, GC)))
+    small = small + swap(small, core_bit)
+    grad_tokens = pl.pallas_call(
         token_kernel,
         grid=(R,),
-        in_specs=[
-            row_d, row_d, row_i, per_row((PIECE, PC)), whole((D, D)), whole((D, D)), whole((D, PC)), par_spec,
-            row_c, per_row((HALO + PIECE, CONV)), per_row((16, DI)), per_row((8, LANES)),
-        ],
-        out_specs=[row_d, whole((8, CONV))],
-        out_shape=[struct((R, PIECE, D), BF16), struct((8, CONV), F32)],
-        scratch_shapes=[
-            pltpu.VMEM((PIECE, D), F32), pltpu.VMEM((HALO + PIECE, LANES), F32), pltpu.VMEM((8, D), F32),
-        ],
-        compiler_params=params(48),
+        in_specs=[row_d, row_d, row_d, per_row((PIECE, PC)), whole((D, PC)), par_spec, anywhere],
+        out_specs=row_d,
+        out_shape=struct((R, PIECE, D), BF16),
+        scratch_shapes=[pltpu.VMEM((PIECE, D), F32)],
+        compiler_params=params(60),
         cost_estimate=cost(R * 2e9, 1.5e7),
         name="token",
-    )(tok, cot, dgate, dproj, wg0, wg1, weight, par, dpre, conv, sums, hsum)
-
-    owned = []
-    for g, (keep_g, send_g) in enumerate(((k0, s0), (k1, s1), (k2, s2))):
-        part = keep_g + swap(send_g, core_bit).astype(F32)
-        part = part.reshape((2,) * (bits - 1) + (rows_in, GC))
-        owned.append(scatter(part, orders[g][::-1]))
-    g_win = jnp.concatenate([g_gate] + owned, axis=1)[:, : w_in.shape[1]]
-    for bit in range(bits):
-        small = small + swap(small, bit)
+    )(tok, cot, dh, dproj, weight, par, states[0])
+    order_s = orders[0][::-1]
+    have = [sorted(order, reverse=True) for order in orders]
+    for turn in range(bits - 1):
+        moved = []
+        for g in range(GROUPS):
+            bit = orders[g][::-1][turn]
+            axis = have[g].index(bit)
+            have[g].remove(bit)
+            moved.append((
+                lax.dynamic_index_in_dim(states[g], bit_of(bit), axis, False),
+                swap(lax.dynamic_index_in_dim(states[g], 1 - bit_of(bit), axis, False).astype(BF16), bit),
+            ))
+        other = swap(small, order_s[turn])
+        states = [mine_g + got.astype(F32) for mine_g, got in moved]
+        small = small + other
+    g_win = jnp.concatenate([g_gate] + states, axis=1)[:, : w_in.shape[1]]
+    g_gin = jnp.sum(g_win * w_in.astype(F32), axis=1) / norm_in.astype(F32)
     taps = lax.dynamic_slice(small, (0, me * own_conv), (5, own_conv))
-    g_gin = lax.dynamic_slice(small, (5, me * own_in), (1, own_in))[0]
     g_gout = lax.dynamic_slice(small, (6, me * own_out), (1, own_out))[0]
     return (
         block_out.reshape(tokens.shape),

time: 378 us -> 286 us (0.76)
  local copies, waits for them, and re-layouts: 67.4 us -> 18.2 us
  waiting for transfers between devices: 106 us -> 76.1 us
  blocking collectives: 26.4 us -> 0 us
  Pallas kernels: 82.6 us -> 104 us
  other arithmetic: 15.4 us -> 10.6 us
    unnamed x144 -> x50, local copies, waits for them, and re-layouts: 54.4 us -> 5.47 us
    all_to_all x3 -> x4, waiting for transfers between devices: 4.69 us -> 46.3 us  [exchange(): return lax.all_to_all(x, 'near', split_axis=0, concat_axis=0, tiled=True)]
    ppermute x42 -> x35, waiting for transfers between devices: 64 us -> 28.5 us  [swap(): return lax.ppermute(x, AX, [(i, i ^ 1 << bit) for i in range(devices)])]
    reduce_scatter x1, waiting for transfers between devices: 34.9 us -> 0.01 us  [local(): lax.psum_scatter(made[0], AX, scatter_dimension=0, tiled=False).astype(F32)]
    all_to_all x1 -> x0, blocking collectives: 26.4 us -> none  [exchange(): return lax.all_to_all(x, 'near', split_axis=0, concat_axis=0, tiled=True)]
    ppermute x42 -> x35, starting transfers between devices: 46.2 us -> 38.3 us  [swap(): return lax.ppermute(x, AX, [(i, i ^ 1 << bit) for i in range(devices)])]
    pallas_call x3 -> x5, Pallas kernels: 34.2 us -> 40.6 us  [the longest x1 14.7 us: local(): pl.pallas_call(functools.partial(enter_kernel, owned_by), grid=(R,), in_s...]
    add x21 -> x14, other arithmetic: 8.38 us -> 3.01 us  [the longest x9 2.14 us: local(): states = [mine_g + got.astype(F32) for mine_g, got in moved]]
  transfers between devices with their start and end apart: 49 -> 43, of which waited for: 25 -> 21; matrix products, arithmetic and copies ran while one was open for 7% -> 7% of each run, Pallas kernels for 15% -> 31%
where the time goes in v2:
time: 286 us; the launch traced here: 285 us
  Pallas kernels  104 us (36%)
  waiting for transfers between devices  76.1 us (27%)
  starting transfers between devices  60.8 us (21%)
  local copies, waits for them, and re-layouts  18.2 us (6%)
  between operations  14.8 us (5%)
  other arithmetic  10.6 us (4%)
    all_to_all x4, waiting for transfers between devices, exchange(): return lax.all_to_all(x, 'near', split_axis=0, concat_axis=0, tiled=True)  46.3 us
    ppermute x35, starting transfers between devices, swap(): return lax.ppermute(x, AX, [(i, i ^ 1 << bit) for i in range(devices)])  38.3 us
    ppermute x35, waiting for transfers between devices, swap(): return lax.ppermute(x, AX, [(i, i ^ 1 << bit) for i in range(devices)])  28.5 us
    all_to_all x4, starting transfers between devices, exchange(): return lax.all_to_all(x, 'near', split_axis=0, concat_axis=0, tiled=True)  18 us
    pallas_call x1, Pallas kernels, local(): pl.pallas_call(middle_kernel, grid=(R,), in_specs=[state_spec, row_c, row...  16.6 us
    pallas_call x1, Pallas kernels, local(): pl.pallas_call(functools.partial(enter_kernel, owned_by), grid=(R,), in_s...  14.7 us
    pallas_call x1, Pallas kernels, local(): pl.pallas_call(back_kernel, grid=(R,), in_specs=[state_spec, state_spec,...  12.2 us
    pallas_call x1, Pallas kernels, local(): pl.pallas_call(pair_kernel, grid=(R,), in_specs=[row_c, row_l, row_l, row...  9.85 us
  transfers between devices with their start and end apart: 43, of which 21 were waited for; matrix products, arithmetic and copies ran while one was open for 7% of the time, Pallas kernels for 31%

profile of v2, /device:TPU:0, one launch (start us, length us, event | category | flops | bytes accessed | tf_op | source)
XLA Modules:
  0.0 285.0 jit_solution(16330642341584095001)
XLA Ops:
  8.0 1.6 pad_maximum_fusion.6
  10.4 2.9 %collective-permute-start.5 = (bf16[24,640]{1,0:T(8,128)(2,1)S(1)}, bf16[24,640]{1,0:T(8,128)(2,1)S(1)}, u32[]{:S(2)}, u32[]{:S(2)}) collective-permute-start(bf16[24,640]{1,0:T(8,128)(2,1)S(1)} %get-tuple-element.150), channel_id=1, source_target_pairs={{0,1},{1,0},{2,3},{3,2},{4,5},{5,4},{6,7},{7,6},{8,9},{9,8},{10,11... | collective-permute-start | bytes 92168 | tf_op jit(solution)/shard_map/ppermute | solution.py:498
  13.3 2.6 collective-permute-start.1
  18.3 1.5 collective-permute-start.9
  20.6 1.0 collective-permute-start.6
  21.6 1.8 collective-permute-start.2
  24.1 1.8 collective-permute-done.6
  25.9 1.4 collective-permute-done.2
  27.7 2.0 collective-permute-start.7
  29.8 2.3 collective-permute-start.11
  32.5 2.2 collective-permute-done.7
  34.8 1.9 collective-permute-start.8
  37.7 1.0 collective-permute-done.4
  38.9 2.2 collective-permute-done.8
  41.2 4.7 %collective-permute-done.12 = bf16[2,2,2,24,640]{4,3,0,2,1:T(8,128)(2,1)S(1)} collective-permute-done((bf16[2,2,2,24,640]{4,3,0,2,1:T(8,128)(2,1)S(1)}, bf16[2,2,2,24,640]{4,3,0,2,1:T(8,128)(2,1)S(1)}, u32[]{:S(2)}, u32[]{:S(2)}) %collective-permute-start.12) | collective-permute-done | bytes 245792 | tf_op jit(solution)/shard_map/ppermute | solution.py:498
  47.8 2.9 %collective-permute-start = (bf16[2,16,768]{2,1,0:T(8,128)(2,1)S(1)}, bf16[2,16,768]{2,1,0:T(8,128)(2,1)S(1)}, u32[]{:S(2)}, u32[]{:S(2)}) collective-permute-start(bf16[2,16,768]{2,1,0:T(8,128)(2,1)S(1)} %slice.144), channel_id=1, source_target_pairs={{0,1},{1,2},{2,3},{3,4},{4,5},{5,6},{6,7},{8,9},{9,10},{10,11},{11... | collective-permute-start | bytes 147464 | tf_op jit(solution)/shard_map/ppermute | solution.py:524
  51.1 1.3 collective-permute-done.halo
  53.5 14.7 %enter.1 = (bf16[2,256,768]{2,1,0:T(8,128)(2,1)}, bf16[2,272,1792]{2,1,0:T(8,128)(2,1)}, f32[2,256,128]{2,1,0:T(8,128)}, bf16[2,256,1792]{2,1,0:T(8,128)(2,1)}, ...) custom-call(s32[1]{0:T(128)} %bitcast.2.core_ref, ...), custom_call_target="tpu_custom_call" | custom-call | flops 4000000000 | bytes 20000000 | tf_op jit(solution)/shard_map/enter/pallas_call | solution.py:562
  68.3 6.9 %all-to-all-start = ((bf16[8,2,16,1664]{3,2,1,0:T(8,128)(2,1)}), bf16[8,2,16,1664]{3,2,1,0:T(8,128)(2,1)S(1)}, u32[]{:S(2)}, u32[]{:S(2)}) async-start(bf16[8,2,16,1664]{3,2,1,0:T(8,128)(2,1)} %get-tuple-element.82), calls=%async_computation | async-start | bytes 1703936 | tf_op jit(solution)/shard_map/all_to_all | solution.py:585
  75.2 6.0 %inside.1._.intra = f32[2,256,1536]{2,1,0:T(8,128)} custom-call(bf16[2,256,1792]{2,1,0:T(8,128)(2,1)} %get-tuple-element.83.act, f32[2,256,128]{2,1,0:T(8,128)} %get-tuple-element.84.step, f32[2,256,128]{2,1,0:T(8,128)} %get-tuple-element.85.cum), custom_call_target="tpu_custom_call" | custom-call | flops 8000000000 | bytes 5000000 | tf_op jit(solution)/shard_map/inside/pallas_call | solution.py:605
  81.2 15.7 %all-to-all-done.p.g = bf16[8,2,16,1664]{3,2,1,0:T(8,128)(2,1)S(1)} async-done(((bf16[8,2,16,1664]{3,2,1,0:T(8,128)(2,1)}), bf16[8,2,16,1664]{3,2,1,0:T(8,128)(2,1)S(1)}, u32[]{:S(2)}, u32[]{:S(2)}) %all-to-all-start) | async-done | bytes 852000 | tf_op jit(solution)/shard_map/all_to_all | solution.py:585
  97.8 2.5 pass.2
  100.3 3.7 %all-to-all-start.1 = ((bf16[8,2,16,1536]{3,2,1,0:T(8,128)(2,1)}), bf16[8,2,16,1536]{3,2,1,0:T(8,128)(2,1)S(1)}, u32[]{:S(2)}, u32[]{:S(2)}) async-start(bf16[8,2,16,1536]{3,2,1,0:T(8,128)(2,1)} %pass.2), calls=%async_computation.1 | async-start | bytes 1572864 | tf_op jit(solution)/shard_map/all_to_all | solution.py:585
  104.1 3.5 %slice.147 = bf16[32,48,768]{2,1,0:T(8,128)(2,1)} slice(bf16[32,96,768]{2,1,0:T(8,128)(2,1)} %bitcast.149), slice={[0:32], [48:96], [0:768]} | slice | bytes 4718592 | tf_op jit(solution)/shard_map/slice | solution.py:553
  107.5 1.6 fusion.26
  109.1 6.6 %gates.1 = (bf16[2,256,1536]{2,1,0:T(8,128)(2,1)}, f32[2,256,1536]{2,1,0:T(8,128)}) custom-call(bf16[2,256,768]{2,1,0:T(8,128)(2,1)} %get-tuple-element.81.hid, bf16[2,256,768]{2,1,0:T(8,128)(2,1)} %bitcast.179, bf16[768,768]{1,0:T(8,128)(2,1)} %bitcast.153, bf16[768,768]{1,0:T(8,128)(2,1)} %bitcast.151, bf16[1536,768]{1,0:T(8,128)(2,1)} %bitcast.162), custom_call_target="tpu_custom_call" | custom-call | flops 4000000000 | bytes 10000000 | tf_op jit(solution)/shard_map/gates/pallas_call | solution.py:616
  115.7 8.4 %all-to-all-done.1.st = bf16[8,2,16,1536]{3,2,1,0:T(8,128)(2,1)S(1)} async-done(((bf16[8,2,16,1536]{3,2,1,0:T(8,128)(2,1)}), bf16[8,2,16,1536]{3,2,1,0:T(8,128)(2,1)S(1)}, u32[]{:S(2)}, u32[]{:S(2)}) %all-to-all-start.1) | async-done | bytes 786464 | tf_op jit(solution)/shard_map/all_to_all | solution.py:585
  125.0 16.6 %middle.1 = (bf16[2,256,1536]{2,1,0:T(8,128)(2,1)}, bf16[2,256,1536]{2,1,0:T(8,128)(2,1)}, bf16[2,256,1536]{2,1,0:T(8,128)(2,1)}, f32[2,256,128]{2,1,0:T(8,128)}...) custom-call(bf16[8,2,16,1536]{3,2,1,0:T(8,128)(2,1)} %copy-done.8, ...), custom_call_target="tpu_custom_call" | custom-call | flops 4000000000 | bytes 15000000 | tf_op jit(solution)/shard_map/middle/pallas_call | solution.py:630
  141.7 3.6 %all-to-all-start.2 = ((bf16[8,2,16,1536]{3,2,1,0:T(8,128)(2,1)}), bf16[8,2,16,1536]{3,2,1,0:T(8,128)(2,1)S(1)}, u32[]{:S(2)}, u32[]{:S(2)}) async-start(bf16[8,2,16,1536]{3,2,1,0:T(8,128)(2,1)} %get-tuple-element.92), calls=%async_computation.2 | async-start | bytes 1572864 | tf_op jit(solution)/shard_map/all_to_all | solution.py:585
  145.3 8.4 %outer.1 = (bf16[2,256,768]{2,1,0:T(8,128)(2,1)}, bf16[32,96,768]{2,1,0:T(8,128)(2,1)}) custom-call(bf16[2,256,768]{2,1,0:T(8,128)(2,1)} %bitcast.172, bf16[2,256,768]{2,1,0:T(8,128)(2,1)} %bitcast.180, bf16[2,256,768]{2,1,0:T(8,128)(2,1)} %get-tuple-element.81.hid, bf16[2,256,1536]{2,1,0:T(8,128)(2,1)} %get-tuple-element.89.normed, ...), custom_call_target="tpu_custom_call" | custom-call | flops 6000000000 | bytes 20000000 | tf_op jit(solution)/shard_map/outer/pallas_call | solution.py:654
  153.7 11.9 %all-to-all-done.2.p = bf16[8,2,16,1536]{3,2,1,0:T(8,128)(2,1)S(1)} async-done(((bf16[8,2,16,1536]{3,2,1,0:T(8,128)(2,1)}), bf16[8,2,16,1536]{3,2,1,0:T(8,128)(2,1)S(1)}, u32[]{:S(2)}, u32[]{:S(2)}) %all-to-all-start.2) | async-done | bytes 786464 | tf_op jit(solution)/shard_map/all_to_all | solution.py:585
  165.6 0.9 copy-done.2
  166.5 2.5 pass.3
  169.1 3.8 %all-to-all-start.3 = ((bf16[8,2,16,1536]{3,2,1,0:T(8,128)(2,1)}), bf16[8,2,16,1536]{3,2,1,0:T(8,128)(2,1)S(1)}, u32[]{:S(2)}, u32[]{:S(2)}) async-start(bf16[8,2,16,1536]{3,2,1,0:T(8,128)(2,1)} %pass.3), calls=%async_computation.3 | async-start | bytes 1572864 | tf_op jit(solution)/shard_map/all_to_all | solution.py:585
  172.9 9.8 %pair.1 = (f32[2,256,1536]{2,1,0:T(8,128)}, f32[2,256,128]{2,1,0:T(8,128)}, f32[2,256,128]{2,1,0:T(8,128)}) custom-call(bf16[2,256,1792]{2,1,0:T(8,128)(2,1)} %get-tuple-element.83.act, f32[2,256,128]{2,1,0:T(8,128)} %get-tuple-element.84.step, f32[2,256,128]{2,1,0:T(8,128)} %get-tuple-element.85.cum, bf16[2,256,1536]{2,1,0:T(8,128)(2,1)} %get-tuple-element.95.dy, ...), custom_call_target="tpu_custom_call" | custom-call | flops 16000000000 | bytes 10000000 | tf_op jit(solution)/shard_map/pair/pallas_call | solution.py:674
  182.7 10.3 %all-to-all-done.3.later = bf16[8,2,16,1536]{3,2,1,0:T(8,128)(2,1)S(1)} async-done(((bf16[8,2,16,1536]{3,2,1,0:T(8,128)(2,1)}), bf16[8,2,16,1536]{3,2,1,0:T(8,128)(2,1)S(1)}, u32[]{:S(2)}, u32[]{:S(2)}) %all-to-all-start.3) | async-done | bytes 786464 | tf_op jit(solution)/shard_map/all_to_all | solution.py:585
  193.9 12.2 %back.1 = (f32[2,256,1792]{2,1,0:T(8,128)}, f32[2,8,1792]{2,1,0:T(8,128)}, f32[2,256,128]{2,1,0:T(8,128)}, f32[2,8,128]{2,1,0:T(8,128)}) custom-call(bf16[8,2,16,1536]{3,2,1,0:T(8,128)(2,1)} %copy-done.9, bf16[8,2,16,1536]{3,2,1,0:T(8,128)(2,1)} %copy-done.8, bf16[2,256,1792]{2,1,0:T(8,128)(2,1)} %get-tuple-element.83.act, ...), custom_call_target="tpu_custom_call" | custom-call | flops 4000000000 | bytes 15000000 | tf_op jit(solution)/shard_map/back/pallas_call | solution.py:697
  206.1 4.3 %taps.1 = f32[8,1792]{1,0:T(8,128)} custom-call(f32[2,256,1792]{2,1,0:T(8,128)} %get-tuple-element.101.dpre, bf16[2,272,1792]{2,1,0:T(8,128)(2,1)} %get-tuple-element.112.conv, f32[2,16,1536]{2,1,0:T(8,128)} %get-tuple-element.113.sums, f32[2,8,128]{2,1,0:T(8,128)} %get-tuple-element.114.hsum), custom_call_target="tpu_custom_call" | custom-call | flops 20000000 | bytes 6000000 | tf_op jit(solution)/shard_map/taps/pallas_call | solution.py:729
  210.4 1.4 collective-permute-done.32
  212.7 1.4 collective-permute-start.33
  214.1 2.8 collective-permute-done.33
  216.9 1.1 collective-permute-start.34
  218.0 1.5 collective-permute-start.16
  219.5 1.6 collective-permute-done.34
  221.1 1.9 collective-permute-start.35
  223.1 4.4 %slope.1.dh = f32[2,256,768]{2,1,0:T(8,128)} custom-call(bf16[2,256,1536]{2,1,0:T(8,128)(2,1)} %get-tuple-element.90.dgate, bf16[768,768]{1,0:T(8,128)(2,1)} %bitcast.154, bf16[768,768]{1,0:T(8,128)(2,1)} %bitcast.152), custom_call_target="tpu_custom_call" | custom-call | flops 1200000000 | bytes 6000000 | tf_op jit(solution)/shard_map/slope/pallas_call | solution.py:685
  227.5 1.4 collective-permute-start.36
  229.6 7.4 %input.1 = (bf16[2,256,1920]{2,1,0:T(8,128)(2,1)}, f32[2,192,640]{2,1,0:T(8,128)}, f32[2,192,640]{2,1,0:T(8,128)}, f32[2,192,640]{2,1,0:T(8,128)}, bf16[2,192,64...) custom-call(s32[1]{0:T(128)} %bitcast.2.core_ref, ...), custom_call_target="tpu_custom_call" | custom-call | flops 2000000000 | bytes 10000000 | tf_op jit(solution)/shard_map/input/pallas_call | solution.py:715
  240.0 1.3 convert_add_fusion.2
  242.1 1.0 collective-permute-start.23
  243.5 8.8 %token_.1 = bf16[2,256,768]{2,1,0:T(8,128)(2,1)} custom-call(bf16[2,256,768]{2,1,0:T(8,128)(2,1)} %bitcast.173, bf16[2,256,768]{2,1,0:T(8,128)(2,1)} %bitcast.181, f32[2,256,768]{2,1,0:T(8,128)} %slope.1.dh, bf16[2,256,1920]{2,1,0:T(8,128)(2,1)} %get-tuple-element.104.dproj, bf16[768,1920]{1,0:T(8,128)(2,1)} %get-tuple-element.105.weight, ...), custom_call_target="tpu_custom_call" | custom-call | flops 4000000000 | bytes 15000000 | tf_op jit(solution)/shard_map/token/pallas_call | solution.py:746
  252.4 1.5 collective-permute-start.19
  253.9 1.0 bitcast_add_fusion.1
  254.9 1.7 collective-permute-start.24
  256.7 1.0 bitcast_add_fusion
  257.7 1.0 collective-permute-start.29
  258.8 1.4 collective-permute-start.20
  260.1 2.5 collective-permute-done.24
  262.7 2.2 collective-permute-start.25
  265.0 3.4 %collective-permute-done.29 = bf16[2,2,24,640]{3,2,0,1:T(8,128)(2,1)S(1)} collective-permute-done((bf16[2,2,24,640]{3,2,0,1:T(8,128)(2,1)S(1)}, bf16[2,2,24,640]{3,2,0,1:T(8,128)(2,1)S(1)}, u32[]{:S(2)}, u32[]{:S(2)}) %collective-permute-start.29) | collective-permute-done | bytes 122912 | tf_op jit(solution)/shard_map/ppermute | solution.py:498
  268.4 1.1 collective-permute-start.30
  269.8 1.4 collective-permute-start.26
  271.2 1.6 collective-permute-done.30
  272.8 1.7 collective-permute-start.31
  (167 shorter events, 23.4 us)
Async XLA Ops:
  7.2 96.9 %all-gather.3.cloned.1.call-start = ((), (), s32[]{:S(2)}) async-start(), calls=%async_computation.6 | async-start | bytes 4866048 | tf_op jit(solution)/shard_map/all_gather | solution.py:550
  10.4 9.4 %collective-permute-start.5 = (bf16[24,640]{1,0:T(8,128)(2,1)S(1)}, bf16[24,640]{1,0:T(8,128)(2,1)S(1)}, u32[]{:S(2)}, u32[]{:S(2)}) collective-permute-start(bf16[24,640]{1,0:T(8,128)(2,1)S(1)} %get-tuple-element.150), channel_id=1, source_target_pairs={{0,1},{1,0},{2,3},{3,2},{4,5},{5,4},{6,7},{7,6},{8,9},{9,8},{10,11... | collective-permute-start | bytes 92168 | tf_op jit(solution)/shard_map/ppermute | solution.py:498
  13.3 6.5 %collective-permute-start.1 = (bf16[24,640]{1,0:T(8,128)(2,1)S(1)}, bf16[24,640]{1,0:T(8,128)(2,1)S(1)}, u32[]{:S(2)}, u32[]{:S(2)}) collective-permute-start(bf16[24,640]{1,0:T(8,128)(2,1)S(1)} %get-tuple-element.151), channel_id=1, source_target_pairs={{0,4},{1,5},{2,6},{3,7},{4,0},{5,1},{6,2},{7,3},{8,12},{9,13},{10,... | collective-permute-start | bytes 92168 | tf_op jit(solution)/shard_map/ppermute | solution.py:498
  18.3 5.2 %collective-permute-start.9 = (bf16[24,640]{1,0:T(8,128)(2,1)S(1)}, bf16[24,640]{1,0:T(8,128)(2,1)S(1)}, u32[]{:S(2)}, u32[]{:S(2)}) collective-permute-start(bf16[24,640]{1,0:T(8,128)(2,1)S(1)} %fusion.15), channel_id=1, source_target_pairs={{0,16},{1,17},{2,18},{3,19},{4,20},{5,21},{6,22},{7,23},{8,24},{9,... | collective-permute-start | bytes 92168 | tf_op jit(solution)/shard_map/ppermute | solution.py:498
  20.6 5.2 %collective-permute-start.6 = (bf16[2,24,640]{2,1,0:T(8,128)(2,1)S(1)}, bf16[2,24,640]{2,1,0:T(8,128)(2,1)S(1)}, u32[]{:S(2)}, u32[]{:S(2)}) collective-permute-start(bf16[2,24,640]{2,1,0:T(8,128)(2,1)S(1)} %pad_maximum_fusion.11), channel_id=1, source_target_pairs={{0,4},{1,5},{2,6},{3,7},{4,0},{5,1},{6,2},{7,3},{8,12},{9,13},{10,... | collective-permute-start | bytes 184328 | tf_op jit(solution)/shard_map/ppermute | solution.py:498
  21.6 5.6 %collective-permute-start.2 = (bf16[2,24,640]{2,1,0:T(8,128)(2,1)S(1)}, bf16[2,24,640]{2,1,0:T(8,128)(2,1)S(1)}, u32[]{:S(2)}, u32[]{:S(2)}) collective-permute-start(bf16[2,24,640]{2,1,0:T(8,128)(2,1)S(1)} %pad_maximum_fusion.10), channel_id=1, source_target_pairs={{0,2},{1,3},{2,0},{3,1},{4,6},{5,7},{6,4},{7,5},{8,10},{9,11},{10,... | collective-permute-start | bytes 184328 | tf_op jit(solution)/shard_map/ppermute | solution.py:498
  23.5 6.3 %collective-permute-start.10 = (bf16[2,24,640]{2,1,0:T(8,128)(2,1)S(1)}, bf16[2,24,640]{2,1,0:T(8,128)(2,1)S(1)}, u32[]{:S(2)}, u32[]{:S(2)}) collective-permute-start(bf16[2,24,640]{2,1,0:T(8,128)(2,1)S(1)} %pad_maximum_fusion.12), channel_id=1, source_target_pairs={{0,1},{1,0},{2,3},{3,2},{4,5},{5,4},{6,7},{7,6},{8,9},{9,8},{10,11... | collective-permute-start | bytes 184328 | tf_op jit(solution)/shard_map/ppermute | solution.py:498
  27.3 5.1 %collective-permute-start.3 = (bf16[2,2,24,640]{3,2,0,1:T(8,128)(2,1)S(1)}, bf16[2,2,24,640]{3,2,0,1:T(8,128)(2,1)S(1)}, u32[]{:S(2)}, u32[]{:S(2)}) collective-permute-start(bf16[2,2,24,640]{3,2,0,1:T(8,128)(2,1)S(1)} %pad_maximum_fusion.7), channel_id=1, source_target_pairs={{0,16},{1,17},{2,18},{3,19},{4,20},{5,21},{6,22},{7,23},{8,24},{9,... | collective-permute-start | bytes 368648 | tf_op jit(solution)/shard_map/ppermute | solution.py:498
  27.7 7.0 %collective-permute-start.7 = (bf16[2,2,24,640]{3,2,1,0:T(8,128)(2,1)S(1)}, bf16[2,2,24,640]{3,2,1,0:T(8,128)(2,1)S(1)}, u32[]{:S(2)}, u32[]{:S(2)}) collective-permute-start(bf16[2,2,24,640]{3,2,1,0:T(8,128)(2,1)S(1)} %pad_maximum_fusion.8), channel_id=1, source_target_pairs={{0,2},{1,3},{2,0},{3,1},{4,6},{5,7},{6,4},{7,5},{8,10},{9,11},{10,... | collective-permute-start | bytes 368648 | tf_op jit(solution)/shard_map/ppermute | solution.py:498
  29.8 7.7 %collective-permute-start.11 = (bf16[2,2,24,640]{3,2,0,1:T(8,128)(2,1)S(1)}, bf16[2,2,24,640]{3,2,0,1:T(8,128)(2,1)S(1)}, u32[]{:S(2)}, u32[]{:S(2)}) collective-permute-start(bf16[2,2,24,640]{3,2,0,1:T(8,128)(2,1)S(1)} %pad_maximum_fusion.9), channel_id=1, source_target_pairs={{0,4},{1,5},{2,6},{3,7},{4,0},{5,1},{6,2},{7,3},{8,12},{9,13},{10,... | collective-permute-start | bytes 368648 | tf_op jit(solution)/shard_map/ppermute | solution.py:498
  32.5 6.3 %collective-permute-start.4 = (bf16[2,2,2,24,640]{4,3,1,2,0:T(8,128)(2,1)S(1)}, bf16[2,2,2,24,640]{4,3,1,2,0:T(8,128)(2,1)S(1)}, u32[]{:S(2)}, u32[]{:S(2)}) collective-permute-start(bf16[2,2,2,24,640]{4,3,1,2,0:T(8,128)(2,1)S(1)} %pad_maximum_fusion.3), channel_id=1, source_target_pairs={{0,1},{1,0},{2,3},{3,2},{4,5},{5,4},{6,7},{7,6},{8,9},{9,8},{10,11... | collective-permute-start | bytes 737288 | tf_op jit(solution)/shard_map/ppermute | solution.py:498
  34.8 6.3 %collective-permute-start.8 = (bf16[2,2,2,24,640]{4,3,2,0,1:T(8,128)(2,1)S(1)}, bf16[2,2,2,24,640]{4,3,2,0,1:T(8,128)(2,1)S(1)}, u32[]{:S(2)}, u32[]{:S(2)}) collective-permute-start(bf16[2,2,2,24,640]{4,3,2,0,1:T(8,128)(2,1)S(1)} %pad_maximum_fusion.4), channel_id=1, source_target_pairs={{0,16},{1,17},{2,18},{3,19},{4,20},{5,21},{6,22},{7,23},{8,24},{9,... | collective-permute-start | bytes 737288 | tf_op jit(solution)/shard_map/ppermute | solution.py:498
  37.6 8.4 %collective-permute-start.12 = (bf16[2,2,2,24,640]{4,3,0,2,1:T(8,128)(2,1)S(1)}, bf16[2,2,2,24,640]{4,3,0,2,1:T(8,128)(2,1)S(1)}, u32[]{:S(2)}, u32[]{:S(2)}) collective-permute-start(bf16[2,2,2,24,640]{4,3,0,2,1:T(8,128)(2,1)S(1)} %pad_maximum_fusion.5), channel_id=1, source_target_pairs={{0,2},{1,3},{2,0},{3,1},{4,6},{5,7},{6,4},{7,5},{8,10},{9,11},{10,... | collective-permute-start | bytes 737288 | tf_op jit(solution)/shard_map/ppermute | solution.py:498
  38.9 7.3 %copy-start.10 = (bf16[2,2,2,2,24,640]{5,4,3,2,1,0:T(8,128)(2,1)}, bf16[2,2,2,2,24,640]{5,4,3,2,1,0:T(8,128)(2,1)S(1)}, u32[]{:S(2)}) copy-start(bf16[2,2,2,2,24,640]{5,4,3,2,1,0:T(8,128)(2,1)S(1)} %copy.22) | copy-start | bytes 1474564
  41.2 9.5 %copy-start.14 = (f32[24]{0:T(128)S(1)}, f32[24]{0:T(128)}, u32[]{:S(2)}) copy-start(f32[24]{0:T(128)} %param.23) | copy-start | bytes 292
  41.2 9.5 %copy-start.15 = (f32[24]{0:T(128)S(1)}, f32[24]{0:T(128)}, u32[]{:S(2)}) copy-start(f32[24]{0:T(128)} %param.24) | copy-start | bytes 292
  41.2 9.7 %copy-start.16 = (f32[24]{0:T(128)S(1)}, f32[24]{0:T(128)}, u32[]{:S(2)}) copy-start(f32[24]{0:T(128)} %param.25) | copy-start | bytes 292
  46.2 6.3 %copy-start.11 = (bf16[2,2,2,2,24,640]{5,4,3,2,1,0:T(8,128)(2,1)}, bf16[2,2,2,2,24,640]{5,4,3,2,1,0:T(8,128)(2,1)S(1)}, u32[]{:S(2)}) copy-start(bf16[2,2,2,2,24,640]{5,4,3,2,1,0:T(8,128)(2,1)S(1)} %copy.25) | copy-start | bytes 1474564
  46.2 6.2 %collective-permute-start.13 = (bf16[2,192,640]{2,1,0:T(8,128)(2,1)S(1)}, bf16[2,192,640]{2,1,0:T(8,128)(2,1)S(1)}, u32[]{:S(2)}, u32[]{:S(2)}) collective-permute-start(bf16[2,192,640]{2,1,0:T(8,128)(2,1)S(1)} %bitcast.166), channel_id=1, source_target_pairs={{0,8},{1,9},{2,10},{3,11},{4,12},{5,13},{6,14},{7,15},{8,0},{9,1},... | collective-permute-start | bytes 1474568 | tf_op jit(solution)/shard_map/ppermute | solution.py:498
  46.3 6.1 %copy-start.12 = (bf16[2,192,640]{2,1,0:T(8,128)(2,1)}, bf16[2,192,640]{2,1,0:T(8,128)(2,1)S(1)}, u32[]{:S(2)}) copy-start(bf16[2,192,640]{2,1,0:T(8,128)(2,1)S(1)} %pad_maximum_fusion.1.m1) | copy-start | bytes 1474564
  46.3 6.1 %collective-permute-start.14 = (bf16[2,192,640]{2,1,0:T(8,128)(2,1)S(1)}, bf16[2,192,640]{2,1,0:T(8,128)(2,1)S(1)}, u32[]{:S(2)}, u32[]{:S(2)}) collective-permute-start(bf16[2,192,640]{2,1,0:T(8,128)(2,1)S(1)} %pad_maximum_fusion.1.m1), channel_id=1, source_target_pairs={{0,8},{1,9},{2,10},{3,11},{4,12},{5,13},{6,14},{7,15},{8,0},{9,1},... | collective-permute-start | bytes 1474568 | tf_op jit(solution)/shard_map/ppermute | solution.py:498
  46.9 5.5 %collective-permute-start.15 = (bf16[2,192,640]{2,1,0:T(8,128)(2,1)S(1)}, bf16[2,192,640]{2,1,0:T(8,128)(2,1)S(1)}, u32[]{:S(2)}, u32[]{:S(2)}) collective-permute-start(bf16[2,192,640]{2,1,0:T(8,128)(2,1)S(1)} %bitcast.168), channel_id=1, source_target_pairs={{0,8},{1,9},{2,10},{3,11},{4,12},{5,13},{6,14},{7,15},{8,0},{9,1},... | collective-permute-start | bytes 1474568 | tf_op jit(solution)/shard_map/ppermute | solution.py:498
  47.8 4.6 %collective-permute-start = (bf16[2,16,768]{2,1,0:T(8,128)(2,1)S(1)}, bf16[2,16,768]{2,1,0:T(8,128)(2,1)S(1)}, u32[]{:S(2)}, u32[]{:S(2)}) collective-permute-start(bf16[2,16,768]{2,1,0:T(8,128)(2,1)S(1)} %slice.144), channel_id=1, source_target_pairs={{0,1},{1,2},{2,3},{3,4},{4,5},{5,6},{6,7},{8,9},{9,10},{10,11},{11... | collective-permute-start | bytes 147464 | tf_op jit(solution)/shard_map/ppermute | solution.py:524
  51.1 1.4 copy-start.13
  52.4 0.9 copy-start.19
  52.4 1.1 copy-start.20
  68.3 28.7 %all-to-all-start = ((bf16[8,2,16,1664]{3,2,1,0:T(8,128)(2,1)}), bf16[8,2,16,1664]{3,2,1,0:T(8,128)(2,1)S(1)}, u32[]{:S(2)}, u32[]{:S(2)}) async-start(bf16[8,2,16,1664]{3,2,1,0:T(8,128)(2,1)} %get-tuple-element.82), calls=%async_computation | async-start | bytes 1703936 | tf_op jit(solution)/shard_map/all_to_all | solution.py:585
  96.9 0.9 copy-start
  100.3 23.8 %all-to-all-start.1 = ((bf16[8,2,16,1536]{3,2,1,0:T(8,128)(2,1)}), bf16[8,2,16,1536]{3,2,1,0:T(8,128)(2,1)S(1)}, u32[]{:S(2)}, u32[]{:S(2)}) async-start(bf16[8,2,16,1536]{3,2,1,0:T(8,128)(2,1)} %pass.2), calls=%async_computation.1 | async-start | bytes 1572864 | tf_op jit(solution)/shard_map/all_to_all | solution.py:585
  104.1 3.5 %copy-start.1 = (bf16[3072,768]{1,0:T(8,128)(2,1)S(1)}, bf16[3072,768]{1,0:T(8,128)(2,1)}, u32[]{:S(2)}) copy-start(bf16[3072,768]{1,0:T(8,128)(2,1)} %all-gather.3.cloned.1.call-done) | copy-start | bytes 14155780
  124.1 0.9 copy-start.8
  141.7 23.9 %all-to-all-start.2 = ((bf16[8,2,16,1536]{3,2,1,0:T(8,128)(2,1)}), bf16[8,2,16,1536]{3,2,1,0:T(8,128)(2,1)S(1)}, u32[]{:S(2)}, u32[]{:S(2)}) async-start(bf16[8,2,16,1536]{3,2,1,0:T(8,128)(2,1)} %get-tuple-element.92), calls=%async_computation.2 | async-start | bytes 1572864 | tf_op jit(solution)/shard_map/all_to_all | solution.py:585
  145.2 129.2 %reduce-scatter.2.cloned.1.call-start = ((), (), s32[]{:S(2)}) async-start(), calls=%async_computation.5 | async-start | bytes 4866048 | tf_op jit(solution)/shard_map/reduce_scatter | solution.py:670
  165.6 0.9 copy-start.2
  169.1 23.9 %all-to-all-start.3 = ((bf16[8,2,16,1536]{3,2,1,0:T(8,128)(2,1)}), bf16[8,2,16,1536]{3,2,1,0:T(8,128)(2,1)S(1)}, u32[]{:S(2)}, u32[]{:S(2)}) async-start(bf16[8,2,16,1536]{3,2,1,0:T(8,128)(2,1)} %pass.3), calls=%async_computation.3 | async-start | bytes 1572864 | tf_op jit(solution)/shard_map/all_to_all | solution.py:585
  193.0 0.9 copy-start.9
  206.1 11.8 %copy-start.21 = (f32[2,8,1792]{2,1,0:T(8,128)S(1)}, f32[2,8,1792]{2,1,0:T(8,128)}, u32[]{:S(2)}) copy-start(f32[2,8,1792]{2,1,0:T(8,128)} %get-tuple-element.102) | copy-start | bytes 344068
  210.4 1.5 collective-permute-start.32
  212.7 4.2 %collective-permute-start.33 = (f32[8,1792]{1,0:T(8,128)S(1)}, f32[8,1792]{1,0:T(8,128)S(1)}, u32[]{:S(2)}, u32[]{:S(2)}) collective-permute-start(f32[8,1792]{1,0:T(8,128)S(1)} %add.164), channel_id=1, source_target_pairs={{0,1},{1,0},{2,3},{3,2},{4,5},{5,4},{6,7},{7,6},{8,9},{9,8},{10,11... | collective-permute-start | bytes 172040 | tf_op jit(solution)/shard_map/ppermute | solution.py:498
  216.9 4.2 %collective-permute-start.34 = (f32[8,1792]{1,0:T(8,128)S(1)}, f32[8,1792]{1,0:T(8,128)S(1)}, u32[]{:S(2)}, u32[]{:S(2)}) collective-permute-start(f32[8,1792]{1,0:T(8,128)S(1)} %add.165), channel_id=1, source_target_pairs={{0,16},{1,17},{2,18},{3,19},{4,20},{5,21},{6,22},{7,23},{8,24},{9,... | collective-permute-start | bytes 172040 | tf_op jit(solution)/shard_map/ppermute | solution.py:498
  218.0 11.0 %collective-permute-start.16 = (f32[2,8,1792]{2,1,0:T(8,128)S(1)}, f32[2,8,1792]{2,1,0:T(8,128)S(1)}, u32[]{:S(2)}, u32[]{:S(2)}) collective-permute-start(f32[2,8,1792]{2,1,0:T(8,128)S(1)} %copy-done.21), channel_id=1, source_target_pairs={{1,0},{2,1},{3,2},{4,3},{5,4},{6,5},{7,6},{9,8},{10,9},{11,10},{12... | collective-permute-start | bytes 344072 | tf_op jit(solution)/shard_map/ppermute | solution.py:713
  221.1 6.4 %collective-permute-start.35 = (f32[8,1792]{1,0:T(8,128)S(1)}, f32[8,1792]{1,0:T(8,128)S(1)}, u32[]{:S(2)}, u32[]{:S(2)}) collective-permute-start(f32[8,1792]{1,0:T(8,128)S(1)} %add.166), channel_id=1, source_target_pairs={{0,2},{1,3},{2,0},{3,1},{4,6},{5,7},{6,4},{7,5},{8,10},{9,11},{10,... | collective-permute-start | bytes 172040 | tf_op jit(solution)/shard_map/ppermute | solution.py:498
  227.5 10.1 %collective-permute-start.36 = (f32[8,1792]{1,0:T(8,128)S(1)}, f32[8,1792]{1,0:T(8,128)S(1)}, u32[]{:S(2)}, u32[]{:S(2)}) collective-permute-start(f32[8,1792]{1,0:T(8,128)S(1)} %add.167), channel_id=1, source_target_pairs={{0,4},{1,5},{2,6},{3,7},{4,0},{5,1},{6,2},{7,3},{8,12},{9,13},{10,... | collective-permute-start | bytes 172040 | tf_op jit(solution)/shard_map/ppermute | solution.py:498
  237.1 4.9 %copy-start.7 = (f32[2,192,640]{2,1,0:T(8,128)S(1)}, f32[2,192,640]{2,1,0:T(8,128)}, u32[]{:S(2)}) copy-start(f32[2,192,640]{2,1,0:T(8,128)} %get-tuple-element.108) | copy-start | bytes 2949124
  237.1 2.9 %collective-permute-start.17 = (bf16[2,192,640]{2,1,0:T(8,128)(2,1)}, bf16[2,192,640]{2,1,0:T(8,128)(2,1)S(1)}, u32[]{:S(2)}, u32[]{:S(2)}) collective-permute-start(bf16[2,192,640]{2,1,0:T(8,128)(2,1)} %get-tuple-element.107), channel_id=1, source_target_pairs={{0,8},{1,9},{2,10},{3,11},{4,12},{5,13},{6,14},{7,15},{8,0},{9,1},... | collective-permute-start | bytes 1474568 | tf_op jit(solution)/shard_map/ppermute | solution.py:498
  237.1 4.9 %collective-permute-start.22 = (bf16[2,192,640]{2,1,0:T(8,128)(2,1)}, bf16[2,192,640]{2,1,0:T(8,128)(2,1)S(1)}, u32[]{:S(2)}, u32[]{:S(2)}) collective-permute-start(bf16[2,192,640]{2,1,0:T(8,128)(2,1)} %get-tuple-element.109), channel_id=1, source_target_pairs={{0,8},{1,9},{2,10},{3,11},{4,12},{5,13},{6,14},{7,15},{8,0},{9,1},... | collective-permute-start | bytes 1474568 | tf_op jit(solution)/shard_map/ppermute | solution.py:498
  237.6 5.6 %collective-permute-start.27 = (bf16[2,192,640]{2,1,0:T(8,128)(2,1)}, bf16[2,192,640]{2,1,0:T(8,128)(2,1)S(1)}, u32[]{:S(2)}, u32[]{:S(2)}) collective-permute-start(bf16[2,192,640]{2,1,0:T(8,128)(2,1)} %get-tuple-element.111), channel_id=1, source_target_pairs={{0,8},{1,9},{2,10},{3,11},{4,12},{5,13},{6,14},{7,15},{8,0},{9,1},... | collective-permute-start | bytes 1474568 | tf_op jit(solution)/shard_map/ppermute | solution.py:498
  241.3 2.0 copy-start.3
  241.3 1.9 copy-start.6
  241.3 11.0 %collective-permute-start.18 = (bf16[2,2,2,24,640]{4,3,2,1,0:T(8,128)(2,1)S(1)}, bf16[2,2,2,24,640]{4,3,2,1,0:T(8,128)(2,1)S(1)}, u32[]{:S(2)}, u32[]{:S(2)}) collective-permute-start(bf16[2,2,2,24,640]{4,3,2,1,0:T(8,128)(2,1)S(1)} %fusion), channel_id=1, source_target_pairs={{0,1},{1,0},{2,3},{3,2},{4,5},{5,4},{6,7},{7,6},{8,9},{9,8},{10,11... | collective-permute-start | bytes 737288 | tf_op jit(solution)/shard_map/ppermute | solution.py:498
  242.1 11.8 %collective-permute-start.23 = (bf16[2,2,2,24,640]{4,3,2,0,1:T(8,128)(2,1)S(1)}, bf16[2,2,2,24,640]{4,3,2,0,1:T(8,128)(2,1)}, u32[]{:S(2)}, u32[]{:S(2)}) collective-permute-start(bf16[2,2,2,24,640]{4,3,2,0,1:T(8,128)(2,1)S(1)} %fusion.1), channel_id=1, source_target_pairs={{0,16},{1,17},{2,18},{3,19},{4,20},{5,21},{6,22},{7,23},{8,24},{9,... | collective-permute-start | bytes 737288 | tf_op jit(solution)/shard_map/ppermute | solution.py:498
  243.3 13.3 %collective-permute-start.28 = (bf16[2,2,2,24,640]{4,3,0,2,1:T(8,128)(2,1)S(1)}, bf16[2,2,2,24,640]{4,3,0,2,1:T(8,128)(2,1)}, u32[]{:S(2)}, u32[]{:S(2)}) collective-permute-start(bf16[2,2,2,24,640]{4,3,0,2,1:T(8,128)(2,1)S(1)} %fusion.2), channel_id=1, source_target_pairs={{0,2},{1,3},{2,0},{3,1},{4,6},{5,7},{6,4},{7,5},{8,10},{9,11},{10,... | collective-permute-start | bytes 737288 | tf_op jit(solution)/shard_map/ppermute | solution.py:498
  243.5 8.8 %copy-start.4 = (f32[2,192,640]{2,1,0:T(8,128)S(1)}, f32[2,192,640]{2,1,0:T(8,128)}, u32[]{:S(2)}) copy-start(f32[2,192,640]{2,1,0:T(8,128)} %copy-done.3) | copy-start | bytes 2949124
  252.4 6.3 %collective-permute-start.19 = (bf16[2,2,24,640]{3,2,1,0:T(8,128)(2,1)S(1)}, bf16[2,2,24,640]{3,2,1,0:T(8,128)(2,1)S(1)}, u32[]{:S(2)}, u32[]{:S(2)}) collective-permute-start(bf16[2,2,24,640]{3,2,1,0:T(8,128)(2,1)S(1)} %fusion.3), channel_id=1, source_target_pairs={{0,16},{1,17},{2,18},{3,19},{4,20},{5,21},{6,22},{7,23},{8,24},{9,... | collective-permute-start | bytes 368648 | tf_op jit(solution)/shard_map/ppermute | solution.py:498
  254.9 7.7 %collective-permute-start.24 = (bf16[2,2,24,640]{3,2,1,0:T(8,128)(2,1)S(1)}, bf16[2,2,24,640]{3,2,1,0:T(8,128)(2,1)S(1)}, u32[]{:S(2)}, u32[]{:S(2)}) collective-permute-start(bf16[2,2,24,640]{3,2,1,0:T(8,128)(2,1)S(1)} %fusion.4), channel_id=1, source_target_pairs={{0,2},{1,3},{2,0},{3,1},{4,6},{5,7},{6,4},{7,5},{8,10},{9,11},{10,... | collective-permute-start | bytes 368648 | tf_op jit(solution)/shard_map/ppermute | solution.py:498
  257.7 10.7 %collective-permute-start.29 = (bf16[2,2,24,640]{3,2,0,1:T(8,128)(2,1)S(1)}, bf16[2,2,24,640]{3,2,0,1:T(8,128)(2,1)S(1)}, u32[]{:S(2)}, u32[]{:S(2)}) collective-permute-start(bf16[2,2,24,640]{3,2,0,1:T(8,128)(2,1)S(1)} %fusion.5), channel_id=1, source_target_pairs={{0,4},{1,5},{2,6},{3,7},{4,0},{5,1},{6,2},{7,3},{8,12},{9,13},{10,... | collective-permute-start | bytes 368648 | tf_op jit(solution)/shard_map/ppermute | solution.py:498
  258.8 18.0 %copy-start.5 = (bf16[24,3352]{1,0:T(8,128)(2,1)S(1)}, bf16[24,3352]{1,0:T(8,128)(2,1)}, u32[]{:S(2)}) copy-start(bf16[24,3352]{1,0:T(8,128)(2,1)} %param.20) | copy-start | bytes 482692
  258.8 10.8 %collective-permute-start.20 = (bf16[2,24,640]{2,1,0:T(8,128)(2,1)S(1)}, bf16[2,24,640]{2,1,0:T(8,128)(2,1)S(1)}, u32[]{:S(2)}, u32[]{:S(2)}) collective-permute-start(bf16[2,24,640]{2,1,0:T(8,128)(2,1)S(1)} %fusion.8), channel_id=1, source_target_pairs={{0,2},{1,3},{2,0},{3,1},{4,6},{5,7},{6,4},{7,5},{8,10},{9,11},{10,... | collective-permute-start | bytes 184328 | tf_op jit(solution)/shard_map/ppermute | solution.py:498
  262.7 14.9 %copy-start.17 = (bf16[24]{0:T(256)(128)(2,1)S(1)}, bf16[24]{0:T(256)(128)(2,1)}, u32[]{:S(2)}) copy-start(bf16[24]{0:T(256)(128)(2,1)} %param.19) | copy-start | bytes 148
  262.7 7.0 %collective-permute-start.25 = (bf16[2,24,640]{2,1,0:T(8,128)(2,1)S(1)}, bf16[2,24,640]{2,1,0:T(8,128)(2,1)S(1)}, u32[]{:S(2)}, u32[]{:S(2)}) collective-permute-start(bf16[2,24,640]{2,1,0:T(8,128)(2,1)S(1)} %fusion.9), channel_id=1, source_target_pairs={{0,4},{1,5},{2,6},{3,7},{4,0},{5,1},{6,2},{7,3},{8,12},{9,13},{10,... | collective-permute-start | bytes 184328 | tf_op jit(solution)/shard_map/ppermute | solution.py:498
  268.4 4.3 %collective-permute-start.30 = (bf16[2,24,640]{2,1,0:T(8,128)(2,1)S(1)}, bf16[2,24,640]{2,1,0:T(8,128)(2,1)S(1)}, u32[]{:S(2)}, u32[]{:S(2)}) collective-permute-start(bf16[2,24,640]{2,1,0:T(8,128)(2,1)S(1)} %fusion.10), channel_id=1, source_target_pairs={{0,1},{1,0},{2,3},{3,2},{4,5},{5,4},{6,7},{7,6},{8,9},{9,8},{10,11... | collective-permute-start | bytes 184328 | tf_op jit(solution)/shard_map/ppermute | solution.py:498
  269.6 6.5 %collective-permute-start.21 = (bf16[24,640]{1,0:T(8,128)(2,1)S(1)}, bf16[24,640]{1,0:T(8,128)(2,1)S(1)}, u32[]{:S(2)}, u32[]{:S(2)}) collective-permute-start(bf16[24,640]{1,0:T(8,128)(2,1)S(1)} %fusion.16), channel_id=1, source_target_pairs={{0,4},{1,5},{2,6},{3,7},{4,0},{5,1},{6,2},{7,3},{8,12},{9,13},{10,... | collective-permute-start | bytes 92168 | tf_op jit(solution)/shard_map/ppermute | solution.py:498
  269.8 6.3 %collective-permute-start.26 = (bf16[24,640]{1,0:T(8,128)(2,1)S(1)}, bf16[24,640]{1,0:T(8,128)(2,1)S(1)}, u32[]{:S(2)}, u32[]{:S(2)}) collective-permute-start(bf16[24,640]{1,0:T(8,128)(2,1)S(1)} %fusion.17), channel_id=1, source_target_pairs={{0,1},{1,0},{2,3},{3,2},{4,5},{5,4},{6,7},{7,6},{8,9},{9,8},{10,11... | collective-permute-start | bytes 92168 | tf_op jit(solution)/shard_map/ppermute | solution.py:498
  272.8 4.0 %collective-permute-start.31 = (bf16[24,640]{1,0:T(8,128)(2,1)S(1)}, bf16[24,640]{1,0:T(8,128)(2,1)S(1)}, u32[]{:S(2)}, u32[]{:S(2)}) collective-permute-start(bf16[24,640]{1,0:T(8,128)(2,1)S(1)} %fusion.18), channel_id=1, source_target_pairs={{0,16},{1,17},{2,18},{3,19},{4,20},{5,21},{6,22},{7,23},{8,24},{9,... | collective-permute-start | bytes 92168 | tf_op jit(solution)/shard_map/ppermute | solution.py:498
  (3 other events, 2.1 us)
Sparse Core Ops, SparseCore 0:
  11.6 67.7 all-gather.2
  153.8 112.2 reduce-scatter.1

commit v3 on v2

--- a/solution.py
+++ b/solution.py
@@ -1,4 +1,5 @@
 import functools
+import itertools
 import math
 
 import jax
@@ -19,12 +20,16 @@
 DI = H * HP
 CONV = DI + 2 * N
 PC = 1920
-GROUPS = 3
-GC = PC // GROUPS
+WIDTHS = (640, 640, 640)
+REST = DI + 2 * D
+RWIDTH = REST // len(WIDTHS)
+GROUPS = len(WIDTHS)
+SPANS = tuple(slice(sum(WIDTHS[:g]), sum(WIDTHS[: g + 1])) for g in range(GROUPS))
 NEAR = SEQ_LEN // PIECE
 NB = N // NEAR
 HALO = 16
 LANES = 128
+HALO_TURN = 2
 EPS = 1e-05
 F32 = jnp.float32
 BF16 = jnp.bfloat16
@@ -106,8 +111,7 @@
 
 def assemble(core, mine, recv, weight_s):
     count, rows, _ = mine[0].shape
-    for g in range(GROUPS):
-        cols = slice(g * GC, (g + 1) * GC)
+    for g, cols in enumerate(SPANS):
         for y in range(count):
             first = pl.multiple_of((2 * y + core) * rows, 16)
             other = pl.multiple_of((2 * y + 1 - core) * rows, 16)
@@ -138,12 +142,14 @@
 
 
 def enter_kernel(
-    owned, core_ref, tok, halo, m0, m1, m2, r0, r1, r2, heads,
-    hid, conv, raw, act, dsilu, step, cum, pay, weight, par, ext
+    owned, core_ref, tok, halo, heads, *refs
 ):
+    mine, recv, rest = refs[:GROUPS], refs[GROUPS : 2 * GROUPS], refs[2 * GROUPS :]
+    hid, conv, raw, act, dsilu, step, cum, pay, weight, par, ext = rest
+
     @pl.when(pl.program_id(0) == 0)
     def _():
-        assemble(core_ref[0], (m0, m1, m2), (r0, r1, r2), weight)
+        assemble(core_ref[0], mine, recv, weight)
         par[...] = jnp.zeros_like(par)
         lay_out(weight, par, owned)
 
@@ -284,38 +290,68 @@
     sums[0, 8:16, LANES:] = jnp.zeros((8, DI - LANES), F32)
 
 
-def outer_kernel(fused, tok, cot, hid, normed, dgate, wo, out, *refs):
-    count = tok.shape[0]
+def outer_kernel(rows_in, core_ref, cot, hid, normed, dgate, keep, send, total, sums):
+    core = core_ref[0]
+    count = cot.shape[0]
     tangent = cot[...].reshape(count * PIECE, D)
     hidden = hid[...].reshape(count * PIECE, D)
-    parts = (
-        lambda: dot_tn(normed[...].reshape(count * PIECE, DI), tangent),
-        lambda: dot_tn(hidden, dgate[:, :, :D].reshape(count * PIECE, D)),
-        lambda: dot_tn(hidden, dgate[:, :, D:].reshape(count * PIECE, D)),
-    )
-    if fused:
-        rest, total = refs
-        devices = rest.shape[0]
-        at = 0
-        for part in parts:
-            made = part()
-            total[at : at + made.shape[0]] = made
-            at += made.shape[0]
-        long, short = DI // devices, D // devices
-        for d in range(devices):
-            rest[d] = jnp.concatenate(
-                [
-                    total[d * long : (d + 1) * long],
-                    total[DI + d * short : DI + (d + 1) * short],
-                    total[DI + D + d * short : DI + D + (d + 1) * short],
-                ],
-                axis=0,
-            ).astype(BF16)
-    else:
-        for ref, part in zip(refs, parts):
-            ref[...] = part().astype(BF16)
-    for r in range(count):
-        out[r] = (tok[r].astype(F32) + dot(normed[r], wo[...])).astype(BF16)
+    total[...] = dot_tn(normed[...].reshape(count * PIECE, DI), tangent)
+    for half in range(2):
+        cols = slice(half * D, (half + 1) * D)
+        sums[:, cols] = dot_tn(hidden, dgate[:, :, cols].reshape(count * PIECE, D))
+    for d in range(D // rows_in):
+        for half in range(2):
+            start = (2 * d + half) * rows_in
+            sums[d * rows_in : (d + 1) * rows_in, DI + half * D : DI + (half + 1) * D] = total[start : start + rows_in]
+    blocks, rows, _ = keep.shape
+    for y in range(blocks):
+        mine = pl.multiple_of((2 * y + core) * rows, 16)
+        other = pl.multiple_of((2 * y + 1 - core) * rows, 16)
+        keep[y] = sums[pl.ds(mine, rows)]
+        send[y] = sums[pl.ds(other, rows)].astype(BF16)
+
+
+def join_kernel(cuts, axes, bit_ref, small, other, _, *refs):
+    count = 1 + max(operand for group in cuts for operand, _, _ in group)
+    keeps, recvs = refs[:count], refs[count : 2 * count]
+    outs, sends = refs[2 * count : 2 * count + GROUPS], refs[2 * count + GROUPS : 2 * count + 2 * GROUPS]
+    refs[-1][...] = small[...] + other[...]
+    for g, group in enumerate(cuts):
+        bit, axis = bit_ref[g], axes[g]
+        base = 0
+        for operand, start, width in group:
+            keep, recv = keeps[operand], recvs[operand]
+            source, target = slice(start, start + width), slice(base, base + width)
+            for place in itertools.product(range(2), repeat=keep.ndim - 3):
+                mine = place[:axis] + (bit,) + place[axis:] + (slice(None), source)
+                away = place[:axis] + (1 - bit,) + place[axis:] + (slice(None), source)
+                here = place + (slice(None), target)
+                outs[g][here] = keep[mine] + recv[mine].astype(F32)
+                sends[g][here] = (keep[away] + recv[away].astype(F32)).astype(BF16)
+            base += width
+
+
+def last_kernel(small, other, w_in, gain, *refs):
+    keeps, recvs = refs[:GROUPS], refs[GROUPS : 2 * GROUPS]
+    small_out, g_win, g_wout, g_gin = refs[2 * GROUPS :]
+    small_out[...] = small[...] + other[...]
+    rows, width = g_win.shape
+    for g in range(GROUPS):
+        total = keeps[g][...] + recvs[g][...].astype(F32)
+        start = DI + SPANS[g].start
+        stop = min(start + WIDTHS[g], width)
+        g_win[:, start:stop] = total[:, : stop - start]
+        first = g * RWIDTH
+        for lo, hi, ref, row in ((0, DI, g_win, 0), (DI, DI + D, g_wout, 0), (DI + D, REST, g_wout, rows)):
+            a, b = max(lo, first), min(hi, first + RWIDTH)
+            if a < b:
+                at = WIDTHS[g] + a - first
+                ref[row : row + rows, a - lo : b - lo] = total[:, at : at + b - a]
+    g_gin[...] = jnp.sum(g_win[...] * w_in[...].astype(F32), axis=-1, keepdims=True) / gain[...].astype(F32)
+
+
+def result_kernel(tok, normed, wo, _, out):
+    out[0] = (tok[0].astype(F32) + dot(normed[0], wo[...])).astype(BF16)
 
 
 def pair_kernel(act, step, cum, dy, st, u, dcm, dbm, xdt_s, doff_s, dsc_s):
@@ -355,7 +391,7 @@
 
 
 def back_kernel(
-    later, st, act, cum, step, raw, u, dcm, dbm, dy, dsilu, reach, heads,
+    later, st, act, cum, step, raw, u, dcm, dbm, dy, dsilu, reach, heads, _, __, ___,
     dpre, edge, draw, hsum, dw_s, far_s, size_s, high_s, low_s, wts_s, sum_s
 ):
     spread = heads_to_lanes()
@@ -413,7 +449,10 @@
     hsum[0] = jnp.where(pick == 0, for_bias, jnp.where(pick == 1, for_log, 0.0))
 
 
-def input_kernel(core_ref, dpre, edge, draw, hid, par, dproj, k0, k1, k2, s0, s1, s2, ext, total):
+def input_kernel(core_ref, dpre, edge, draw, hid, par, gone, dproj, small, *refs):
+    keeps, sends = refs[:GROUPS], refs[GROUPS : 2 * GROUPS]
+    ext, *totals = refs[2 * GROUPS :]
+    small[...] = gone[...]
     core = core_ref[0]
     count = dpre.shape[0]
     for r in range(count):
@@ -427,8 +466,8 @@
             dproj[r, :, cols] = sum_k.astype(BF16)
         dproj[r, :, CONV:] = draw[r].astype(BF16)
     hidden = hid[...].reshape(count * PIECE, D)
-    for g, (keep, send) in enumerate(((k0, s0), (k1, s1), (k2, s2))):
-        total[...] = dot_tn(hidden, dproj[:, :, g * GC : (g + 1) * GC].reshape(count * PIECE, GC))
+    for keep, send, total, cols in zip(keeps, sends, totals, SPANS):
+        total[...] = dot_tn(hidden, dproj[:, :, cols].reshape(count * PIECE, cols.stop - cols.start))
         blocks, rows, _ = keep.shape
         for y in range(blocks):
             mine = pl.multiple_of((2 * y + core) * rows, 16)
@@ -488,21 +527,28 @@
     high_bits = list(range(bits - 1, core_bit, -1))
     far_bits = list(range(core_bit - 1, -1, -1))
     dims = [far_bits[-1:], far_bits[:-1], high_bits] if core_bit == 3 else [far_bits[-3:], far_bits[:-3], high_bits]
-    orders = [
-        dims[1] + dims[2] + dims[0],
-        dims[0] + dims[1] + dims[2],
-        dims[2] + dims[0] + dims[1],
-    ]
+    orders = [dims[1] + dims[2] + dims[0], dims[0] + dims[1] + dims[2], dims[2] + dims[0] + dims[1]]
+    if [len(dim) for dim in dims] == [1, 2, 1]:
+        x, (top, low), y = dims[0][0], dims[1], dims[2][0]
+        orders = [[top, low, y, x], [top, x, low, y], [top, y, x, low]]
 
     def swap(x, bit):
         return lax.ppermute(x, AX, [(i, i ^ (1 << bit)) for i in range(devices)])
 
     def bit_of(bit):
         return (me >> bit) & 1
+
+    def after(x, other):
+        rows, cols = min(x.shape[-2], other.shape[-2], 8), min(x.shape[-1], other.shape[-1])
+        part = other[(0,) * (other.ndim - 2)][:rows, :cols].astype(x.dtype)
+        return x + 0 * jnp.pad(part, ((0, x.shape[-2] - rows), (0, x.shape[-1] - cols)))
 
     def gather(x, order):
         have = []
         for bit in order:
+            if order is orders[0]:
+                if len(have) == HALO_TURN:
+                    x = after(x, halo)
             other = swap(x, bit)
             have = sorted(have + [bit], reverse=True)
             mine = bit_of(bit) == 0
@@ -541,8 +587,8 @@
     blocks = devices // (2 * along)
     mine, recv = [], []
     for g in range(GROUPS):
-        part = gather(first[:, g * GC : (g + 1) * GC], orders[g])
-        part = part.reshape(blocks, along * rows_in, GC)
+        part = gather(first[:, SPANS[g]], orders[g])
+        part = part.reshape(blocks, along * rows_in, WIDTHS[g])
         mine.append(part)
         recv.append(swap(part, core_bit))
 
@@ -554,7 +600,8 @@
 
     smem = pl.BlockSpec(memory_space=pltpu.SMEM)
     anywhere = pl.BlockSpec(memory_space=pl.ANY)
-    half = (blocks, along * rows_in, GC)
+    inside = pl.BlockSpec(memory_space=pltpu.VMEM)
+    halves = [(blocks, along * rows_in, width) for width in WIDTHS]
     par_spec, head_spec = whole((8, CONV)), whole((8, LANES))
     row_d, row_i, row_c = per_row((PIECE, D)), per_row((PIECE, DI)), per_row((PIECE, CONV))
     row_l = per_row((PIECE, LANES))
@@ -562,7 +609,7 @@
     hid, conv, raw, act, dsilu, step, cum, pay, weight, par = pl.pallas_call(
         functools.partial(enter_kernel, owned_by),
         grid=(R,),
-        in_specs=[smem, row_d, per_row((HALO, D))] + [whole(half)] * 6 + [head_spec],
+        in_specs=[smem, row_d, per_row((HALO, D)), head_spec] + [whole(half) for half in halves] * 2,
         out_specs=[
             row_d, per_row((HALO + PIECE, CONV)), row_l, row_c, row_c, row_l, row_l,
             pl.BlockSpec((NEAR, 1, NB, DI + LANES), lambda r: (0, r, 0, 0)),
@@ -579,7 +626,7 @@
         compiler_params=params(60),
         cost_estimate=cost(R * 2e9, 2e7),
         name="enter",
-    )(core_arg, tok, halo, *mine, *recv, heads)
+    )(core_arg, tok, halo, heads, *mine, *recv)
 
     def exchange(x):
         return lax.all_to_all(x, "near", split_axis=0, concat_axis=0, tiled=True)
@@ -644,32 +691,18 @@
 
     pieces_b = exchange(back)
     rows_out = w_out.shape[0]
-    fused = rows_in % 8 == 0
-    if fused:
-        shapes = [(devices, rows_out + 2 * rows_in, D)]
-        scratch = [pltpu.VMEM((DI + 2 * D, D), F32)]
-    else:
-        shapes = [(DI, D), (D, D), (D, D)]
-        scratch = []
-    block_out, *made = pl.pallas_call(
-        functools.partial(outer_kernel, fused),
-        grid=(1,),
-        in_specs=[
-            whole((R, PIECE, D)), whole((R, PIECE, D)), whole((R, PIECE, D)),
-            whole((R, PIECE, DI)), whole((R, PIECE, DI)), whole((DI, D)),
-        ],
-        out_specs=[whole((R, PIECE, D))] + [whole(shape) for shape in shapes],
-        out_shape=[struct((R, PIECE, D), BF16)] + [struct(shape, BF16) for shape in shapes],
-        scratch_shapes=scratch,
+    rest_shape = (blocks, along * rows_in, REST)
+    rest_keep, rest_send = pl.pallas_call(
+        functools.partial(outer_kernel, rows_in),
+        in_specs=[smem] + [inside] * 4,
+        out_specs=[inside] * 2,
+        out_shape=[struct(rest_shape, F32), struct(rest_shape, BF16)],
+        scratch_shapes=[pltpu.VMEM((DI, D), F32), pltpu.VMEM((D, REST), F32)],
         compiler_params=params(60),
         cost_estimate=cost(6e9, 2e7),
         name="outer",
-    )(tok, cot, hid, normed, dgate, wo)
-    if not fused:
-        made = [jnp.concatenate([part.reshape(devices, part.shape[0] // devices, D) for part in made], axis=1)]
-    own = lax.psum_scatter(made[0], AX, scatter_dimension=0, tiled=False).astype(F32)
-    g_wout = own[:rows_out]
-    g_gate = jnp.concatenate([own[rows_out : rows_out + rows_in], own[rows_out + rows_in :]], axis=1)
+    )(core_arg, cot, hid, normed, dgate)
+    rest_recv = swap(rest_send, core_bit)
 
     u, dcm, dbm = pl.pallas_call(
         pair_kernel,
@@ -692,13 +725,25 @@
         cost_estimate=cost(R * 6e8, 6e6),
         name="slope",
     )(dgate, wg0, wg1)
-    later = exchange(carry_on(pieces_b, pieces, True, made[0]))
+    later_p = carry_on(pieces_b, pieces, True, rest_keep)
+    block_out = pl.pallas_call(
+        result_kernel,
+        grid=(R,),
+        in_specs=[row_d, row_i, whole((DI, D)), anywhere],
+        out_specs=row_d,
+        out_shape=struct((R, PIECE, D), BF16),
+        compiler_params=params(60),
+        cost_estimate=cost(R * 6e8, 6e6),
+        name="result",
+    )(tok, normed, wo, later_p)
+    later = exchange(later_p)
 
     dpre, edge, draw, hsum = pl.pallas_call(
         back_kernel,
         grid=(R,),
         in_specs=[
             state_spec, state_spec, row_c, row_l, row_l, row_l, row_i, row_l, row_l, row_i, row_c, row_l, head_spec,
+            anywhere, anywhere, anywhere,
         ],
         out_specs=[row_c, per_row((8, CONV)), row_l, per_row((8, LANES))],
         out_shape=[
@@ -709,22 +754,8 @@
         compiler_params=params(60),
         cost_estimate=cost(R * 2e9, 1.5e7),
         name="back",
-    )(later, st, act, cum, step, raw, u, dcm, dbm, dy, dsilu, reach, heads)
+    )(later, st, act, cum, step, raw, u, dcm, dbm, dy, dsilu, reach, heads, dh, block_out, rest_recv)
     edge = lax.ppermute(edge, "near", [(i + 1, i) for i in range(NEAR - 1)])
-
-    dproj, k0, k1, k2, s0, s1, s2 = pl.pallas_call(
-        input_kernel,
-        grid=(1,),
-        in_specs=[
-            smem, whole((R, PIECE, CONV)), whole((R, 8, CONV)), whole((R, PIECE, LANES)), whole((R, PIECE, D)), par_spec,
-        ],
-        out_specs=[whole((R, PIECE, PC))] + [whole(half)] * 6,
-        out_shape=[struct((R, PIECE, PC), BF16)] + [struct(half, F32)] * 3 + [struct(half, BF16)] * 3,
-        scratch_shapes=[pltpu.VMEM((PIECE + 8, CONV), F32), pltpu.VMEM((D, GC), F32)],
-        compiler_params=params(60),
-        cost_estimate=cost(2e9, 1e7),
-        name="input",
-    )(core_arg, dpre, edge, draw, hid, par)
 
     small = pl.pallas_call(
         taps_kernel,
@@ -738,39 +769,77 @@
         name="taps",
     )(dpre, conv, sums, hsum)
 
-    states = []
-    for keep_g, send_g in ((k0, s0), (k1, s1), (k2, s2)):
-        part = keep_g + swap(send_g, core_bit).astype(F32)
-        states.append(part.reshape((2,) * (bits - 1) + (rows_in, GC)))
-    small = small + swap(small, core_bit)
-    grad_tokens = pl.pallas_call(
-        token_kernel,
-        grid=(R,),
-        in_specs=[row_d, row_d, row_d, per_row((PIECE, PC)), whole((D, PC)), par_spec, anywhere],
-        out_specs=row_d,
-        out_shape=struct((R, PIECE, D), BF16),
-        scratch_shapes=[pltpu.VMEM((PIECE, D), F32)],
-        compiler_params=params(60),
-        cost_estimate=cost(R * 2e9, 1.5e7),
-        name="token",
-    )(tok, cot, dh, dproj, weight, par, states[0])
-    order_s = orders[0][::-1]
+    dproj, small, *parts = pl.pallas_call(
+        input_kernel,
+        in_specs=[smem] + [inside] * 6,
+        out_specs=[inside] * (2 + 2 * GROUPS),
+        out_shape=[struct((R, PIECE, PC), BF16), struct((8, CONV), F32)]
+        + [pltpu.VMEM(half, F32) for half in halves] + [pltpu.VMEM(half, BF16) for half in halves],
+        scratch_shapes=[pltpu.VMEM((PIECE + 8, CONV), F32), *(pltpu.VMEM((D, width), F32) for width in WIDTHS)],
+        compiler_params=params(44),
+        cost_estimate=cost(2e9, 1e7),
+        name="input",
+    )(core_arg, dpre, edge, draw, hid, par, small)
+
+    def by_bits(x):
+        count = x.size // (rows_in * x.shape[-1])
+        return x.reshape((2,) * int(math.log2(count)) + (rows_in, x.shape[-1]))
+
     have = [sorted(order, reverse=True) for order in orders]
+    cuts = [[(g, 0, WIDTHS[g]), (GROUPS, g * RWIDTH, RWIDTH)] for g in range(GROUPS)]
+    keeps = parts[:GROUPS] + [rest_keep]
+    recvs = [swap(x, core_bit) for x in parts[GROUPS:]] + [rest_recv]
+    other = swap(small, core_bit)
+    ahead = small
     for turn in range(bits - 1):
-        moved = []
+        now = [order[::-1][turn] for order in orders]
+        axes = [have[g].index(now[g]) for g in range(GROUPS)]
+        shapes = [(2,) * (bits - 2 - turn) + (rows_in, WIDTHS[g] + RWIDTH) for g in range(GROUPS)]
+        *made, small = pl.pallas_call(
+            functools.partial(join_kernel, cuts, axes),
+            in_specs=[smem, inside, inside, anywhere] + [inside] * (2 * len(keeps)),
+            out_specs=[inside] * (2 * GROUPS + 1),
+            out_shape=[pltpu.VMEM(shape, F32) for shape in shapes]
+            + [pltpu.VMEM(shape, BF16) for shape in shapes] + [pltpu.VMEM((8, CONV), F32)],
+            compiler_params=params(40),
+            cost_estimate=cost(1e6, 8e6),
+            name="join",
+        )(
+            jnp.stack([bit_of(bit) for bit in now]).astype(jnp.int32),
+            small, other, ahead, *map(by_bits, keeps), *map(by_bits, recvs),
+        )
+        if turn == 0:
+            grad_tokens = pl.pallas_call(
+                token_kernel,
+                grid=(R,),
+                in_specs=[row_d, row_d, row_d, per_row((PIECE, PC)), whole((D, PC)), par_spec, anywhere],
+                out_specs=row_d,
+                out_shape=struct((R, PIECE, D), BF16),
+                scratch_shapes=[pltpu.VMEM((PIECE, D), F32)],
+                compiler_params=params(32),
+                cost_estimate=cost(R * 2e9, 1.5e7),
+                name="token",
+            )(tok, cot, dh, dproj, weight, par, small)
+            ahead = grad_tokens
         for g in range(GROUPS):
-            bit = orders[g][::-1][turn]
-            axis = have[g].index(bit)
-            have[g].remove(bit)
-            moved.append((
-                lax.dynamic_index_in_dim(states[g], bit_of(bit), axis, False),
-                swap(lax.dynamic_index_in_dim(states[g], 1 - bit_of(bit), axis, False).astype(BF16), bit),
-            ))
-        other = swap(small, order_s[turn])
-        states = [mine_g + got.astype(F32) for mine_g, got in moved]
-        small = small + other
-    g_win = jnp.concatenate([g_gate] + states, axis=1)[:, : w_in.shape[1]]
-    g_gin = jnp.sum(g_win * w_in.astype(F32), axis=1) / norm_in.astype(F32)
+            have[g].remove(now[g])
+        cuts = [[(g, 0, WIDTHS[g] + RWIDTH)] for g in range(GROUPS)]
+        keeps = made[:GROUPS]
+        recvs = [swap(x, now[g]) for g, x in enumerate(made[GROUPS:])]
+        other = swap(small, orders[0][::-1][turn])
+    flat = [x.reshape(rows_in, x.shape[-1]) for x in keeps + recvs]
+    small, g_win, g_wout, g_gin = pl.pallas_call(
+        last_kernel,
+        in_specs=[inside] * (4 + 2 * GROUPS),
+        out_specs=[inside] * 4,
+        out_shape=[
+            struct((8, CONV), F32), struct(w_in.shape, F32), struct(w_out.shape, F32), struct((rows_in, 1), F32),
+        ],
+        compiler_params=params(32),
+        cost_estimate=cost(1e6, 1e6),
+        name="last",
+    )(small, other, w_in, norm_in[:, None], *flat)
+    g_gin = g_gin[:, 0]
     taps = lax.dynamic_slice(small, (0, me * own_conv), (5, own_conv))
     g_gout = lax.dynamic_slice(small, (6, me * own_out), (1, own_out))[0]
     return (

time: 286 us -> 290 us (1.014)
  Pallas kernels: 104 us -> 110 us
  other arithmetic: 10.6 us -> 5.45 us
  waiting for transfers between devices: 76.1 us -> 80.3 us
    ppermute x35 -> x36, waiting for transfers between devices: 28.5 us -> 37.7 us  [swap(): return lax.ppermute(x, AX, [(i, i ^ 1 << bit) for i in range(devices)])]
    pallas_call x2 -> x8, Pallas kernels: 15.9 us -> 24.2 us  [the longest x1 8.19 us: local(): pl.pallas_call(functools.partial(outer_kernel, rows_in), in_specs=[smem]...]
    all_to_all x4, waiting for transfers between devices: 46.3 us -> 41.5 us  [exchange(): return lax.all_to_all(x, 'near', split_axis=0, concat_axis=0, tiled=True)]
    add x17 -> x1, other arithmetic: 4.47 us -> 0.02 us  [after(): x + 0 * jnp.pad(part, ((0, x.shape[-2] - rows), (0, x.shape[-1] - cols)))]
    unnamed x50 -> x60, local copies, waits for them, and re-layouts: 5.47 us -> 6.39 us
    ppermute x35 -> x36, starting transfers between devices: 38.3 us -> 38.7 us  [swap(): return lax.ppermute(x, AX, [(i, i ^ 1 << bit) for i in range(devices)])]
  transfers between devices with their start and end apart: 43 -> 43, of which waited for: 21 -> 21; matrix products, arithmetic and copies ran while one was open for 7% -> 4% of each run, Pallas kernels for 31% -> 24%
where the time goes in v3:
time: 290 us; the launch traced here: 289 us
  Pallas kernels  110 us (38%)
  waiting for transfers between devices  80.3 us (28%)
  starting transfers between devices  60.8 us (21%)
  local copies, waits for them, and re-layouts  18.2 us (6%)
  between operations  14.7 us (5%)
  other arithmetic  5.45 us (2%)
    all_to_all x4, waiting for transfers between devices, exchange(): return lax.all_to_all(x, 'near', split_axis=0, concat_axis=0, tiled=True)  41.5 us
    ppermute x36, starting transfers between devices, swap(): return lax.ppermute(x, AX, [(i, i ^ 1 << bit) for i in range(devices)])  38.7 us
    ppermute x36, waiting for transfers between devices, swap(): return lax.ppermute(x, AX, [(i, i ^ 1 << bit) for i in range(devices)])  37.7 us
    pallas_call x1, Pallas kernels, local(): pl.pallas_call(middle_kernel, grid=(R,), in_specs=[state_spec, row_c, row...  16.5 us
    all_to_all x4, starting transfers between devices, exchange(): return lax.all_to_all(x, 'near', split_axis=0, concat_axis=0, tiled=True)  15.7 us
    pallas_call x1, Pallas kernels, local(): pl.pallas_call(functools.partial(enter_kernel, owned_by), grid=(R,), in_s...  14.7 us
    pallas_call x1, Pallas kernels, local(): pl.pallas_call(back_kernel, grid=(R,), in_specs=[state_spec, state_spec,...  12.3 us
    pallas_call x1, Pallas kernels, local(): pl.pallas_call(pair_kernel, grid=(R,), in_specs=[row_c, row_l, row_l, row...  9.75 us
  transfers between devices with their start and end apart: 43, of which 21 were waited for; matrix products, arithmetic and copies ran while one was open for 4% of the time, Pallas kernels for 24%

profile of v3, /device:TPU:0, one launch (start us, length us, event | category | flops | bytes accessed | tf_op | source)
XLA Modules:
  0.0 289.1 jit_solution(14435885293693037813)
XLA Ops:
  8.0 1.6 pad_maximum_fusion.6
  10.4 4.8 %collective-permute-start = (bf16[2,16,768]{2,1,0:T(8,128)(2,1)S(1)}, bf16[2,16,768]{2,1,0:T(8,128)(2,1)S(1)}, u32[]{:S(2)}, u32[]{:S(2)}) collective-permute-start(bf16[2,16,768]{2,1,0:T(8,128)(2,1)S(1)} %slice.124), channel_id=1, source_target_pairs={{0,1},{1,2},{2,3},{3,4},{4,5},{5,6},{6,7},{8,9},{9,10},{10,11},{11... | collective-permute-start | bytes 147464 | tf_op jit(solution)/shard_map/ppermute | solution.py:570
  16.0 2.6 collective-permute-start.5
  22.1 2.7 collective-permute-start.1
  24.8 1.6 collective-permute-start.6
  26.4 1.6 collective-permute-start.10
  28.8 1.2 collective-permute-start.2
  30.1 1.0 collective-permute-start.7
  31.1 1.0 collective-permute-start.11
  32.1 1.5 collective-permute-done.2
  33.6 1.5 collective-permute-start.3
  35.8 1.4 collective-permute-start.8
  38.1 1.7 collective-permute-done.3
  39.9 1.2 collective-permute-start.4
  41.1 2.7 collective-permute-done.8
  43.9 1.7 collective-permute-done.12
  46.5 2.6 collective-permute-done.4
  49.9 1.4 collective-permute-done.13.refs_3_
  52.0 14.7 %enter.1 = (bf16[2,256,768]{2,1,0:T(8,128)(2,1)}, bf16[2,272,1792]{2,1,0:T(8,128)(2,1)}, f32[2,256,128]{2,1,0:T(8,128)}, bf16[2,256,1792]{2,1,0:T(8,128)(2,1)}, ...) custom-call(s32[1]{0:T(128)} %bitcast.1.core_ref, ...), custom_call_target="tpu_custom_call" | custom-call | flops 4000000000 | bytes 20000000 | tf_op jit(solution)/shard_map/enter/pallas_call | solution.py:609
  66.7 4.6 %all-to-all-start = ((bf16[8,2,16,1664]{3,2,1,0:T(8,128)(2,1)}), bf16[8,2,16,1664]{3,2,1,0:T(8,128)(2,1)S(1)}, u32[]{:S(2)}, u32[]{:S(2)}) async-start(bf16[8,2,16,1664]{3,2,1,0:T(8,128)(2,1)} %get-tuple-element.114), calls=%async_computation | async-start | bytes 1703936 | tf_op jit(solution)/shard_map/all_to_all | solution.py:632
  71.4 6.0 %inside.1._.intra = f32[2,256,1536]{2,1,0:T(8,128)} custom-call(bf16[2,256,1792]{2,1,0:T(8,128)(2,1)} %get-tuple-element.115.act, f32[2,256,128]{2,1,0:T(8,128)} %get-tuple-element.116.step, f32[2,256,128]{2,1,0:T(8,128)} %get-tuple-element.117.cum), custom_call_target="tpu_custom_call" | custom-call | flops 8000000000 | bytes 5000000 | tf_op jit(solution)/shard_map/inside/pallas_call | solution.py:652
  77.4 19.1 %all-to-all-done.p.g = bf16[8,2,16,1664]{3,2,1,0:T(8,128)(2,1)S(1)} async-done(((bf16[8,2,16,1664]{3,2,1,0:T(8,128)(2,1)}), bf16[8,2,16,1664]{3,2,1,0:T(8,128)(2,1)S(1)}, u32[]{:S(2)}, u32[]{:S(2)}) %all-to-all-start) | async-done | bytes 852000 | tf_op jit(solution)/shard_map/all_to_all | solution.py:632
  96.5 0.9 copy-done.13
  97.4 2.5 pass.2
  99.9 3.7 %all-to-all-start.1 = ((bf16[8,2,16,1536]{3,2,1,0:T(8,128)(2,1)}), bf16[8,2,16,1536]{3,2,1,0:T(8,128)(2,1)S(1)}, u32[]{:S(2)}, u32[]{:S(2)}) async-start(bf16[8,2,16,1536]{3,2,1,0:T(8,128)(2,1)} %pass.2), calls=%async_computation.1 | async-start | bytes 1572864 | tf_op jit(solution)/shard_map/all_to_all | solution.py:632
  103.7 3.4 %slice.129 = bf16[32,48,768]{2,1,0:T(8,128)(2,1)} slice(bf16[32,96,768]{2,1,0:T(8,128)(2,1)} %bitcast.114), slice={[0:32], [48:96], [0:768]} | slice | bytes 4718592 | tf_op jit(solution)/shard_map/slice | solution.py:599
  107.1 1.5 fusion.9
  108.6 6.6 %gates.1 = (bf16[2,256,1536]{2,1,0:T(8,128)(2,1)}, f32[2,256,1536]{2,1,0:T(8,128)}) custom-call(bf16[2,256,768]{2,1,0:T(8,128)(2,1)} %get-tuple-element.118.hid, bf16[2,256,768]{2,1,0:T(8,128)(2,1)} %bitcast.108, bf16[768,768]{1,0:T(8,128)(2,1)} %bitcast.118, bf16[768,768]{1,0:T(8,128)(2,1)} %bitcast.116, bf16[1536,768]{1,0:T(8,128)(2,1)} %bitcast.112), custom_call_target="tpu_custom_call" | custom-call | flops 4000000000 | bytes 10000000 | tf_op jit(solution)/shard_map/gates/pallas_call | solution.py:663
  115.2 8.7 %all-to-all-done.1.st = bf16[8,2,16,1536]{3,2,1,0:T(8,128)(2,1)S(1)} async-done(((bf16[8,2,16,1536]{3,2,1,0:T(8,128)(2,1)}), bf16[8,2,16,1536]{3,2,1,0:T(8,128)(2,1)S(1)}, u32[]{:S(2)}, u32[]{:S(2)}) %all-to-all-start.1) | async-done | bytes 786464 | tf_op jit(solution)/shard_map/all_to_all | solution.py:632
  124.8 16.5 %middle.1 = (bf16[2,256,1536]{2,1,0:T(8,128)(2,1)}, bf16[2,256,1536]{2,1,0:T(8,128)(2,1)}, bf16[2,256,1536]{2,1,0:T(8,128)(2,1)}, f32[2,256,128]{2,1,0:T(8,128)}...) custom-call(bf16[8,2,16,1536]{3,2,1,0:T(8,128)(2,1)} %copy-done.15, ...), custom_call_target="tpu_custom_call" | custom-call | flops 4000000000 | bytes 15000000 | tf_op jit(solution)/shard_map/middle/pallas_call | solution.py:677
  141.3 3.6 %all-to-all-start.2 = ((bf16[8,2,16,1536]{3,2,1,0:T(8,128)(2,1)}), bf16[8,2,16,1536]{3,2,1,0:T(8,128)(2,1)S(1)}, u32[]{:S(2)}, u32[]{:S(2)}) async-start(bf16[8,2,16,1536]{3,2,1,0:T(8,128)(2,1)} %get-tuple-element.123), calls=%async_computation.2 | async-start | bytes 1572864 | tf_op jit(solution)/shard_map/all_to_all | solution.py:632
  144.9 8.2 %outer.1 = (f32[2,192,3072]{2,1,0:T(8,128)}, bf16[2,192,3072]{2,1,0:T(8,128)(2,1)}) custom-call(s32[1]{0:T(128)} %bitcast.1.core_ref, bf16[2,256,768]{2,1,0:T(8,128)(2,1)} %bitcast.109, bf16[2,256,768]{2,1,0:T(8,128)(2,1)} %get-tuple-element.118.hid, bf16[2,256,1536]{2,1,0:T(8,128)(2,1)} %get-tuple-element.122.normed, ...), custom_call_target="tpu_custom_call" | custom-call | flops 6000000000 | bytes 20000000 | tf_op jit(solution)/shard_map/outer/pallas_call | solution.py:695
  153.1 4.4 %slope.1._.dh = f32[2,256,768]{2,1,0:T(8,128)} custom-call(bf16[2,256,1536]{2,1,0:T(8,128)(2,1)} %get-tuple-element.124.dgate, bf16[768,768]{1,0:T(8,128)(2,1)} %bitcast.119, bf16[768,768]{1,0:T(8,128)(2,1)} %bitcast.117), custom_call_target="tpu_custom_call" | custom-call | flops 1200000000 | bytes 6000000 | tf_op jit(solution)/shard_map/slope/pallas_call | solution.py:718
  157.5 7.8 %all-to-all-done.2.p = bf16[8,2,16,1536]{3,2,1,0:T(8,128)(2,1)S(1)} async-done(((bf16[8,2,16,1536]{3,2,1,0:T(8,128)(2,1)}), bf16[8,2,16,1536]{3,2,1,0:T(8,128)(2,1)S(1)}, u32[]{:S(2)}, u32[]{:S(2)}) %all-to-all-start.2) | async-done | bytes 786464 | tf_op jit(solution)/shard_map/all_to_all | solution.py:632
  166.2 2.5 pass.3._
  168.6 3.8 %all-to-all-start.3 = ((bf16[8,2,16,1536]{3,2,1,0:T(8,128)(2,1)}), bf16[8,2,16,1536]{3,2,1,0:T(8,128)(2,1)S(1)}, u32[]{:S(2)}, u32[]{:S(2)}) async-start(bf16[8,2,16,1536]{3,2,1,0:T(8,128)(2,1)} %pass.3._), calls=%async_computation.3 | async-start | bytes 1572864 | tf_op jit(solution)/shard_map/all_to_all | solution.py:632
  172.4 9.8 %pair.1 = (f32[2,256,1536]{2,1,0:T(8,128)}, f32[2,256,128]{2,1,0:T(8,128)}, f32[2,256,128]{2,1,0:T(8,128)}) custom-call(bf16[2,256,1792]{2,1,0:T(8,128)(2,1)} %get-tuple-element.115.act, f32[2,256,128]{2,1,0:T(8,128)} %get-tuple-element.116.step, f32[2,256,128]{2,1,0:T(8,128)} %get-tuple-element.117.cum, bf16[2,256,1536]{2,1,0:T(8,128)(2,1)} %get-tuple-element.127.dy, ...), custom_call_target="tpu_custom_call" | custom-call | flops 16000000000 | bytes 10000000 | tf_op jit(solution)/shard_map/pair/pallas_call | solution.py:707
  182.2 4.4 %result.1.__ = bf16[2,256,768]{2,1,0:T(8,128)(2,1)} custom-call(bf16[2,256,768]{2,1,0:T(8,128)(2,1)} %bitcast.103, bf16[2,256,1536]{2,1,0:T(8,128)(2,1)} %get-tuple-element.122.normed, bf16[1536,768]{1,0:T(8,128)(2,1)} %bitcast.113, bf16[8,2,16,1536]{3,2,1,0:T(8,128)(2,1)} %pass.3._), custom_call_target="tpu_custom_call" | custom-call | flops 1200000000 | bytes 6000000 | tf_op jit(solution)/shard_map/result/pallas_call | solution.py:729
  186.6 6.0 %all-to-all-done.3.later = bf16[8,2,16,1536]{3,2,1,0:T(8,128)(2,1)S(1)} async-done(((bf16[8,2,16,1536]{3,2,1,0:T(8,128)(2,1)}), bf16[8,2,16,1536]{3,2,1,0:T(8,128)(2,1)S(1)}, u32[]{:S(2)}, u32[]{:S(2)}) %all-to-all-start.3) | async-done | bytes 786464 | tf_op jit(solution)/shard_map/all_to_all | solution.py:632
  192.5 0.9 copy-done.16
  193.4 12.3 %back.1 = (f32[2,256,1792]{2,1,0:T(8,128)}, f32[2,8,1792]{2,1,0:T(8,128)}, f32[2,256,128]{2,1,0:T(8,128)}, f32[2,8,128]{2,1,0:T(8,128)}) custom-call(bf16[8,2,16,1536]{3,2,1,0:T(8,128)(2,1)} %copy-done.16, bf16[8,2,16,1536]{3,2,1,0:T(8,128)(2,1)} %copy-done.15, bf16[2,256,1792]{2,1,0:T(8,128)(2,1)} %get-tuple-element.115.act, ...), custom_call_target="tpu_custom_call" | custom-call | flops 4000000000 | bytes 15000000 | tf_op jit(solution)/shard_map/back/pallas_call | solution.py:741
  205.7 1.6 collective-permute-start.17
  207.3 4.3 %taps.1.gone = f32[8,1792]{1,0:T(8,128)} custom-call(f32[2,256,1792]{2,1,0:T(8,128)} %get-tuple-element.134.dpre, bf16[2,272,1792]{2,1,0:T(8,128)(2,1)} %get-tuple-element.137.conv, f32[2,16,1536]{2,1,0:T(8,128)} %get-tuple-element.138.sums, f32[2,8,128]{2,1,0:T(8,128)} %get-tuple-element.139.hsum), custom_call_target="tpu_custom_call" | custom-call | flops 20000000 | bytes 6000000 | tf_op jit(solution)/shard_map/taps/pallas_call | solution.py:760
  211.7 1.0 collective-permute-done.17.edge
  213.5 5.4 %input.1 = (bf16[2,256,1920]{2,1,0:T(8,128)(2,1)S(1)}, f32[8,1792]{1,0:T(8,128)S(1)}, f32[2,192,640]{2,1,0:T(8,128)S(1)}, f32[2,192,640]{2,1,0:T(8,128)S(1)}, f3...) custom-call(s32[1]{0:T(128)} %bitcast.1.core_ref, ...), custom_call_target="tpu_custom_call" | custom-call | flops 2000000000 | bytes 10000000 | tf_op jit(solution)/shard_map/input/pallas_call | solution.py:772
  220.0 2.3 collective-permute-done.18.other
  222.3 3.1 %join.4 = (f32[2,2,2,24,1664]{4,3,2,1,0:T(8,128)S(1)}, f32[2,2,2,24,1664]{4,3,2,1,0:T(8,128)S(1)}, f32[2,2,2,24,1664]{4,3,2,1,0:T(8,128)S(1)}, bf16[2,2,2,24,166...) custom-call(s32[3]{0:T(128)S(1)} %pad_add_fusion.bit_ref, ...), custom_call_target="tpu_custom_call" | custom-call | flops 1000000 | bytes 8000000 | tf_op jit(solution)/shard_map/join/pallas_call | solution.py:798
  225.4 2.4 collective-permute-start.23
  227.8 1.5 collective-permute-start.24
  229.7 1.9 collective-permute-start.22
  231.7 6.0 %token_.1._ = bf16[2,256,768]{2,1,0:T(8,128)(2,1)} custom-call(bf16[2,256,768]{2,1,0:T(8,128)(2,1)S(1)} %bitcast.104, bf16[2,256,768]{2,1,0:T(8,128)(2,1)S(1)} %bitcast.110, f32[2,256,768]{2,1,0:T(8,128)S(1)} %copy-done.4, bf16[2,256,1920]{2,1,0:T(8,128)(2,1)S(1)} %get-tuple-element.140.dproj, bf16[768,1920]{1,0:T(8,128)(2,1)S(1)} %copy-done.11, ...), custom_call_target="tpu_custom_call" | custom-call | flops 4000000000 | bytes 15000000 | tf_op jit(solution)/shard_map/token/pallas_call | solution.py:812
  237.6 6.1 %collective-permute-done.22.other = f32[8,1792]{1,0:T(8,128)S(1)} collective-permute-done((f32[8,1792]{1,0:T(8,128)S(1)}, f32[8,1792]{1,0:T(8,128)S(1)}, u32[]{:S(2)}, u32[]{:S(2)}) %collective-permute-start.22) | collective-permute-done | bytes 57376 | tf_op jit(solution)/shard_map/ppermute | solution.py:536
  243.9 1.3 collective-permute-done.25.refs_5_
  245.2 1.1 copy-done.2
  246.3 0.9 join.5
  247.8 1.5 collective-permute-start.28
  250.1 1.5 collective-permute-start.26
  251.7 5.0 %collective-permute-done.26.other = f32[8,1792]{1,0:T(8,128)S(1)} collective-permute-done((f32[8,1792]{1,0:T(8,128)S(1)}, f32[8,1792]{1,0:T(8,128)S(1)}, u32[]{:S(2)}, u32[]{:S(2)}) %collective-permute-start.26) | collective-permute-done | bytes 57376 | tf_op jit(solution)/shard_map/ppermute | solution.py:536
  258.8 1.4 collective-permute-start.32
  260.8 1.2 collective-permute-start.30
  262.0 3.0 %collective-permute-done.30.other = f32[8,1792]{1,0:T(8,128)S(1)} collective-permute-done((f32[8,1792]{1,0:T(8,128)S(1)}, f32[8,1792]{1,0:T(8,128)S(1)}, u32[]{:S(2)}, u32[]{:S(2)}) %collective-permute-start.30) | collective-permute-done | bytes 57376 | tf_op jit(solution)/shard_map/ppermute | solution.py:536
  266.2 2.9 %collective-permute-start.36 = (bf16[24,1664]{1,0:T(8,128)(2,1)S(1)}, bf16[24,1664]{1,0:T(8,128)(2,1)S(1)}, u32[]{:S(2)}, u32[]{:S(2)}) collective-permute-start(bf16[24,1664]{1,0:T(8,128)(2,1)S(1)} %get-tuple-element.175), channel_id=1, source_target_pairs={{0,4},{1,5},{2,6},{3,7},{4,0},{5,1},{6,2},{7,3},{8,12},{9,13},{10,... | collective-permute-start | bytes 239624 | tf_op jit(solution)/shard_map/ppermute | solution.py:536
  269.2 2.8 collective-permute-start.34
  272.1 6.4 %collective-permute-done.34.other = f32[8,1792]{1,0:T(8,128)S(1)} collective-permute-done((f32[8,1792]{1,0:T(8,128)S(1)}, f32[8,1792]{1,0:T(8,128)S(1)}, u32[]{:S(2)}, u32[]{:S(2)}) %collective-permute-start.34) | collective-permute-done | bytes 57376 | tf_op jit(solution)/shard_map/ppermute | solution.py:536
  (157 shorter events, 24.4 us)
Async XLA Ops:
  7.2 96.5 %all-gather.3.cloned.1.call-start = ((), (), s32[]{:S(2)}) async-start(), calls=%async_computation.4 | async-start | bytes 4866048 | tf_op jit(solution)/shard_map/all_gather | solution.py:596
  10.4 17.6 %collective-permute-start = (bf16[2,16,768]{2,1,0:T(8,128)(2,1)S(1)}, bf16[2,16,768]{2,1,0:T(8,128)(2,1)S(1)}, u32[]{:S(2)}, u32[]{:S(2)}) collective-permute-start(bf16[2,16,768]{2,1,0:T(8,128)(2,1)S(1)} %slice.124), channel_id=1, source_target_pairs={{0,1},{1,2},{2,3},{3,4},{4,5},{5,6},{6,7},{8,9},{9,10},{10,11},{11... | collective-permute-start | bytes 147464 | tf_op jit(solution)/shard_map/ppermute | solution.py:570
  16.0 5.3 %collective-permute-start.5 = (bf16[24,640]{1,0:T(8,128)(2,1)S(1)}, bf16[24,640]{1,0:T(8,128)(2,1)S(1)}, u32[]{:S(2)}, u32[]{:S(2)}) collective-permute-start(bf16[24,640]{1,0:T(8,128)(2,1)S(1)} %slice.111), channel_id=1, source_target_pairs={{0,4},{1,5},{2,6},{3,7},{4,0},{5,1},{6,2},{7,3},{8,12},{9,13},{10,... | collective-permute-start | bytes 92168 | tf_op jit(solution)/shard_map/ppermute | solution.py:536
  21.0 5.4 %collective-permute-start.9 = (bf16[24,640]{1,0:T(8,128)(2,1)S(1)}, bf16[24,640]{1,0:T(8,128)(2,1)S(1)}, u32[]{:S(2)}, u32[]{:S(2)}) collective-permute-start(bf16[24,640]{1,0:T(8,128)(2,1)S(1)} %fusion.1), channel_id=1, source_target_pairs={{0,4},{1,5},{2,6},{3,7},{4,0},{5,1},{6,2},{7,3},{8,12},{9,13},{10,... | collective-permute-start | bytes 92168 | tf_op jit(solution)/shard_map/ppermute | solution.py:536
  22.1 5.9 %collective-permute-start.1 = (bf16[24,640]{1,0:T(8,128)(2,1)S(1)}, bf16[24,640]{1,0:T(8,128)(2,1)S(1)}, u32[]{:S(2)}, u32[]{:S(2)}) collective-permute-start(bf16[24,640]{1,0:T(8,128)(2,1)S(1)} %get-tuple-element.223), channel_id=1, source_target_pairs={{0,4},{1,5},{2,6},{3,7},{4,0},{5,1},{6,2},{7,3},{8,12},{9,13},{10,... | collective-permute-start | bytes 92168 | tf_op jit(solution)/shard_map/ppermute | solution.py:536
  24.8 5.3 %collective-permute-start.6 = (bf16[2,24,640]{2,1,0:T(8,128)(2,1)S(1)}, bf16[2,24,640]{2,1,0:T(8,128)(2,1)S(1)}, u32[]{:S(2)}, u32[]{:S(2)}) collective-permute-start(bf16[2,24,640]{2,1,0:T(8,128)(2,1)S(1)} %pad_maximum_fusion.10), channel_id=1, source_target_pairs={{0,1},{1,0},{2,3},{3,2},{4,5},{5,4},{6,7},{7,6},{8,9},{9,8},{10,11... | collective-permute-start | bytes 184328 | tf_op jit(solution)/shard_map/ppermute | solution.py:536
  26.4 4.6 %collective-permute-start.10 = (bf16[2,24,640]{2,1,0:T(8,128)(2,1)S(1)}, bf16[2,24,640]{2,1,0:T(8,128)(2,1)S(1)}, u32[]{:S(2)}, u32[]{:S(2)}) collective-permute-start(bf16[2,24,640]{2,1,0:T(8,128)(2,1)S(1)} %pad_maximum_fusion.11), channel_id=1, source_target_pairs={{0,16},{1,17},{2,18},{3,19},{4,20},{5,21},{6,22},{7,23},{8,24},{9,... | collective-permute-start | bytes 184328 | tf_op jit(solution)/shard_map/ppermute | solution.py:536
  28.0 11.9 %copy-start.22 = (bf16[2,16,768]{2,1,0:T(8,128)(2,1)}, bf16[2,16,768]{2,1,0:T(8,128)(2,1)S(1)}, u32[]{:S(2)}) copy-start(bf16[2,16,768]{2,1,0:T(8,128)(2,1)S(1)} %collective-permute-done.halo) | copy-start | bytes 147460
  28.8 4.8 %collective-permute-start.2 = (bf16[2,24,640]{2,1,0:T(8,128)(2,1)S(1)}, bf16[2,24,640]{2,1,0:T(8,128)(2,1)S(1)}, u32[]{:S(2)}, u32[]{:S(2)}) collective-permute-start(bf16[2,24,640]{2,1,0:T(8,128)(2,1)S(1)} %pad_maximum_fusion.9), channel_id=1, source_target_pairs={{0,2},{1,3},{2,0},{3,1},{4,6},{5,7},{6,4},{7,5},{8,10},{9,11},{10,... | collective-permute-start | bytes 184328 | tf_op jit(solution)/shard_map/ppermute | solution.py:536
  30.1 5.7 %collective-permute-start.7 = (bf16[2,2,24,640]{3,2,0,1:T(8,128)(2,1)S(1)}, bf16[2,2,24,640]{3,2,0,1:T(8,128)(2,1)S(1)}, u32[]{:S(2)}, u32[]{:S(2)}) collective-permute-start(bf16[2,2,24,640]{3,2,0,1:T(8,128)(2,1)S(1)} %pad_maximum_fusion.7), channel_id=1, source_target_pairs={{0,2},{1,3},{2,0},{3,1},{4,6},{5,7},{6,4},{7,5},{8,10},{9,11},{10,... | collective-permute-start | bytes 368648 | tf_op jit(solution)/shard_map/ppermute | solution.py:536
  31.1 6.1 %collective-permute-start.11 = (bf16[2,2,24,640]{3,2,1,0:T(8,128)(2,1)S(1)}, bf16[2,2,24,640]{3,2,1,0:T(8,128)(2,1)S(1)}, u32[]{:S(2)}, u32[]{:S(2)}) collective-permute-start(bf16[2,2,24,640]{3,2,1,0:T(8,128)(2,1)S(1)} %pad_maximum_fusion.8), channel_id=1, source_target_pairs={{0,1},{1,0},{2,3},{3,2},{4,5},{5,4},{6,7},{7,6},{8,9},{9,8},{10,11... | collective-permute-start | bytes 368648 | tf_op jit(solution)/shard_map/ppermute | solution.py:536
  33.6 6.2 %collective-permute-start.3 = (bf16[2,2,24,640]{3,2,0,1:T(8,128)(2,1)S(1)}, bf16[2,2,24,640]{3,2,0,1:T(8,128)(2,1)S(1)}, u32[]{:S(2)}, u32[]{:S(2)}) collective-permute-start(bf16[2,2,24,640]{3,2,0,1:T(8,128)(2,1)S(1)} %maximum_add_fusion), channel_id=1, source_target_pairs={{0,16},{1,17},{2,18},{3,19},{4,20},{5,21},{6,22},{7,23},{8,24},{9,... | collective-permute-start | bytes 368648 | tf_op jit(solution)/shard_map/ppermute | solution.py:536
  35.8 8.0 %collective-permute-start.8 = (bf16[2,2,2,24,640]{4,3,0,2,1:T(8,128)(2,1)S(1)}, bf16[2,2,2,24,640]{4,3,0,2,1:T(8,128)(2,1)S(1)}, u32[]{:S(2)}, u32[]{:S(2)}) collective-permute-start(bf16[2,2,2,24,640]{4,3,0,2,1:T(8,128)(2,1)S(1)} %pad_maximum_fusion.4), channel_id=1, source_target_pairs={{0,16},{1,17},{2,18},{3,19},{4,20},{5,21},{6,22},{7,23},{8,24},{9,... | collective-permute-start | bytes 737288 | tf_op jit(solution)/shard_map/ppermute | solution.py:536
  37.3 8.4 %collective-permute-start.12 = (bf16[2,2,2,24,640]{4,3,1,0,2:T(8,128)(2,1)S(1)}, bf16[2,2,2,24,640]{4,3,1,0,2:T(8,128)(2,1)S(1)}, u32[]{:S(2)}, u32[]{:S(2)}) collective-permute-start(bf16[2,2,2,24,640]{4,3,1,0,2:T(8,128)(2,1)S(1)} %pad_maximum_fusion.5), channel_id=1, source_target_pairs={{0,2},{1,3},{2,0},{3,1},{4,6},{5,7},{6,4},{7,5},{8,10},{9,11},{10,... | collective-permute-start | bytes 737288 | tf_op jit(solution)/shard_map/ppermute | solution.py:536
  39.9 9.2 %collective-permute-start.4 = (bf16[2,2,2,24,640]{4,3,1,2,0:T(8,128)(2,1)S(1)}, bf16[2,2,2,24,640]{4,3,1,2,0:T(8,128)(2,1)S(1)}, u32[]{:S(2)}, u32[]{:S(2)}) collective-permute-start(bf16[2,2,2,24,640]{4,3,1,2,0:T(8,128)(2,1)S(1)} %pad_maximum_fusion.3), channel_id=1, source_target_pairs={{0,1},{1,0},{2,3},{3,2},{4,5},{5,4},{6,7},{7,6},{8,9},{9,8},{10,11... | collective-permute-start | bytes 737288 | tf_op jit(solution)/shard_map/ppermute | solution.py:536
  45.8 3.5 %copy-start.18 = (bf16[2,2,2,2,24,640]{5,4,3,2,1,0:T(8,128)(2,1)}, bf16[2,2,2,2,24,640]{5,4,3,2,1,0:T(8,128)(2,1)S(1)}, u32[]{:S(2)}) copy-start(bf16[2,2,2,2,24,640]{5,4,3,2,1,0:T(8,128)(2,1)S(1)} %copy.32) | copy-start | bytes 1474564
  45.8 3.6 %copy-start.24 = (f32[24]{0:T(128)S(1)}, f32[24]{0:T(128)}, u32[]{:S(2)}) copy-start(f32[24]{0:T(128)} %param.23) | copy-start | bytes 292
  45.8 3.6 %copy-start.25 = (f32[24]{0:T(128)S(1)}, f32[24]{0:T(128)}, u32[]{:S(2)}) copy-start(f32[24]{0:T(128)} %param.24) | copy-start | bytes 292
  45.8 3.8 %copy-start.26 = (f32[24]{0:T(128)S(1)}, f32[24]{0:T(128)}, u32[]{:S(2)}) copy-start(f32[24]{0:T(128)} %param.25) | copy-start | bytes 292
  45.9 5.3 %copy-start.19 = (bf16[2,192,640]{2,1,0:T(8,128)(2,1)}, bf16[2,192,640]{2,1,0:T(8,128)(2,1)S(1)}, u32[]{:S(2)}) copy-start(bf16[2,192,640]{2,1,0:T(8,128)(2,1)S(1)} %pad_maximum_fusion.1.refs_1_) | copy-start | bytes 1474564
  45.9 3.9 %collective-permute-start.14 = (bf16[2,192,640]{2,1,0:T(8,128)(2,1)S(1)}, bf16[2,192,640]{2,1,0:T(8,128)(2,1)S(1)}, u32[]{:S(2)}, u32[]{:S(2)}) collective-permute-start(bf16[2,192,640]{2,1,0:T(8,128)(2,1)S(1)} %pad_maximum_fusion.1.refs_1_), channel_id=1, source_target_pairs={{0,8},{1,9},{2,10},{3,11},{4,12},{5,13},{6,14},{7,15},{8,0},{9,1},... | collective-permute-start | bytes 1474568 | tf_op jit(solution)/shard_map/ppermute | solution.py:536
  46.0 3.9 %collective-permute-start.15 = (bf16[2,192,640]{2,1,0:T(8,128)(2,1)S(1)}, bf16[2,192,640]{2,1,0:T(8,128)(2,1)S(1)}, u32[]{:S(2)}, u32[]{:S(2)}) collective-permute-start(bf16[2,192,640]{2,1,0:T(8,128)(2,1)S(1)} %bitcast.123), channel_id=1, source_target_pairs={{0,8},{1,9},{2,10},{3,11},{4,12},{5,13},{6,14},{7,15},{8,0},{9,1},... | collective-permute-start | bytes 1474568 | tf_op jit(solution)/shard_map/ppermute | solution.py:536
  49.3 1.9 copy-start.20
  49.3 1.9 collective-permute-start.13
  49.8 1.4 copy-start.21
  66.7 29.8 %all-to-all-start = ((bf16[8,2,16,1664]{3,2,1,0:T(8,128)(2,1)}), bf16[8,2,16,1664]{3,2,1,0:T(8,128)(2,1)S(1)}, u32[]{:S(2)}, u32[]{:S(2)}) async-start(bf16[8,2,16,1664]{3,2,1,0:T(8,128)(2,1)} %get-tuple-element.114), calls=%async_computation | async-start | bytes 1703936 | tf_op jit(solution)/shard_map/all_to_all | solution.py:632
  99.9 24.0 %all-to-all-start.1 = ((bf16[8,2,16,1536]{3,2,1,0:T(8,128)(2,1)}), bf16[8,2,16,1536]{3,2,1,0:T(8,128)(2,1)S(1)}, u32[]{:S(2)}, u32[]{:S(2)}) async-start(bf16[8,2,16,1536]{3,2,1,0:T(8,128)(2,1)} %pass.2), calls=%async_computation.1 | async-start | bytes 1572864 | tf_op jit(solution)/shard_map/all_to_all | solution.py:632
  103.6 3.4 %copy-start.14 = (bf16[3072,768]{1,0:T(8,128)(2,1)S(1)}, bf16[3072,768]{1,0:T(8,128)(2,1)}, u32[]{:S(2)}) copy-start(bf16[3072,768]{1,0:T(8,128)(2,1)} %all-gather.3.cloned.1.call-done) | copy-start | bytes 14155780
  141.3 24.0 %all-to-all-start.2 = ((bf16[8,2,16,1536]{3,2,1,0:T(8,128)(2,1)}), bf16[8,2,16,1536]{3,2,1,0:T(8,128)(2,1)S(1)}, u32[]{:S(2)}, u32[]{:S(2)}) async-start(bf16[8,2,16,1536]{3,2,1,0:T(8,128)(2,1)} %get-tuple-element.123), calls=%async_computation.2 | async-start | bytes 1572864 | tf_op jit(solution)/shard_map/all_to_all | solution.py:632
  153.1 33.4 %collective-permute-start.16 = (bf16[2,192,3072]{2,1,0:T(8,128)(2,1)}, bf16[2,192,3072]{2,1,0:T(8,128)(2,1)S(1)}, u32[]{:S(2)}, u32[]{:S(2)}) collective-permute-start(bf16[2,192,3072]{2,1,0:T(8,128)(2,1)} %get-tuple-element.133), channel_id=1, source_target_pairs={{0,8},{1,9},{2,10},{3,11},{4,12},{5,13},{6,14},{7,15},{8,0},{9,1},... | collective-permute-start | bytes 7077896 | tf_op jit(solution)/shard_map/ppermute | solution.py:536
  168.6 23.9 %all-to-all-start.3 = ((bf16[8,2,16,1536]{3,2,1,0:T(8,128)(2,1)}), bf16[8,2,16,1536]{3,2,1,0:T(8,128)(2,1)S(1)}, u32[]{:S(2)}, u32[]{:S(2)}) async-start(bf16[8,2,16,1536]{3,2,1,0:T(8,128)(2,1)} %pass.3._), calls=%async_computation.3 | async-start | bytes 1572864 | tf_op jit(solution)/shard_map/all_to_all | solution.py:632
  186.5 6.0 %copy-start = (bf16[2,192,3072]{2,1,0:T(8,128)(2,1)}, bf16[2,192,3072]{2,1,0:T(8,128)(2,1)S(1)}, u32[]{:S(2)}) copy-start(bf16[2,192,3072]{2,1,0:T(8,128)(2,1)S(1)} %collective-permute-done.16.___) | copy-start | bytes 7077892
  205.7 6.9 %collective-permute-start.17 = (f32[2,8,1792]{2,1,0:T(8,128)}, f32[2,8,1792]{2,1,0:T(8,128)S(1)}, u32[]{:S(2)}, u32[]{:S(2)}) collective-permute-start(f32[2,8,1792]{2,1,0:T(8,128)} %get-tuple-element.135), channel_id=1, source_target_pairs={{1,0},{2,1},{3,2},{4,3},{5,4},{6,5},{7,6},{9,8},{10,9},{11,10},{12... | collective-permute-start | bytes 344072 | tf_op jit(solution)/shard_map/ppermute | solution.py:758
  207.3 5.3 %copy-start.9 = (f32[2,256,128]{2,1,0:T(8,128)S(1)}, f32[2,256,128]{2,1,0:T(8,128)}, u32[]{:S(2)}) copy-start(f32[2,256,128]{2,1,0:T(8,128)} %get-tuple-element.136.draw) | copy-start | bytes 786436
  207.3 5.3 %copy-start.10 = (bf16[2,256,768]{2,1,0:T(8,128)(2,1)S(1)}, bf16[2,256,768]{2,1,0:T(8,128)(2,1)}, u32[]{:S(2)}) copy-start(bf16[2,256,768]{2,1,0:T(8,128)(2,1)} %get-tuple-element.118.hid) | copy-start | bytes 2359300
  207.3 5.3 %copy-start.12 = (f32[8,1792]{1,0:T(8,128)S(1)}, f32[8,1792]{1,0:T(8,128)}, u32[]{:S(2)}) copy-start(f32[8,1792]{1,0:T(8,128)} %get-tuple-element.121.par) | copy-start | bytes 172036
  213.4 8.8 %copy-start.1 = (bf16[2,192,3072]{2,1,0:T(8,128)(2,1)S(1)}, bf16[2,192,3072]{2,1,0:T(8,128)(2,1)}, u32[]{:S(2)}) copy-start(bf16[2,192,3072]{2,1,0:T(8,128)(2,1)} %copy-done) | copy-start | bytes 7077892
  218.8 3.4 %collective-permute-start.19 = (bf16[2,192,640]{2,1,0:T(8,128)(2,1)S(1)}, bf16[2,192,640]{2,1,0:T(8,128)(2,1)S(1)}, u32[]{:S(2)}, u32[]{:S(2)}) collective-permute-start(bf16[2,192,640]{2,1,0:T(8,128)(2,1)S(1)} %get-tuple-element.146), channel_id=1, source_target_pairs={{0,8},{1,9},{2,10},{3,11},{4,12},{5,13},{6,14},{7,15},{8,0},{9,1},... | collective-permute-start | bytes 1474568 | tf_op jit(solution)/shard_map/ppermute | solution.py:536
  218.9 3.3 %collective-permute-start.20 = (bf16[2,192,640]{2,1,0:T(8,128)(2,1)S(1)}, bf16[2,192,640]{2,1,0:T(8,128)(2,1)S(1)}, u32[]{:S(2)}, u32[]{:S(2)}) collective-permute-start(bf16[2,192,640]{2,1,0:T(8,128)(2,1)S(1)} %get-tuple-element.147), channel_id=1, source_target_pairs={{0,8},{1,9},{2,10},{3,11},{4,12},{5,13},{6,14},{7,15},{8,0},{9,1},... | collective-permute-start | bytes 1474568 | tf_op jit(solution)/shard_map/ppermute | solution.py:536
  219.4 2.9 collective-permute-start.21
  219.5 2.8 collective-permute-start.18
  222.3 9.4 %copy-start.4 = (f32[2,256,768]{2,1,0:T(8,128)S(1)}, f32[2,256,768]{2,1,0:T(8,128)}, u32[]{:S(2)}) copy-start(f32[2,256,768]{2,1,0:T(8,128)} %slope.1._.dh) | copy-start | bytes 4718596
  222.3 9.4 %copy-start.6 = (bf16[2,1,256,768]{3,2,1,0:T(8,128)(2,1)S(1)}, bf16[2,1,256,768]{3,2,1,0:T(8,128)(2,1)}, u32[]{:S(2)}) copy-start(bf16[2,1,256,768]{3,2,1,0:T(8,128)(2,1)} %param.17) | copy-start | bytes 2359300
  222.3 9.4 %copy-start.8 = (bf16[2,1,256,768]{3,2,1,0:T(8,128)(2,1)S(1)}, bf16[2,1,256,768]{3,2,1,0:T(8,128)(2,1)}, u32[]{:S(2)}) copy-start(bf16[2,1,256,768]{3,2,1,0:T(8,128)(2,1)} %param.18) | copy-start | bytes 2359300
  222.3 9.4 %copy-start.11 = (bf16[768,1920]{1,0:T(8,128)(2,1)S(1)}, bf16[768,1920]{1,0:T(8,128)(2,1)}, u32[]{:S(2)}) copy-start(bf16[768,1920]{1,0:T(8,128)(2,1)} %get-tuple-element.141.weight) | copy-start | bytes 8847364
  225.4 18.3 %collective-permute-start.23 = (bf16[2,2,2,24,1664]{4,3,2,1,0:T(8,128)(2,1)S(1)}, bf16[2,2,2,24,1664]{4,3,2,1,0:T(8,128)(2,1)S(1)}, u32[]{:S(2)}, u32[]{:S(2)}) collective-permute-start(bf16[2,2,2,24,1664]{4,3,2,1,0:T(8,128)(2,1)S(1)} %get-tuple-element.153), channel_id=1, source_target_pairs={{0,1},{1,0},{2,3},{3,2},{4,5},{5,4},{6,7},{7,6},{8,9},{9,8},{10,11... | collective-permute-start | bytes 1916936 | tf_op jit(solution)/shard_map/ppermute | solution.py:536
  227.8 16.1 %collective-permute-start.24 = (bf16[2,2,2,24,1664]{4,3,2,1,0:T(8,128)(2,1)S(1)}, bf16[2,2,2,24,1664]{4,3,2,1,0:T(8,128)(2,1)S(1)}, u32[]{:S(2)}, u32[]{:S(2)}) collective-permute-start(bf16[2,2,2,24,1664]{4,3,2,1,0:T(8,128)(2,1)S(1)} %get-tuple-element.154), channel_id=1, source_target_pairs={{0,16},{1,17},{2,18},{3,19},{4,20},{5,21},{6,22},{7,23},{8,24},{9,... | collective-permute-start | bytes 1916936 | tf_op jit(solution)/shard_map/ppermute | solution.py:536
  229.3 15.9 %collective-permute-start.25 = (bf16[2,2,2,24,1664]{4,3,2,1,0:T(8,128)(2,1)S(1)}, bf16[2,2,2,24,1664]{4,3,2,1,0:T(8,128)(2,1)S(1)}, u32[]{:S(2)}, u32[]{:S(2)}) collective-permute-start(bf16[2,2,2,24,1664]{4,3,2,1,0:T(8,128)(2,1)S(1)} %get-tuple-element.155), channel_id=1, source_target_pairs={{0,2},{1,3},{2,0},{3,1},{4,6},{5,7},{6,4},{7,5},{8,10},{9,11},{10,... | collective-permute-start | bytes 1916936 | tf_op jit(solution)/shard_map/ppermute | solution.py:536
  229.7 14.0 %collective-permute-start.22 = (f32[8,1792]{1,0:T(8,128)S(1)}, f32[8,1792]{1,0:T(8,128)S(1)}, u32[]{:S(2)}, u32[]{:S(2)}) collective-permute-start(f32[8,1792]{1,0:T(8,128)S(1)} %get-tuple-element.149._.small), channel_id=1, source_target_pairs={{0,1},{1,0},{2,3},{3,2},{4,5},{5,4},{6,7},{7,6},{8,9},{9,8},{10,11... | collective-permute-start | bytes 172040 | tf_op jit(solution)/shard_map/ppermute | solution.py:536
  246.3 11.2 %copy-start.3 = (bf16[2,256,768]{2,1,0:T(8,128)(2,1)S(1)}, bf16[2,256,768]{2,1,0:T(8,128)(2,1)}, u32[]{:S(2)}) copy-start(bf16[2,256,768]{2,1,0:T(8,128)(2,1)} %token_.1._) | copy-start | bytes 2359300
  247.3 9.4 %collective-permute-start.27 = (bf16[2,2,24,1664]{3,2,1,0:T(8,128)(2,1)S(1)}, bf16[2,2,24,1664]{3,2,1,0:T(8,128)(2,1)S(1)}, u32[]{:S(2)}, u32[]{:S(2)}) collective-permute-start(bf16[2,2,24,1664]{3,2,1,0:T(8,128)(2,1)S(1)} %get-tuple-element.160), channel_id=1, source_target_pairs={{0,16},{1,17},{2,18},{3,19},{4,20},{5,21},{6,22},{7,23},{8,24},{9,... | collective-permute-start | bytes 958472 | tf_op jit(solution)/shard_map/ppermute | solution.py:536
  247.8 8.9 %collective-permute-start.28 = (bf16[2,2,24,1664]{3,2,1,0:T(8,128)(2,1)S(1)}, bf16[2,2,24,1664]{3,2,1,0:T(8,128)(2,1)S(1)}, u32[]{:S(2)}, u32[]{:S(2)}) collective-permute-start(bf16[2,2,24,1664]{3,2,1,0:T(8,128)(2,1)S(1)} %get-tuple-element.161), channel_id=1, source_target_pairs={{0,2},{1,3},{2,0},{3,1},{4,6},{5,7},{6,4},{7,5},{8,10},{9,11},{10,... | collective-permute-start | bytes 958472 | tf_op jit(solution)/shard_map/ppermute | solution.py:536
  249.4 8.2 %collective-permute-start.29 = (bf16[2,2,24,1664]{3,2,1,0:T(8,128)(2,1)S(1)}, bf16[2,2,24,1664]{3,2,1,0:T(8,128)(2,1)S(1)}, u32[]{:S(2)}, u32[]{:S(2)}) collective-permute-start(bf16[2,2,24,1664]{3,2,1,0:T(8,128)(2,1)S(1)} %get-tuple-element.162), channel_id=1, source_target_pairs={{0,1},{1,0},{2,3},{3,2},{4,5},{5,4},{6,7},{7,6},{8,9},{9,8},{10,11... | collective-permute-start | bytes 958472 | tf_op jit(solution)/shard_map/ppermute | solution.py:536
  250.1 6.6 %collective-permute-start.26 = (f32[8,1792]{1,0:T(8,128)S(1)}, f32[8,1792]{1,0:T(8,128)S(1)}, u32[]{:S(2)}, u32[]{:S(2)}) collective-permute-start(f32[8,1792]{1,0:T(8,128)S(1)} %get-tuple-element.156.small), channel_id=1, source_target_pairs={{0,16},{1,17},{2,18},{3,19},{4,20},{5,21},{6,22},{7,23},{8,24},{9,... | collective-permute-start | bytes 172040 | tf_op jit(solution)/shard_map/ppermute | solution.py:536
  258.3 13.7 %copy-start.23 = (bf16[24]{0:T(256)(128)(2,1)S(1)}, bf16[24]{0:T(256)(128)(2,1)}, u32[]{:S(2)}) copy-start(bf16[24]{0:T(256)(128)(2,1)} %param.19) | copy-start | bytes 148
  258.3 20.2 %copy-start.5 = (bf16[24,3352]{1,0:T(8,128)(2,1)S(1)}, bf16[24,3352]{1,0:T(8,128)(2,1)}, u32[]{:S(2)}) copy-start(bf16[24,3352]{1,0:T(8,128)(2,1)} %w_in.1) | copy-start | bytes 482692
  258.3 6.7 %collective-permute-start.31 = (bf16[2,24,1664]{2,1,0:T(8,128)(2,1)S(1)}, bf16[2,24,1664]{2,1,0:T(8,128)(2,1)S(1)}, u32[]{:S(2)}, u32[]{:S(2)}) collective-permute-start(bf16[2,24,1664]{2,1,0:T(8,128)(2,1)S(1)} %get-tuple-element.167), channel_id=1, source_target_pairs={{0,2},{1,3},{2,0},{3,1},{4,6},{5,7},{6,4},{7,5},{8,10},{9,11},{10,... | collective-permute-start | bytes 479240 | tf_op jit(solution)/shard_map/ppermute | solution.py:536
  258.8 6.2 %collective-permute-start.32 = (bf16[2,24,1664]{2,1,0:T(8,128)(2,1)S(1)}, bf16[2,24,1664]{2,1,0:T(8,128)(2,1)S(1)}, u32[]{:S(2)}, u32[]{:S(2)}) collective-permute-start(bf16[2,24,1664]{2,1,0:T(8,128)(2,1)S(1)} %get-tuple-element.168), channel_id=1, source_target_pairs={{0,1},{1,0},{2,3},{3,2},{4,5},{5,4},{6,7},{7,6},{8,9},{9,8},{10,11... | collective-permute-start | bytes 479240 | tf_op jit(solution)/shard_map/ppermute | solution.py:536
  260.2 5.3 %collective-permute-start.33 = (bf16[2,24,1664]{2,1,0:T(8,128)(2,1)S(1)}, bf16[2,24,1664]{2,1,0:T(8,128)(2,1)S(1)}, u32[]{:S(2)}, u32[]{:S(2)}) collective-permute-start(bf16[2,24,1664]{2,1,0:T(8,128)(2,1)S(1)} %get-tuple-element.169), channel_id=1, source_target_pairs={{0,16},{1,17},{2,18},{3,19},{4,20},{5,21},{6,22},{7,23},{8,24},{9,... | collective-permute-start | bytes 479240 | tf_op jit(solution)/shard_map/ppermute | solution.py:536
  260.8 4.2 %collective-permute-start.30 = (f32[8,1792]{1,0:T(8,128)S(1)}, f32[8,1792]{1,0:T(8,128)S(1)}, u32[]{:S(2)}, u32[]{:S(2)}) collective-permute-start(f32[8,1792]{1,0:T(8,128)S(1)} %get-tuple-element.163.small), channel_id=1, source_target_pairs={{0,2},{1,3},{2,0},{3,1},{4,6},{5,7},{6,4},{7,5},{8,10},{9,11},{10,... | collective-permute-start | bytes 172040 | tf_op jit(solution)/shard_map/ppermute | solution.py:536
  266.1 12.4 %collective-permute-start.35 = (bf16[24,1664]{1,0:T(8,128)(2,1)S(1)}, bf16[24,1664]{1,0:T(8,128)(2,1)S(1)}, u32[]{:S(2)}, u32[]{:S(2)}) collective-permute-start(bf16[24,1664]{1,0:T(8,128)(2,1)S(1)} %get-tuple-element.174), channel_id=1, source_target_pairs={{0,4},{1,5},{2,6},{3,7},{4,0},{5,1},{6,2},{7,3},{8,12},{9,13},{10,... | collective-permute-start | bytes 239624 | tf_op jit(solution)/shard_map/ppermute | solution.py:536
  266.2 12.3 %collective-permute-start.36 = (bf16[24,1664]{1,0:T(8,128)(2,1)S(1)}, bf16[24,1664]{1,0:T(8,128)(2,1)S(1)}, u32[]{:S(2)}, u32[]{:S(2)}) collective-permute-start(bf16[24,1664]{1,0:T(8,128)(2,1)S(1)} %get-tuple-element.175), channel_id=1, source_target_pairs={{0,4},{1,5},{2,6},{3,7},{4,0},{5,1},{6,2},{7,3},{8,12},{9,13},{10,... | collective-permute-start | bytes 239624 | tf_op jit(solution)/shard_map/ppermute | solution.py:536
  269.1 9.4 %collective-permute-start.37 = (bf16[24,1664]{1,0:T(8,128)(2,1)S(1)}, bf16[24,1664]{1,0:T(8,128)(2,1)S(1)}, u32[]{:S(2)}, u32[]{:S(2)}) collective-permute-start(bf16[24,1664]{1,0:T(8,128)(2,1)S(1)} %get-tuple-element.176), channel_id=1, source_target_pairs={{0,4},{1,5},{2,6},{3,7},{4,0},{5,1},{6,2},{7,3},{8,12},{9,13},{10,... | collective-permute-start | bytes 239624 | tf_op jit(solution)/shard_map/ppermute | solution.py:536
  269.2 9.3 %collective-permute-start.34 = (f32[8,1792]{1,0:T(8,128)S(1)}, f32[8,1792]{1,0:T(8,128)S(1)}, u32[]{:S(2)}, u32[]{:S(2)}) collective-permute-start(f32[8,1792]{1,0:T(8,128)S(1)} %get-tuple-element.170.small), channel_id=1, source_target_pairs={{0,4},{1,5},{2,6},{3,7},{4,0},{5,1},{6,2},{7,3},{8,12},{9,13},{10,... | collective-permute-start | bytes 172040 | tf_op jit(solution)/shard_map/ppermute | solution.py:536
  (9 other events, 9.1 us)
Sparse Core Ops, SparseCore 0:
  11.6 69.8 all-gather.2

commit v4 on v3

--- a/solution.py
+++ b/solution.py
@@ -280,7 +280,7 @@
         low_s[at, :] = low
         return carry
 
-    lax.fori_loop(0, PIECE // size, chunk, 0)
+    lax.fori_loop(0, PIECE // size, chunk, 0, unroll=True)
     d_state = dot_tn(cmat, doff_s[...]).astype(BF16)
     pay[:, 0] = d_state.reshape(NEAR, NB, DI)
     reach[0] = collect(high_s[...], low_s[...], spread)
@@ -422,7 +422,7 @@
         sum_s[0:8] += (xdt * through).reshape(rows // 8, 8, DI).sum(axis=0)
         return carry
 
-    lax.fori_loop(0, PIECE // rows, chunk, 0)
+    lax.fori_loop(0, PIECE // rows, chunk, 0, unroll=True)
     for j in range(NEAR):
         prod = later[j, 0].astype(F32) * st[j, 0].astype(F32)
         sum_s[8:16] += prod.reshape(NB // 8, 8, DI).sum(axis=0)
@@ -514,7 +514,7 @@
         grad[0, at, :] = (cot[0, at, :].astype(F32) + scale * (d_unit - unit * along)).astype(BF16)
         return carry
 
-    lax.fori_loop(0, PIECE // rows, chunk, 0)
+    lax.fori_loop(0, PIECE // rows, chunk, 0, unroll=True)
 
 
 def local(size, tokens, cotangent, norm_in, w_in, conv_w, conv_b, dt_bias, a_log, skip, norm_out, w_out):

time: 290 us -> 283 us (0.976)
  Pallas kernels: 110 us -> 100 us
    pallas_call x1, Pallas kernels: 16.5 us -> 11.4 us  [local(): pl.pallas_call(middle_kernel, grid=(R,), in_specs=[state_spec, row_c, row...]
where the time goes in v4:
time: 283 us; the launch traced here: 282 us
  Pallas kernels  100 us (35%)
  waiting for transfers between devices  82.9 us (29%)
  starting transfers between devices  60.8 us (21%)
  local copies, waits for them, and re-layouts  18.2 us (6%)
  between operations  14.7 us (5%)
  other arithmetic  5.45 us (2%)
    all_to_all x4, waiting for transfers between devices, exchange(): return lax.all_to_all(x, 'near', split_axis=0, concat_axis=0, tiled=True)  41.5 us
    ppermute x36, waiting for transfers between devices, swap(): return lax.ppermute(x, AX, [(i, i ^ 1 << bit) for i in range(devices)])  40.4 us
    ppermute x36, starting transfers between devices, swap(): return lax.ppermute(x, AX, [(i, i ^ 1 << bit) for i in range(devices)])  38.7 us
    all_to_all x4, starting transfers between devices, exchange(): return lax.all_to_all(x, 'near', split_axis=0, concat_axis=0, tiled=True)  15.7 us
    pallas_call x1, Pallas kernels, local(): pl.pallas_call(functools.partial(enter_kernel, owned_by), grid=(R,), in_s...  14.7 us
    pallas_call x1, Pallas kernels, local(): pl.pallas_call(middle_kernel, grid=(R,), in_specs=[state_spec, row_c, row...  11.4 us
    pallas_call x1, Pallas kernels, local(): pl.pallas_call(back_kernel, grid=(R,), in_specs=[state_spec, state_spec,...  10.5 us
    pallas_call x1, Pallas kernels, local(): pl.pallas_call(pair_kernel, grid=(R,), in_specs=[row_c, row_l, row_l, row...  9.76 us
  transfers between devices with their start and end apart: 43, of which 21 were waited for; matrix products, arithmetic and copies ran while one was open for 4% of the time, Pallas kernels for 24%

profile of v4, /device:TPU:0, one launch (start us, length us, event | category | flops | bytes accessed | tf_op | source)
XLA Modules:
  0.0 282.2 jit_solution(11302029276761045768)
XLA Ops:
  8.0 1.6 pad_maximum_fusion.6
  10.4 4.8 %collective-permute-start = (bf16[2,16,768]{2,1,0:T(8,128)(2,1)S(1)}, bf16[2,16,768]{2,1,0:T(8,128)(2,1)S(1)}, u32[]{:S(2)}, u32[]{:S(2)}) collective-permute-start(bf16[2,16,768]{2,1,0:T(8,128)(2,1)S(1)} %slice.124), channel_id=1, source_target_pairs={{0,1},{1,2},{2,3},{3,4},{4,5},{5,6},{6,7},{8,9},{9,10},{10,11},{11... | collective-permute-start | bytes 147464 | tf_op jit(solution)/shard_map/ppermute | solution.py:570
  16.0 2.6 collective-permute-start.5
  22.1 2.7 collective-permute-start.1
  24.8 1.6 collective-permute-start.6
  26.4 1.6 collective-permute-start.10
  28.8 1.2 collective-permute-start.2
  30.1 1.0 collective-permute-start.7
  31.1 1.0 collective-permute-start.11
  32.1 1.5 collective-permute-done.2
  33.6 1.5 collective-permute-start.3
  35.8 1.4 collective-permute-start.8
  38.1 1.7 collective-permute-done.3
  39.9 1.2 collective-permute-start.4
  41.1 2.7 collective-permute-done.8
  43.9 1.7 collective-permute-done.12
  46.5 2.6 collective-permute-done.4
  49.9 1.4 collective-permute-done.13.refs_3_
  52.0 14.7 %enter.1 = (bf16[2,256,768]{2,1,0:T(8,128)(2,1)}, bf16[2,272,1792]{2,1,0:T(8,128)(2,1)}, f32[2,256,128]{2,1,0:T(8,128)}, bf16[2,256,1792]{2,1,0:T(8,128)(2,1)}, ...) custom-call(s32[1]{0:T(128)} %bitcast.1.core_ref, ...), custom_call_target="tpu_custom_call" | custom-call | flops 4000000000 | bytes 20000000 | tf_op jit(solution)/shard_map/enter/pallas_call | solution.py:609
  66.7 4.6 %all-to-all-start = ((bf16[8,2,16,1664]{3,2,1,0:T(8,128)(2,1)}), bf16[8,2,16,1664]{3,2,1,0:T(8,128)(2,1)S(1)}, u32[]{:S(2)}, u32[]{:S(2)}) async-start(bf16[8,2,16,1664]{3,2,1,0:T(8,128)(2,1)} %get-tuple-element.114), calls=%async_computation | async-start | bytes 1703936 | tf_op jit(solution)/shard_map/all_to_all | solution.py:632
  71.4 6.0 %inside.1._.intra = f32[2,256,1536]{2,1,0:T(8,128)} custom-call(bf16[2,256,1792]{2,1,0:T(8,128)(2,1)} %get-tuple-element.115.act, f32[2,256,128]{2,1,0:T(8,128)} %get-tuple-element.116.step, f32[2,256,128]{2,1,0:T(8,128)} %get-tuple-element.117.cum), custom_call_target="tpu_custom_call" | custom-call | flops 8000000000 | bytes 5000000 | tf_op jit(solution)/shard_map/inside/pallas_call | solution.py:652
  77.4 19.1 %all-to-all-done.p.g = bf16[8,2,16,1664]{3,2,1,0:T(8,128)(2,1)S(1)} async-done(((bf16[8,2,16,1664]{3,2,1,0:T(8,128)(2,1)}), bf16[8,2,16,1664]{3,2,1,0:T(8,128)(2,1)S(1)}, u32[]{:S(2)}, u32[]{:S(2)}) %all-to-all-start) | async-done | bytes 852000 | tf_op jit(solution)/shard_map/all_to_all | solution.py:632
  96.5 0.9 copy-done.13
  97.4 2.5 pass.2
  99.9 3.7 %all-to-all-start.1 = ((bf16[8,2,16,1536]{3,2,1,0:T(8,128)(2,1)}), bf16[8,2,16,1536]{3,2,1,0:T(8,128)(2,1)S(1)}, u32[]{:S(2)}, u32[]{:S(2)}) async-start(bf16[8,2,16,1536]{3,2,1,0:T(8,128)(2,1)} %pass.2), calls=%async_computation.1 | async-start | bytes 1572864 | tf_op jit(solution)/shard_map/all_to_all | solution.py:632
  103.7 3.4 %slice.129 = bf16[32,48,768]{2,1,0:T(8,128)(2,1)} slice(bf16[32,96,768]{2,1,0:T(8,128)(2,1)} %bitcast.114), slice={[0:32], [48:96], [0:768]} | slice | bytes 4718592 | tf_op jit(solution)/shard_map/slice | solution.py:599
  107.1 1.5 fusion.9
  108.6 6.6 %gates.1 = (bf16[2,256,1536]{2,1,0:T(8,128)(2,1)}, f32[2,256,1536]{2,1,0:T(8,128)}) custom-call(bf16[2,256,768]{2,1,0:T(8,128)(2,1)} %get-tuple-element.118.hid, bf16[2,256,768]{2,1,0:T(8,128)(2,1)} %bitcast.108, bf16[768,768]{1,0:T(8,128)(2,1)} %bitcast.118, bf16[768,768]{1,0:T(8,128)(2,1)} %bitcast.116, bf16[1536,768]{1,0:T(8,128)(2,1)} %bitcast.112), custom_call_target="tpu_custom_call" | custom-call | flops 4000000000 | bytes 10000000 | tf_op jit(solution)/shard_map/gates/pallas_call | solution.py:663
  115.2 8.7 %all-to-all-done.1.st = bf16[8,2,16,1536]{3,2,1,0:T(8,128)(2,1)S(1)} async-done(((bf16[8,2,16,1536]{3,2,1,0:T(8,128)(2,1)}), bf16[8,2,16,1536]{3,2,1,0:T(8,128)(2,1)S(1)}, u32[]{:S(2)}, u32[]{:S(2)}) %all-to-all-start.1) | async-done | bytes 786464 | tf_op jit(solution)/shard_map/all_to_all | solution.py:632
  124.8 11.4 %middle.1 = (bf16[2,256,1536]{2,1,0:T(8,128)(2,1)}, bf16[2,256,1536]{2,1,0:T(8,128)(2,1)}, bf16[2,256,1536]{2,1,0:T(8,128)(2,1)}, f32[2,256,128]{2,1,0:T(8,128)}...) custom-call(bf16[8,2,16,1536]{3,2,1,0:T(8,128)(2,1)} %copy-done.15, ...), custom_call_target="tpu_custom_call" | custom-call | flops 4000000000 | bytes 15000000 | tf_op jit(solution)/shard_map/middle/pallas_call | solution.py:677
  136.2 3.6 %all-to-all-start.2 = ((bf16[8,2,16,1536]{3,2,1,0:T(8,128)(2,1)}), bf16[8,2,16,1536]{3,2,1,0:T(8,128)(2,1)S(1)}, u32[]{:S(2)}, u32[]{:S(2)}) async-start(bf16[8,2,16,1536]{3,2,1,0:T(8,128)(2,1)} %get-tuple-element.123), calls=%async_computation.2 | async-start | bytes 1572864 | tf_op jit(solution)/shard_map/all_to_all | solution.py:632
  139.8 8.2 %outer.1 = (f32[2,192,3072]{2,1,0:T(8,128)}, bf16[2,192,3072]{2,1,0:T(8,128)(2,1)}) custom-call(s32[1]{0:T(128)} %bitcast.1.core_ref, bf16[2,256,768]{2,1,0:T(8,128)(2,1)} %bitcast.109, bf16[2,256,768]{2,1,0:T(8,128)(2,1)} %get-tuple-element.118.hid, bf16[2,256,1536]{2,1,0:T(8,128)(2,1)} %get-tuple-element.122.normed, ...), custom_call_target="tpu_custom_call" | custom-call | flops 6000000000 | bytes 20000000 | tf_op jit(solution)/shard_map/outer/pallas_call | solution.py:695
  148.0 4.4 %slope.1._.dh = f32[2,256,768]{2,1,0:T(8,128)} custom-call(bf16[2,256,1536]{2,1,0:T(8,128)(2,1)} %get-tuple-element.124.dgate, bf16[768,768]{1,0:T(8,128)(2,1)} %bitcast.119, bf16[768,768]{1,0:T(8,128)(2,1)} %bitcast.117), custom_call_target="tpu_custom_call" | custom-call | flops 1200000000 | bytes 6000000 | tf_op jit(solution)/shard_map/slope/pallas_call | solution.py:718
  152.4 7.8 %all-to-all-done.2.p = bf16[8,2,16,1536]{3,2,1,0:T(8,128)(2,1)S(1)} async-done(((bf16[8,2,16,1536]{3,2,1,0:T(8,128)(2,1)}), bf16[8,2,16,1536]{3,2,1,0:T(8,128)(2,1)S(1)}, u32[]{:S(2)}, u32[]{:S(2)}) %all-to-all-start.2) | async-done | bytes 786464 | tf_op jit(solution)/shard_map/all_to_all | solution.py:632
  161.0 2.5 pass.3._
  163.5 3.8 %all-to-all-start.3 = ((bf16[8,2,16,1536]{3,2,1,0:T(8,128)(2,1)}), bf16[8,2,16,1536]{3,2,1,0:T(8,128)(2,1)S(1)}, u32[]{:S(2)}, u32[]{:S(2)}) async-start(bf16[8,2,16,1536]{3,2,1,0:T(8,128)(2,1)} %pass.3._), calls=%async_computation.3 | async-start | bytes 1572864 | tf_op jit(solution)/shard_map/all_to_all | solution.py:632
  167.3 9.8 %pair.1 = (f32[2,256,1536]{2,1,0:T(8,128)}, f32[2,256,128]{2,1,0:T(8,128)}, f32[2,256,128]{2,1,0:T(8,128)}) custom-call(bf16[2,256,1792]{2,1,0:T(8,128)(2,1)} %get-tuple-element.115.act, f32[2,256,128]{2,1,0:T(8,128)} %get-tuple-element.116.step, f32[2,256,128]{2,1,0:T(8,128)} %get-tuple-element.117.cum, bf16[2,256,1536]{2,1,0:T(8,128)(2,1)} %get-tuple-element.127.dy, ...), custom_call_target="tpu_custom_call" | custom-call | flops 16000000000 | bytes 10000000 | tf_op jit(solution)/shard_map/pair/pallas_call | solution.py:707
  177.0 4.4 %result.1.__ = bf16[2,256,768]{2,1,0:T(8,128)(2,1)} custom-call(bf16[2,256,768]{2,1,0:T(8,128)(2,1)} %bitcast.103, bf16[2,256,1536]{2,1,0:T(8,128)(2,1)} %get-tuple-element.122.normed, bf16[1536,768]{1,0:T(8,128)(2,1)} %bitcast.113, bf16[8,2,16,1536]{3,2,1,0:T(8,128)(2,1)} %pass.3._), custom_call_target="tpu_custom_call" | custom-call | flops 1200000000 | bytes 6000000 | tf_op jit(solution)/shard_map/result/pallas_call | solution.py:729
  181.4 6.0 %all-to-all-done.3.later = bf16[8,2,16,1536]{3,2,1,0:T(8,128)(2,1)S(1)} async-done(((bf16[8,2,16,1536]{3,2,1,0:T(8,128)(2,1)}), bf16[8,2,16,1536]{3,2,1,0:T(8,128)(2,1)S(1)}, u32[]{:S(2)}, u32[]{:S(2)}) %all-to-all-start.3) | async-done | bytes 786464 | tf_op jit(solution)/shard_map/all_to_all | solution.py:632
  187.4 0.9 copy-done.16
  188.3 10.5 %back.1 = (f32[2,256,1792]{2,1,0:T(8,128)}, f32[2,8,1792]{2,1,0:T(8,128)}, f32[2,256,128]{2,1,0:T(8,128)}, f32[2,8,128]{2,1,0:T(8,128)}) custom-call(bf16[8,2,16,1536]{3,2,1,0:T(8,128)(2,1)} %copy-done.16, bf16[8,2,16,1536]{3,2,1,0:T(8,128)(2,1)} %copy-done.15, bf16[2,256,1792]{2,1,0:T(8,128)(2,1)} %get-tuple-element.115.act, ...), custom_call_target="tpu_custom_call" | custom-call | flops 4000000000 | bytes 15000000 | tf_op jit(solution)/shard_map/back/pallas_call | solution.py:741
  198.8 1.6 collective-permute-start.17
  200.4 4.3 %taps.1.gone = f32[8,1792]{1,0:T(8,128)} custom-call(f32[2,256,1792]{2,1,0:T(8,128)} %get-tuple-element.134.dpre, bf16[2,272,1792]{2,1,0:T(8,128)(2,1)} %get-tuple-element.137.conv, f32[2,16,1536]{2,1,0:T(8,128)} %get-tuple-element.138.sums, f32[2,8,128]{2,1,0:T(8,128)} %get-tuple-element.139.hsum), custom_call_target="tpu_custom_call" | custom-call | flops 20000000 | bytes 6000000 | tf_op jit(solution)/shard_map/taps/pallas_call | solution.py:760
  204.7 1.0 collective-permute-done.17.edge
  206.5 5.4 %input.1 = (bf16[2,256,1920]{2,1,0:T(8,128)(2,1)S(1)}, f32[8,1792]{1,0:T(8,128)S(1)}, f32[2,192,640]{2,1,0:T(8,128)S(1)}, f32[2,192,640]{2,1,0:T(8,128)S(1)}, f3...) custom-call(s32[1]{0:T(128)} %bitcast.1.core_ref, ...), custom_call_target="tpu_custom_call" | custom-call | flops 2000000000 | bytes 10000000 | tf_op jit(solution)/shard_map/input/pallas_call | solution.py:772
  213.1 2.3 collective-permute-done.18.other
  215.4 3.1 %join.4 = (f32[2,2,2,24,1664]{4,3,2,1,0:T(8,128)S(1)}, f32[2,2,2,24,1664]{4,3,2,1,0:T(8,128)S(1)}, f32[2,2,2,24,1664]{4,3,2,1,0:T(8,128)S(1)}, bf16[2,2,2,24,166...) custom-call(s32[3]{0:T(128)S(1)} %pad_add_fusion.bit_ref, ...), custom_call_target="tpu_custom_call" | custom-call | flops 1000000 | bytes 8000000 | tf_op jit(solution)/shard_map/join/pallas_call | solution.py:798
  218.5 2.4 collective-permute-start.23
  220.9 1.5 collective-permute-start.24
  222.8 1.9 collective-permute-start.22
  224.7 3.3 %token_.1._ = bf16[2,256,768]{2,1,0:T(8,128)(2,1)} custom-call(bf16[2,256,768]{2,1,0:T(8,128)(2,1)S(1)} %bitcast.104, bf16[2,256,768]{2,1,0:T(8,128)(2,1)S(1)} %bitcast.110, f32[2,256,768]{2,1,0:T(8,128)S(1)} %copy-done.4, bf16[2,256,1920]{2,1,0:T(8,128)(2,1)S(1)} %get-tuple-element.140.dproj, bf16[768,1920]{1,0:T(8,128)(2,1)S(1)} %copy-done.11, ...), custom_call_target="tpu_custom_call" | custom-call | flops 4000000000 | bytes 15000000 | tf_op jit(solution)/shard_map/token/pallas_call | solution.py:812
  228.0 8.8 %collective-permute-done.22.other = f32[8,1792]{1,0:T(8,128)S(1)} collective-permute-done((f32[8,1792]{1,0:T(8,128)S(1)}, f32[8,1792]{1,0:T(8,128)S(1)}, u32[]{:S(2)}, u32[]{:S(2)}) %collective-permute-start.22) | collective-permute-done | bytes 57376 | tf_op jit(solution)/shard_map/ppermute | solution.py:536
  237.0 1.3 collective-permute-done.25.refs_5_
  238.3 1.1 copy-done.2
  239.4 0.9 join.5
  240.9 1.5 collective-permute-start.28
  243.1 1.5 collective-permute-start.26
  244.7 5.0 %collective-permute-done.26.other = f32[8,1792]{1,0:T(8,128)S(1)} collective-permute-done((f32[8,1792]{1,0:T(8,128)S(1)}, f32[8,1792]{1,0:T(8,128)S(1)}, u32[]{:S(2)}, u32[]{:S(2)}) %collective-permute-start.26) | collective-permute-done | bytes 57376 | tf_op jit(solution)/shard_map/ppermute | solution.py:536
  251.8 1.4 collective-permute-start.32
  253.9 1.2 collective-permute-start.30
  255.1 3.0 %collective-permute-done.30.other = f32[8,1792]{1,0:T(8,128)S(1)} collective-permute-done((f32[8,1792]{1,0:T(8,128)S(1)}, f32[8,1792]{1,0:T(8,128)S(1)}, u32[]{:S(2)}, u32[]{:S(2)}) %collective-permute-start.30) | collective-permute-done | bytes 57376 | tf_op jit(solution)/shard_map/ppermute | solution.py:536
  259.2 2.9 %collective-permute-start.36 = (bf16[24,1664]{1,0:T(8,128)(2,1)S(1)}, bf16[24,1664]{1,0:T(8,128)(2,1)S(1)}, u32[]{:S(2)}, u32[]{:S(2)}) collective-permute-start(bf16[24,1664]{1,0:T(8,128)(2,1)S(1)} %get-tuple-element.175), channel_id=1, source_target_pairs={{0,4},{1,5},{2,6},{3,7},{4,0},{5,1},{6,2},{7,3},{8,12},{9,13},{10,... | collective-permute-start | bytes 239624 | tf_op jit(solution)/shard_map/ppermute | solution.py:536
  262.2 2.8 %collective-permute-start.34 = (f32[8,1792]{1,0:T(8,128)S(1)}, f32[8,1792]{1,0:T(8,128)S(1)}, u32[]{:S(2)}, u32[]{:S(2)}) collective-permute-start(f32[8,1792]{1,0:T(8,128)S(1)} %get-tuple-element.170.small), channel_id=1, source_target_pairs={{0,4},{1,5},{2,6},{3,7},{4,0},{5,1},{6,2},{7,3},{8,12},{9,13},{10,... | collective-permute-start | bytes 172040 | tf_op jit(solution)/shard_map/ppermute | solution.py:536
  265.2 6.4 %collective-permute-done.34.other = f32[8,1792]{1,0:T(8,128)S(1)} collective-permute-done((f32[8,1792]{1,0:T(8,128)S(1)}, f32[8,1792]{1,0:T(8,128)S(1)}, u32[]{:S(2)}, u32[]{:S(2)}) %collective-permute-start.34) | collective-permute-done | bytes 57376 | tf_op jit(solution)/shard_map/ppermute | solution.py:536
  (157 shorter events, 24.4 us)
Async XLA Ops:
  7.2 96.5 %all-gather.3.cloned.1.call-start = ((), (), s32[]{:S(2)}) async-start(), calls=%async_computation.4 | async-start | bytes 4866048 | tf_op jit(solution)/shard_map/all_gather | solution.py:596
  10.4 17.6 %collective-permute-start = (bf16[2,16,768]{2,1,0:T(8,128)(2,1)S(1)}, bf16[2,16,768]{2,1,0:T(8,128)(2,1)S(1)}, u32[]{:S(2)}, u32[]{:S(2)}) collective-permute-start(bf16[2,16,768]{2,1,0:T(8,128)(2,1)S(1)} %slice.124), channel_id=1, source_target_pairs={{0,1},{1,2},{2,3},{3,4},{4,5},{5,6},{6,7},{8,9},{9,10},{10,11},{11... | collective-permute-start | bytes 147464 | tf_op jit(solution)/shard_map/ppermute | solution.py:570
  16.0 5.3 %collective-permute-start.5 = (bf16[24,640]{1,0:T(8,128)(2,1)S(1)}, bf16[24,640]{1,0:T(8,128)(2,1)S(1)}, u32[]{:S(2)}, u32[]{:S(2)}) collective-permute-start(bf16[24,640]{1,0:T(8,128)(2,1)S(1)} %slice.111), channel_id=1, source_target_pairs={{0,4},{1,5},{2,6},{3,7},{4,0},{5,1},{6,2},{7,3},{8,12},{9,13},{10,... | collective-permute-start | bytes 92168 | tf_op jit(solution)/shard_map/ppermute | solution.py:536
  21.0 5.4 %collective-permute-start.9 = (bf16[24,640]{1,0:T(8,128)(2,1)S(1)}, bf16[24,640]{1,0:T(8,128)(2,1)S(1)}, u32[]{:S(2)}, u32[]{:S(2)}) collective-permute-start(bf16[24,640]{1,0:T(8,128)(2,1)S(1)} %fusion.1), channel_id=1, source_target_pairs={{0,4},{1,5},{2,6},{3,7},{4,0},{5,1},{6,2},{7,3},{8,12},{9,13},{10,... | collective-permute-start | bytes 92168 | tf_op jit(solution)/shard_map/ppermute | solution.py:536
  22.1 5.9 %collective-permute-start.1 = (bf16[24,640]{1,0:T(8,128)(2,1)S(1)}, bf16[24,640]{1,0:T(8,128)(2,1)S(1)}, u32[]{:S(2)}, u32[]{:S(2)}) collective-permute-start(bf16[24,640]{1,0:T(8,128)(2,1)S(1)} %get-tuple-element.223), channel_id=1, source_target_pairs={{0,4},{1,5},{2,6},{3,7},{4,0},{5,1},{6,2},{7,3},{8,12},{9,13},{10,... | collective-permute-start | bytes 92168 | tf_op jit(solution)/shard_map/ppermute | solution.py:536
  24.8 5.3 %collective-permute-start.6 = (bf16[2,24,640]{2,1,0:T(8,128)(2,1)S(1)}, bf16[2,24,640]{2,1,0:T(8,128)(2,1)S(1)}, u32[]{:S(2)}, u32[]{:S(2)}) collective-permute-start(bf16[2,24,640]{2,1,0:T(8,128)(2,1)S(1)} %pad_maximum_fusion.10), channel_id=1, source_target_pairs={{0,1},{1,0},{2,3},{3,2},{4,5},{5,4},{6,7},{7,6},{8,9},{9,8},{10,11... | collective-permute-start | bytes 184328 | tf_op jit(solution)/shard_map/ppermute | solution.py:536
  26.4 4.6 %collective-permute-start.10 = (bf16[2,24,640]{2,1,0:T(8,128)(2,1)S(1)}, bf16[2,24,640]{2,1,0:T(8,128)(2,1)S(1)}, u32[]{:S(2)}, u32[]{:S(2)}) collective-permute-start(bf16[2,24,640]{2,1,0:T(8,128)(2,1)S(1)} %pad_maximum_fusion.11), channel_id=1, source_target_pairs={{0,16},{1,17},{2,18},{3,19},{4,20},{5,21},{6,22},{7,23},{8,24},{9,... | collective-permute-start | bytes 184328 | tf_op jit(solution)/shard_map/ppermute | solution.py:536
  28.0 11.9 %copy-start.22 = (bf16[2,16,768]{2,1,0:T(8,128)(2,1)}, bf16[2,16,768]{2,1,0:T(8,128)(2,1)S(1)}, u32[]{:S(2)}) copy-start(bf16[2,16,768]{2,1,0:T(8,128)(2,1)S(1)} %collective-permute-done.halo) | copy-start | bytes 147460
  28.8 4.8 %collective-permute-start.2 = (bf16[2,24,640]{2,1,0:T(8,128)(2,1)S(1)}, bf16[2,24,640]{2,1,0:T(8,128)(2,1)S(1)}, u32[]{:S(2)}, u32[]{:S(2)}) collective-permute-start(bf16[2,24,640]{2,1,0:T(8,128)(2,1)S(1)} %pad_maximum_fusion.9), channel_id=1, source_target_pairs={{0,2},{1,3},{2,0},{3,1},{4,6},{5,7},{6,4},{7,5},{8,10},{9,11},{10,... | collective-permute-start | bytes 184328 | tf_op jit(solution)/shard_map/ppermute | solution.py:536
  30.1 5.7 %collective-permute-start.7 = (bf16[2,2,24,640]{3,2,0,1:T(8,128)(2,1)S(1)}, bf16[2,2,24,640]{3,2,0,1:T(8,128)(2,1)S(1)}, u32[]{:S(2)}, u32[]{:S(2)}) collective-permute-start(bf16[2,2,24,640]{3,2,0,1:T(8,128)(2,1)S(1)} %pad_maximum_fusion.7), channel_id=1, source_target_pairs={{0,2},{1,3},{2,0},{3,1},{4,6},{5,7},{6,4},{7,5},{8,10},{9,11},{10,... | collective-permute-start | bytes 368648 | tf_op jit(solution)/shard_map/ppermute | solution.py:536
  31.1 6.1 %collective-permute-start.11 = (bf16[2,2,24,640]{3,2,1,0:T(8,128)(2,1)S(1)}, bf16[2,2,24,640]{3,2,1,0:T(8,128)(2,1)S(1)}, u32[]{:S(2)}, u32[]{:S(2)}) collective-permute-start(bf16[2,2,24,640]{3,2,1,0:T(8,128)(2,1)S(1)} %pad_maximum_fusion.8), channel_id=1, source_target_pairs={{0,1},{1,0},{2,3},{3,2},{4,5},{5,4},{6,7},{7,6},{8,9},{9,8},{10,11... | collective-permute-start | bytes 368648 | tf_op jit(solution)/shard_map/ppermute | solution.py:536
  33.6 6.2 %collective-permute-start.3 = (bf16[2,2,24,640]{3,2,0,1:T(8,128)(2,1)S(1)}, bf16[2,2,24,640]{3,2,0,1:T(8,128)(2,1)S(1)}, u32[]{:S(2)}, u32[]{:S(2)}) collective-permute-start(bf16[2,2,24,640]{3,2,0,1:T(8,128)(2,1)S(1)} %maximum_add_fusion), channel_id=1, source_target_pairs={{0,16},{1,17},{2,18},{3,19},{4,20},{5,21},{6,22},{7,23},{8,24},{9,... | collective-permute-start | bytes 368648 | tf_op jit(solution)/shard_map/ppermute | solution.py:536
  35.8 8.0 %collective-permute-start.8 = (bf16[2,2,2,24,640]{4,3,0,2,1:T(8,128)(2,1)S(1)}, bf16[2,2,2,24,640]{4,3,0,2,1:T(8,128)(2,1)S(1)}, u32[]{:S(2)}, u32[]{:S(2)}) collective-permute-start(bf16[2,2,2,24,640]{4,3,0,2,1:T(8,128)(2,1)S(1)} %pad_maximum_fusion.4), channel_id=1, source_target_pairs={{0,16},{1,17},{2,18},{3,19},{4,20},{5,21},{6,22},{7,23},{8,24},{9,... | collective-permute-start | bytes 737288 | tf_op jit(solution)/shard_map/ppermute | solution.py:536
  37.3 8.4 %collective-permute-start.12 = (bf16[2,2,2,24,640]{4,3,1,0,2:T(8,128)(2,1)S(1)}, bf16[2,2,2,24,640]{4,3,1,0,2:T(8,128)(2,1)S(1)}, u32[]{:S(2)}, u32[]{:S(2)}) collective-permute-start(bf16[2,2,2,24,640]{4,3,1,0,2:T(8,128)(2,1)S(1)} %pad_maximum_fusion.5), channel_id=1, source_target_pairs={{0,2},{1,3},{2,0},{3,1},{4,6},{5,7},{6,4},{7,5},{8,10},{9,11},{10,... | collective-permute-start | bytes 737288 | tf_op jit(solution)/shard_map/ppermute | solution.py:536
  39.9 9.2 %collective-permute-start.4 = (bf16[2,2,2,24,640]{4,3,1,2,0:T(8,128)(2,1)S(1)}, bf16[2,2,2,24,640]{4,3,1,2,0:T(8,128)(2,1)S(1)}, u32[]{:S(2)}, u32[]{:S(2)}) collective-permute-start(bf16[2,2,2,24,640]{4,3,1,2,0:T(8,128)(2,1)S(1)} %pad_maximum_fusion.3), channel_id=1, source_target_pairs={{0,1},{1,0},{2,3},{3,2},{4,5},{5,4},{6,7},{7,6},{8,9},{9,8},{10,11... | collective-permute-start | bytes 737288 | tf_op jit(solution)/shard_map/ppermute | solution.py:536
  45.8 3.5 %copy-start.18 = (bf16[2,2,2,2,24,640]{5,4,3,2,1,0:T(8,128)(2,1)}, bf16[2,2,2,2,24,640]{5,4,3,2,1,0:T(8,128)(2,1)S(1)}, u32[]{:S(2)}) copy-start(bf16[2,2,2,2,24,640]{5,4,3,2,1,0:T(8,128)(2,1)S(1)} %copy.32) | copy-start | bytes 1474564
  45.8 3.6 %copy-start.24 = (f32[24]{0:T(128)S(1)}, f32[24]{0:T(128)}, u32[]{:S(2)}) copy-start(f32[24]{0:T(128)} %param.23) | copy-start | bytes 292
  45.8 3.6 %copy-start.25 = (f32[24]{0:T(128)S(1)}, f32[24]{0:T(128)}, u32[]{:S(2)}) copy-start(f32[24]{0:T(128)} %param.24) | copy-start | bytes 292
  45.8 3.8 %copy-start.26 = (f32[24]{0:T(128)S(1)}, f32[24]{0:T(128)}, u32[]{:S(2)}) copy-start(f32[24]{0:T(128)} %param.25) | copy-start | bytes 292
  45.9 5.3 %copy-start.19 = (bf16[2,192,640]{2,1,0:T(8,128)(2,1)}, bf16[2,192,640]{2,1,0:T(8,128)(2,1)S(1)}, u32[]{:S(2)}) copy-start(bf16[2,192,640]{2,1,0:T(8,128)(2,1)S(1)} %pad_maximum_fusion.1.refs_1_) | copy-start | bytes 1474564
  45.9 3.9 %collective-permute-start.14 = (bf16[2,192,640]{2,1,0:T(8,128)(2,1)S(1)}, bf16[2,192,640]{2,1,0:T(8,128)(2,1)S(1)}, u32[]{:S(2)}, u32[]{:S(2)}) collective-permute-start(bf16[2,192,640]{2,1,0:T(8,128)(2,1)S(1)} %pad_maximum_fusion.1.refs_1_), channel_id=1, source_target_pairs={{0,8},{1,9},{2,10},{3,11},{4,12},{5,13},{6,14},{7,15},{8,0},{9,1},... | collective-permute-start | bytes 1474568 | tf_op jit(solution)/shard_map/ppermute | solution.py:536
  46.0 3.9 %collective-permute-start.15 = (bf16[2,192,640]{2,1,0:T(8,128)(2,1)S(1)}, bf16[2,192,640]{2,1,0:T(8,128)(2,1)S(1)}, u32[]{:S(2)}, u32[]{:S(2)}) collective-permute-start(bf16[2,192,640]{2,1,0:T(8,128)(2,1)S(1)} %bitcast.123), channel_id=1, source_target_pairs={{0,8},{1,9},{2,10},{3,11},{4,12},{5,13},{6,14},{7,15},{8,0},{9,1},... | collective-permute-start | bytes 1474568 | tf_op jit(solution)/shard_map/ppermute | solution.py:536
  49.3 1.9 copy-start.20
  49.3 1.9 collective-permute-start.13
  49.8 1.4 copy-start.21
  66.7 29.8 %all-to-all-start = ((bf16[8,2,16,1664]{3,2,1,0:T(8,128)(2,1)}), bf16[8,2,16,1664]{3,2,1,0:T(8,128)(2,1)S(1)}, u32[]{:S(2)}, u32[]{:S(2)}) async-start(bf16[8,2,16,1664]{3,2,1,0:T(8,128)(2,1)} %get-tuple-element.114), calls=%async_computation | async-start | bytes 1703936 | tf_op jit(solution)/shard_map/all_to_all | solution.py:632
  99.9 24.0 %all-to-all-start.1 = ((bf16[8,2,16,1536]{3,2,1,0:T(8,128)(2,1)}), bf16[8,2,16,1536]{3,2,1,0:T(8,128)(2,1)S(1)}, u32[]{:S(2)}, u32[]{:S(2)}) async-start(bf16[8,2,16,1536]{3,2,1,0:T(8,128)(2,1)} %pass.2), calls=%async_computation.1 | async-start | bytes 1572864 | tf_op jit(solution)/shard_map/all_to_all | solution.py:632
  103.6 3.4 %copy-start.14 = (bf16[3072,768]{1,0:T(8,128)(2,1)S(1)}, bf16[3072,768]{1,0:T(8,128)(2,1)}, u32[]{:S(2)}) copy-start(bf16[3072,768]{1,0:T(8,128)(2,1)} %all-gather.3.cloned.1.call-done) | copy-start | bytes 14155780
  136.2 24.0 %all-to-all-start.2 = ((bf16[8,2,16,1536]{3,2,1,0:T(8,128)(2,1)}), bf16[8,2,16,1536]{3,2,1,0:T(8,128)(2,1)S(1)}, u32[]{:S(2)}, u32[]{:S(2)}) async-start(bf16[8,2,16,1536]{3,2,1,0:T(8,128)(2,1)} %get-tuple-element.123), calls=%async_computation.2 | async-start | bytes 1572864 | tf_op jit(solution)/shard_map/all_to_all | solution.py:632
  148.0 33.4 %collective-permute-start.16 = (bf16[2,192,3072]{2,1,0:T(8,128)(2,1)}, bf16[2,192,3072]{2,1,0:T(8,128)(2,1)S(1)}, u32[]{:S(2)}, u32[]{:S(2)}) collective-permute-start(bf16[2,192,3072]{2,1,0:T(8,128)(2,1)} %get-tuple-element.133), channel_id=1, source_target_pairs={{0,8},{1,9},{2,10},{3,11},{4,12},{5,13},{6,14},{7,15},{8,0},{9,1},... | collective-permute-start | bytes 7077896 | tf_op jit(solution)/shard_map/ppermute | solution.py:536
  163.5 23.9 %all-to-all-start.3 = ((bf16[8,2,16,1536]{3,2,1,0:T(8,128)(2,1)}), bf16[8,2,16,1536]{3,2,1,0:T(8,128)(2,1)S(1)}, u32[]{:S(2)}, u32[]{:S(2)}) async-start(bf16[8,2,16,1536]{3,2,1,0:T(8,128)(2,1)} %pass.3._), calls=%async_computation.3 | async-start | bytes 1572864 | tf_op jit(solution)/shard_map/all_to_all | solution.py:632
  181.4 6.0 %copy-start = (bf16[2,192,3072]{2,1,0:T(8,128)(2,1)}, bf16[2,192,3072]{2,1,0:T(8,128)(2,1)S(1)}, u32[]{:S(2)}) copy-start(bf16[2,192,3072]{2,1,0:T(8,128)(2,1)S(1)} %collective-permute-done.16.___) | copy-start | bytes 7077892
  198.8 6.9 %collective-permute-start.17 = (f32[2,8,1792]{2,1,0:T(8,128)}, f32[2,8,1792]{2,1,0:T(8,128)S(1)}, u32[]{:S(2)}, u32[]{:S(2)}) collective-permute-start(f32[2,8,1792]{2,1,0:T(8,128)} %get-tuple-element.135), channel_id=1, source_target_pairs={{1,0},{2,1},{3,2},{4,3},{5,4},{6,5},{7,6},{9,8},{10,9},{11,10},{12... | collective-permute-start | bytes 344072 | tf_op jit(solution)/shard_map/ppermute | solution.py:758
  200.3 5.3 %copy-start.9 = (f32[2,256,128]{2,1,0:T(8,128)S(1)}, f32[2,256,128]{2,1,0:T(8,128)}, u32[]{:S(2)}) copy-start(f32[2,256,128]{2,1,0:T(8,128)} %get-tuple-element.136.draw) | copy-start | bytes 786436
  200.4 5.3 %copy-start.10 = (bf16[2,256,768]{2,1,0:T(8,128)(2,1)S(1)}, bf16[2,256,768]{2,1,0:T(8,128)(2,1)}, u32[]{:S(2)}) copy-start(bf16[2,256,768]{2,1,0:T(8,128)(2,1)} %get-tuple-element.118.hid) | copy-start | bytes 2359300
  200.4 5.3 %copy-start.12 = (f32[8,1792]{1,0:T(8,128)S(1)}, f32[8,1792]{1,0:T(8,128)}, u32[]{:S(2)}) copy-start(f32[8,1792]{1,0:T(8,128)} %get-tuple-element.121.par) | copy-start | bytes 172036
  206.5 8.8 %copy-start.1 = (bf16[2,192,3072]{2,1,0:T(8,128)(2,1)S(1)}, bf16[2,192,3072]{2,1,0:T(8,128)(2,1)}, u32[]{:S(2)}) copy-start(bf16[2,192,3072]{2,1,0:T(8,128)(2,1)} %copy-done) | copy-start | bytes 7077892
  211.9 3.4 %collective-permute-start.19 = (bf16[2,192,640]{2,1,0:T(8,128)(2,1)S(1)}, bf16[2,192,640]{2,1,0:T(8,128)(2,1)S(1)}, u32[]{:S(2)}, u32[]{:S(2)}) collective-permute-start(bf16[2,192,640]{2,1,0:T(8,128)(2,1)S(1)} %get-tuple-element.146), channel_id=1, source_target_pairs={{0,8},{1,9},{2,10},{3,11},{4,12},{5,13},{6,14},{7,15},{8,0},{9,1},... | collective-permute-start | bytes 1474568 | tf_op jit(solution)/shard_map/ppermute | solution.py:536
  212.0 3.3 %collective-permute-start.20 = (bf16[2,192,640]{2,1,0:T(8,128)(2,1)S(1)}, bf16[2,192,640]{2,1,0:T(8,128)(2,1)S(1)}, u32[]{:S(2)}, u32[]{:S(2)}) collective-permute-start(bf16[2,192,640]{2,1,0:T(8,128)(2,1)S(1)} %get-tuple-element.147), channel_id=1, source_target_pairs={{0,8},{1,9},{2,10},{3,11},{4,12},{5,13},{6,14},{7,15},{8,0},{9,1},... | collective-permute-start | bytes 1474568 | tf_op jit(solution)/shard_map/ppermute | solution.py:536
  212.5 2.9 %collective-permute-start.21 = (bf16[2,192,640]{2,1,0:T(8,128)(2,1)S(1)}, bf16[2,192,640]{2,1,0:T(8,128)(2,1)S(1)}, u32[]{:S(2)}, u32[]{:S(2)}) collective-permute-start(bf16[2,192,640]{2,1,0:T(8,128)(2,1)S(1)} %get-tuple-element.148), channel_id=1, source_target_pairs={{0,8},{1,9},{2,10},{3,11},{4,12},{5,13},{6,14},{7,15},{8,0},{9,1},... | collective-permute-start | bytes 1474568 | tf_op jit(solution)/shard_map/ppermute | solution.py:536
  212.5 2.8 collective-permute-start.18
  215.3 9.4 %copy-start.4 = (f32[2,256,768]{2,1,0:T(8,128)S(1)}, f32[2,256,768]{2,1,0:T(8,128)}, u32[]{:S(2)}) copy-start(f32[2,256,768]{2,1,0:T(8,128)} %slope.1._.dh) | copy-start | bytes 4718596
  215.3 9.4 %copy-start.6 = (bf16[2,1,256,768]{3,2,1,0:T(8,128)(2,1)S(1)}, bf16[2,1,256,768]{3,2,1,0:T(8,128)(2,1)}, u32[]{:S(2)}) copy-start(bf16[2,1,256,768]{3,2,1,0:T(8,128)(2,1)} %param.17) | copy-start | bytes 2359300
  215.4 9.4 %copy-start.8 = (bf16[2,1,256,768]{3,2,1,0:T(8,128)(2,1)S(1)}, bf16[2,1,256,768]{3,2,1,0:T(8,128)(2,1)}, u32[]{:S(2)}) copy-start(bf16[2,1,256,768]{3,2,1,0:T(8,128)(2,1)} %param.18) | copy-start | bytes 2359300
  215.4 9.4 %copy-start.11 = (bf16[768,1920]{1,0:T(8,128)(2,1)S(1)}, bf16[768,1920]{1,0:T(8,128)(2,1)}, u32[]{:S(2)}) copy-start(bf16[768,1920]{1,0:T(8,128)(2,1)} %get-tuple-element.141.weight) | copy-start | bytes 8847364
  218.5 18.3 %collective-permute-start.23 = (bf16[2,2,2,24,1664]{4,3,2,1,0:T(8,128)(2,1)S(1)}, bf16[2,2,2,24,1664]{4,3,2,1,0:T(8,128)(2,1)S(1)}, u32[]{:S(2)}, u32[]{:S(2)}) collective-permute-start(bf16[2,2,2,24,1664]{4,3,2,1,0:T(8,128)(2,1)S(1)} %get-tuple-element.153), channel_id=1, source_target_pairs={{0,1},{1,0},{2,3},{3,2},{4,5},{5,4},{6,7},{7,6},{8,9},{9,8},{10,11... | collective-permute-start | bytes 1916936 | tf_op jit(solution)/shard_map/ppermute | solution.py:536
  220.9 16.1 %collective-permute-start.24 = (bf16[2,2,2,24,1664]{4,3,2,1,0:T(8,128)(2,1)S(1)}, bf16[2,2,2,24,1664]{4,3,2,1,0:T(8,128)(2,1)S(1)}, u32[]{:S(2)}, u32[]{:S(2)}) collective-permute-start(bf16[2,2,2,24,1664]{4,3,2,1,0:T(8,128)(2,1)S(1)} %get-tuple-element.154), channel_id=1, source_target_pairs={{0,16},{1,17},{2,18},{3,19},{4,20},{5,21},{6,22},{7,23},{8,24},{9,... | collective-permute-start | bytes 1916936 | tf_op jit(solution)/shard_map/ppermute | solution.py:536
  222.4 15.9 %collective-permute-start.25 = (bf16[2,2,2,24,1664]{4,3,2,1,0:T(8,128)(2,1)S(1)}, bf16[2,2,2,24,1664]{4,3,2,1,0:T(8,128)(2,1)S(1)}, u32[]{:S(2)}, u32[]{:S(2)}) collective-permute-start(bf16[2,2,2,24,1664]{4,3,2,1,0:T(8,128)(2,1)S(1)} %get-tuple-element.155), channel_id=1, source_target_pairs={{0,2},{1,3},{2,0},{3,1},{4,6},{5,7},{6,4},{7,5},{8,10},{9,11},{10,... | collective-permute-start | bytes 1916936 | tf_op jit(solution)/shard_map/ppermute | solution.py:536
  222.8 14.0 %collective-permute-start.22 = (f32[8,1792]{1,0:T(8,128)S(1)}, f32[8,1792]{1,0:T(8,128)S(1)}, u32[]{:S(2)}, u32[]{:S(2)}) collective-permute-start(f32[8,1792]{1,0:T(8,128)S(1)} %get-tuple-element.149._.small), channel_id=1, source_target_pairs={{0,1},{1,0},{2,3},{3,2},{4,5},{5,4},{6,7},{7,6},{8,9},{9,8},{10,11... | collective-permute-start | bytes 172040 | tf_op jit(solution)/shard_map/ppermute | solution.py:536
  239.4 11.2 %copy-start.3 = (bf16[2,256,768]{2,1,0:T(8,128)(2,1)S(1)}, bf16[2,256,768]{2,1,0:T(8,128)(2,1)}, u32[]{:S(2)}) copy-start(bf16[2,256,768]{2,1,0:T(8,128)(2,1)} %token_.1._) | copy-start | bytes 2359300
  240.3 9.4 %collective-permute-start.27 = (bf16[2,2,24,1664]{3,2,1,0:T(8,128)(2,1)S(1)}, bf16[2,2,24,1664]{3,2,1,0:T(8,128)(2,1)S(1)}, u32[]{:S(2)}, u32[]{:S(2)}) collective-permute-start(bf16[2,2,24,1664]{3,2,1,0:T(8,128)(2,1)S(1)} %get-tuple-element.160), channel_id=1, source_target_pairs={{0,16},{1,17},{2,18},{3,19},{4,20},{5,21},{6,22},{7,23},{8,24},{9,... | collective-permute-start | bytes 958472 | tf_op jit(solution)/shard_map/ppermute | solution.py:536
  240.9 8.9 %collective-permute-start.28 = (bf16[2,2,24,1664]{3,2,1,0:T(8,128)(2,1)S(1)}, bf16[2,2,24,1664]{3,2,1,0:T(8,128)(2,1)S(1)}, u32[]{:S(2)}, u32[]{:S(2)}) collective-permute-start(bf16[2,2,24,1664]{3,2,1,0:T(8,128)(2,1)S(1)} %get-tuple-element.161), channel_id=1, source_target_pairs={{0,2},{1,3},{2,0},{3,1},{4,6},{5,7},{6,4},{7,5},{8,10},{9,11},{10,... | collective-permute-start | bytes 958472 | tf_op jit(solution)/shard_map/ppermute | solution.py:536
  242.4 8.2 %collective-permute-start.29 = (bf16[2,2,24,1664]{3,2,1,0:T(8,128)(2,1)S(1)}, bf16[2,2,24,1664]{3,2,1,0:T(8,128)(2,1)S(1)}, u32[]{:S(2)}, u32[]{:S(2)}) collective-permute-start(bf16[2,2,24,1664]{3,2,1,0:T(8,128)(2,1)S(1)} %get-tuple-element.162), channel_id=1, source_target_pairs={{0,1},{1,0},{2,3},{3,2},{4,5},{5,4},{6,7},{7,6},{8,9},{9,8},{10,11... | collective-permute-start | bytes 958472 | tf_op jit(solution)/shard_map/ppermute | solution.py:536
  243.1 6.6 %collective-permute-start.26 = (f32[8,1792]{1,0:T(8,128)S(1)}, f32[8,1792]{1,0:T(8,128)S(1)}, u32[]{:S(2)}, u32[]{:S(2)}) collective-permute-start(f32[8,1792]{1,0:T(8,128)S(1)} %get-tuple-element.156.small), channel_id=1, source_target_pairs={{0,16},{1,17},{2,18},{3,19},{4,20},{5,21},{6,22},{7,23},{8,24},{9,... | collective-permute-start | bytes 172040 | tf_op jit(solution)/shard_map/ppermute | solution.py:536
  251.4 13.7 %copy-start.23 = (bf16[24]{0:T(256)(128)(2,1)S(1)}, bf16[24]{0:T(256)(128)(2,1)}, u32[]{:S(2)}) copy-start(bf16[24]{0:T(256)(128)(2,1)} %param.19) | copy-start | bytes 148
  251.4 20.2 %copy-start.5 = (bf16[24,3352]{1,0:T(8,128)(2,1)S(1)}, bf16[24,3352]{1,0:T(8,128)(2,1)}, u32[]{:S(2)}) copy-start(bf16[24,3352]{1,0:T(8,128)(2,1)} %w_in.1) | copy-start | bytes 482692
  251.4 6.7 %collective-permute-start.31 = (bf16[2,24,1664]{2,1,0:T(8,128)(2,1)S(1)}, bf16[2,24,1664]{2,1,0:T(8,128)(2,1)S(1)}, u32[]{:S(2)}, u32[]{:S(2)}) collective-permute-start(bf16[2,24,1664]{2,1,0:T(8,128)(2,1)S(1)} %get-tuple-element.167), channel_id=1, source_target_pairs={{0,2},{1,3},{2,0},{3,1},{4,6},{5,7},{6,4},{7,5},{8,10},{9,11},{10,... | collective-permute-start | bytes 479240 | tf_op jit(solution)/shard_map/ppermute | solution.py:536
  251.8 6.2 %collective-permute-start.32 = (bf16[2,24,1664]{2,1,0:T(8,128)(2,1)S(1)}, bf16[2,24,1664]{2,1,0:T(8,128)(2,1)S(1)}, u32[]{:S(2)}, u32[]{:S(2)}) collective-permute-start(bf16[2,24,1664]{2,1,0:T(8,128)(2,1)S(1)} %get-tuple-element.168), channel_id=1, source_target_pairs={{0,1},{1,0},{2,3},{3,2},{4,5},{5,4},{6,7},{7,6},{8,9},{9,8},{10,11... | collective-permute-start | bytes 479240 | tf_op jit(solution)/shard_map/ppermute | solution.py:536
  253.2 5.3 %collective-permute-start.33 = (bf16[2,24,1664]{2,1,0:T(8,128)(2,1)S(1)}, bf16[2,24,1664]{2,1,0:T(8,128)(2,1)S(1)}, u32[]{:S(2)}, u32[]{:S(2)}) collective-permute-start(bf16[2,24,1664]{2,1,0:T(8,128)(2,1)S(1)} %get-tuple-element.169), channel_id=1, source_target_pairs={{0,16},{1,17},{2,18},{3,19},{4,20},{5,21},{6,22},{7,23},{8,24},{9,... | collective-permute-start | bytes 479240 | tf_op jit(solution)/shard_map/ppermute | solution.py:536
  253.9 4.2 %collective-permute-start.30 = (f32[8,1792]{1,0:T(8,128)S(1)}, f32[8,1792]{1,0:T(8,128)S(1)}, u32[]{:S(2)}, u32[]{:S(2)}) collective-permute-start(f32[8,1792]{1,0:T(8,128)S(1)} %get-tuple-element.163.small), channel_id=1, source_target_pairs={{0,2},{1,3},{2,0},{3,1},{4,6},{5,7},{6,4},{7,5},{8,10},{9,11},{10,... | collective-permute-start | bytes 172040 | tf_op jit(solution)/shard_map/ppermute | solution.py:536
  259.2 12.4 %collective-permute-start.35 = (bf16[24,1664]{1,0:T(8,128)(2,1)S(1)}, bf16[24,1664]{1,0:T(8,128)(2,1)S(1)}, u32[]{:S(2)}, u32[]{:S(2)}) collective-permute-start(bf16[24,1664]{1,0:T(8,128)(2,1)S(1)} %get-tuple-element.174), channel_id=1, source_target_pairs={{0,4},{1,5},{2,6},{3,7},{4,0},{5,1},{6,2},{7,3},{8,12},{9,13},{10,... | collective-permute-start | bytes 239624 | tf_op jit(solution)/shard_map/ppermute | solution.py:536
  259.2 12.3 %collective-permute-start.36 = (bf16[24,1664]{1,0:T(8,128)(2,1)S(1)}, bf16[24,1664]{1,0:T(8,128)(2,1)S(1)}, u32[]{:S(2)}, u32[]{:S(2)}) collective-permute-start(bf16[24,1664]{1,0:T(8,128)(2,1)S(1)} %get-tuple-element.175), channel_id=1, source_target_pairs={{0,4},{1,5},{2,6},{3,7},{4,0},{5,1},{6,2},{7,3},{8,12},{9,13},{10,... | collective-permute-start | bytes 239624 | tf_op jit(solution)/shard_map/ppermute | solution.py:536
  262.2 9.4 %collective-permute-start.37 = (bf16[24,1664]{1,0:T(8,128)(2,1)S(1)}, bf16[24,1664]{1,0:T(8,128)(2,1)S(1)}, u32[]{:S(2)}, u32[]{:S(2)}) collective-permute-start(bf16[24,1664]{1,0:T(8,128)(2,1)S(1)} %get-tuple-element.176), channel_id=1, source_target_pairs={{0,4},{1,5},{2,6},{3,7},{4,0},{5,1},{6,2},{7,3},{8,12},{9,13},{10,... | collective-permute-start | bytes 239624 | tf_op jit(solution)/shard_map/ppermute | solution.py:536
  262.2 9.3 %collective-permute-start.34 = (f32[8,1792]{1,0:T(8,128)S(1)}, f32[8,1792]{1,0:T(8,128)S(1)}, u32[]{:S(2)}, u32[]{:S(2)}) collective-permute-start(f32[8,1792]{1,0:T(8,128)S(1)} %get-tuple-element.170.small), channel_id=1, source_target_pairs={{0,4},{1,5},{2,6},{3,7},{4,0},{5,1},{6,2},{7,3},{8,12},{9,13},{10,... | collective-permute-start | bytes 172040 | tf_op jit(solution)/shard_map/ppermute | solution.py:536
  (9 other events, 9.1 us)
Sparse Core Ops, SparseCore 0:
  11.6 69.8 all-gather.2
